TPU v7x, 32 devices: a whole 2x2x4 slice. The times are simulated.
32 devices in a mesh: rep: 2 (over core), shard: 8 (over z, y), seq: 2 (over x).
Axes of the slice: x: 2, y: 2, z: 4, core: 2. Of those that a mesh axis runs over, the one named last changes fastest.
Arguments:
- latents: bfloat16 [16, 1024, 768], P(('rep', 'shard'), 'seq'), may hold values from -6 to 6
- image_loads: int32 [16], P(('rep', 'shard')), may hold values from 0 to 1, as said below
- timesteps: int32 [16], P(('rep', 'shard')), may hold values from 0 to 999
- classes: int32 [16], P(('rep', 'shard')), may hold values from 0 to 999
- label_table: bfloat16 [1000, 768], replicated, may hold values from -6 to 6
- ada_weight: bfloat16 [2, 768, 4608], P(None, 'shard'), may hold values from -0.21875 to 0.21875
- ada_bias: bfloat16 [2, 4608], P(None, 'shard'), may hold values from -3 to 3
- qkv_weight: bfloat16 [2, 768, 2304], P(None, 'shard'), may hold values from -0.21875 to 0.21875
- qv_bias: bfloat16 [2, 1536], P(None, 'shard'), may hold values from -3 to 3
- proj_weight: bfloat16 [2, 768, 768], P(None, 'shard'), may hold values from -0.625 to 0.625
- proj_bias: bfloat16 [2, 768], P(None, 'shard'), may hold values from -3 to 3
- fc1_weight: bfloat16 [2, 768, 3072], P(None, 'shard'), may hold values from -0.21875 to 0.21875
- fc1_bias: bfloat16 [2, 3072], P(None, 'shard'), may hold values from -3 to 3
- fc2_weight: bfloat16 [2, 3072, 768], P(None, 'shard'), may hold values from -0.109375 to 0.109375
- fc2_bias: bfloat16 [2, 768], P(None, 'shard'), may hold values from -3 to 3
- cotangent: bfloat16 [16, 1024, 768], P(('rep', 'shard'), 'seq'), may hold values from -6 to 6
Outputs:
- activations: float32 [16, 1024, 768], P(('rep', 'shard'), 'seq')
- latent_grad: float32 [16, 1024, 768], P(('rep', 'shard'), 'seq')
- cond_grad: float32 [16, 768], P(('rep', 'shard'))
- ada_weight_grad: float32 [2, 768, 4608], P(None, 'shard')
- ada_bias_grad: float32 [2, 4608], P(None, 'shard')
- qkv_weight_grad: float32 [2, 768, 2304], P(None, 'shard')
- qv_bias_grad: float32 [2, 1536], P(None, 'shard')
- proj_weight_grad: float32 [2, 768, 768], P(None, 'shard')
- proj_bias_grad: float32 [2, 768], P(None, 'shard')
- fc1_weight_grad: float32 [2, 768, 3072], P(None, 'shard')
- fc1_bias_grad: float32 [2, 3072], P(None, 'shard')
- fc2_weight_grad: float32 [2, 3072, 768], P(None, 'shard')
- fc2_bias_grad: float32 [2, 768], P(None, 'shard')
Inputs may be any that keep to these rules, and one draw needn't show every extreme that they name: Position p holds image_loads[p] live images in its first slots; its other slots of the 1 are empty and give zero outputs. Some position holds 1 live images and some holds none.
All inputs are finite; a program needn't handle non-finite values.
Results may differ from a plain program's by a relative error of at most 0.04.
Values may be sent and summed in bfloat16 or wider, within the bound.
No kernel may reach another device: no remote copies, remote signals or barrier semaphores. Data moves between devices by JAX's collectives and lax.ppermute only.
A program may use at most 320 MiB of HBM per device.

v0:
```python
import math

import jax
import jax.numpy as jnp
from jax import lax
from jax.sharding import PartitionSpec as P

HEADS = 12
LAYERS = 2


EPSILON = 1e-06


def partner(value, axis, apart):
    mask = 2**apart
    pairs = [(source, source ^ mask) for source in range(lax.axis_size(axis))]
    return lax.ppermute(value, axis, pairs)


def normalize(values):
    centered = values - jnp.mean(values, axis=-1, keepdims=True)
    return centered * lax.rsqrt(jnp.mean(centered * centered, axis=-1, keepdims=True) + EPSILON)


def modulate(values, shift, factor):
    return normalize(values) * (1.0 + factor[:, None, :]) + shift[:, None, :]


def gelu_tanh(values):
    return jax.nn.gelu(values, approximate=True)


def time_embed(steps, width):
    half_width = width // 2
    freqs = jnp.exp(-math.log(10000.0) * jnp.arange(half_width, dtype=jnp.float32) / half_width)
    angles = steps.astype(jnp.float32)[:, None] * freqs[None, :]
    return jnp.concatenate([jnp.cos(angles), jnp.sin(angles)], axis=-1)


def matmul(left, right):
    return lax.dot_general(
        left, right, (((left.ndim - 1,), (0,)), ((), ())), preferred_element_type=jnp.float32
    )


def matmul_t(left, right):
    return lax.dot_general(
        left, right, (((left.ndim - 1,), (1,)), ((), ())), preferred_element_type=jnp.float32
    )


def outer_sum(left, right):
    lead = tuple(range(left.ndim - 1))
    return lax.dot_general(
        left, right, ((lead, lead), ((), ())), preferred_element_type=jnp.float32
    )


def row_sum(values):
    return jnp.sum(values.astype(jnp.float32), axis=tuple(range(values.ndim - 1)))


def split_heads(values, heads):
    return values.reshape(values.shape[0], values.shape[1], heads, values.shape[2] // heads)


def fetch_forward(params, layer_index):
    return (
        lax.all_gather(params[0][layer_index], "shard", axis=0, tiled=True),
        lax.all_gather(params[1][layer_index], "shard", axis=0, tiled=True),
        lax.all_gather(params[2][layer_index], "shard", axis=0, tiled=True),
        lax.all_gather(params[3][layer_index], "shard", axis=0, tiled=True),
        lax.all_gather(params[4][layer_index], "shard", axis=0, tiled=True),
        lax.all_gather(params[5][layer_index], "shard", axis=0, tiled=True),
        lax.all_gather(params[6][layer_index], "shard", axis=0, tiled=True),
        lax.all_gather(params[7][layer_index], "shard", axis=0, tiled=True),
        lax.all_gather(params[8][layer_index], "shard", axis=0, tiled=True),
        lax.all_gather(params[9][layer_index], "shard", axis=0, tiled=True),
    )


def fetch_backward(params, layer_index):
    return (
        lax.all_gather(params[0][layer_index], "shard", axis=0, tiled=True),
        lax.all_gather(params[1][layer_index], "shard", axis=0, tiled=True),
        lax.all_gather(params[2][layer_index], "shard", axis=0, tiled=True),
        lax.all_gather(params[3][layer_index], "shard", axis=0, tiled=True),
        lax.all_gather(params[4][layer_index], "shard", axis=0, tiled=True),
        lax.all_gather(params[5][layer_index], "shard", axis=0, tiled=True),
        lax.all_gather(params[6][layer_index], "shard", axis=0, tiled=True),
        lax.all_gather(params[7][layer_index], "shard", axis=0, tiled=True),
        lax.all_gather(params[8][layer_index], "shard", axis=0, tiled=True),
        lax.all_gather(params[9][layer_index], "shard", axis=0, tiled=True),
    )


def reduce_layer(grads):
    owned = (
        lax.psum_scatter(grads[0], "shard", scatter_dimension=0, tiled=True),
        lax.psum_scatter(grads[1], "shard", scatter_dimension=0, tiled=True),
        lax.psum_scatter(grads[2], "shard", scatter_dimension=0, tiled=True),
        lax.psum_scatter(grads[3], "shard", scatter_dimension=0, tiled=True),
        lax.psum_scatter(grads[4], "shard", scatter_dimension=0, tiled=True),
        lax.psum_scatter(grads[5], "shard", scatter_dimension=0, tiled=True),
        lax.psum_scatter(grads[6], "shard", scatter_dimension=0, tiled=True),
        lax.psum_scatter(grads[7], "shard", scatter_dimension=0, tiled=True),
        lax.psum_scatter(grads[8], "shard", scatter_dimension=0, tiled=True),
        lax.psum_scatter(grads[9], "shard", scatter_dimension=0, tiled=True),
    )
    return (
        lax.psum(owned[0].astype(jnp.bfloat16), ("rep", "seq")).astype(jnp.float32),
        lax.psum(owned[1].astype(jnp.bfloat16), ("rep", "seq")).astype(jnp.float32),
        lax.psum(owned[2].astype(jnp.bfloat16), ("rep", "seq")).astype(jnp.float32),
        lax.psum(owned[3].astype(jnp.bfloat16), ("rep", "seq")).astype(jnp.float32),
        lax.psum(owned[4].astype(jnp.bfloat16), ("rep", "seq")).astype(jnp.float32),
        lax.psum(owned[5].astype(jnp.bfloat16), ("rep", "seq")).astype(jnp.float32),
        lax.psum(owned[6].astype(jnp.bfloat16), ("rep", "seq")).astype(jnp.float32),
        lax.psum(owned[7].astype(jnp.bfloat16), ("rep", "seq")).astype(jnp.float32),
        lax.psum(owned[8].astype(jnp.bfloat16), ("rep", "seq")).astype(jnp.float32),
        lax.psum(owned[9].astype(jnp.bfloat16), ("rep", "seq")).astype(jnp.float32),
    )


def attend(query_part, keys_values, heads):
    width = query_part.shape[-1]
    scale_factor = (width // heads) ** (-0.5)
    queries = split_heads(query_part, heads)
    keys = split_heads(keys_values[..., :width], heads)
    values = split_heads(keys_values[..., width:], heads)
    scores = (
        jnp.einsum("sqhd,skhd->shqk", queries, keys, preferred_element_type=jnp.float32)
        * scale_factor
    )
    top_score = jnp.max(scores, axis=-1, keepdims=True)
    expo = jnp.exp(scores - top_score)
    totals = jnp.sum(expo, axis=-1, keepdims=True)
    probs_low = (expo / totals).astype(jnp.bfloat16)
    mixed = jnp.einsum("shqk,skhd->sqhd", probs_low, values, preferred_element_type=jnp.float32)
    mixed_low = mixed.reshape(query_part.shape).astype(jnp.bfloat16)
    return (mixed_low, top_score + jnp.log(totals))


def attend_slots(query_part, keys_values, heads):

    def one_slot(inputs):
        mixed_low, log_total = attend(inputs[0][None], inputs[1][None], heads)
        return (mixed_low[0], log_total[0])

    return lax.map(one_slot, (query_part, keys_values))


def attend_back(query_part, keys_values, log_total, grad_mixed_low, heads):
    width = query_part.shape[-1]
    scale_factor = (width // heads) ** (-0.5)
    queries = split_heads(query_part, heads)
    keys = split_heads(keys_values[..., :width], heads)
    values = split_heads(keys_values[..., width:], heads)
    grad_heads = split_heads(grad_mixed_low, heads)
    scores = (
        jnp.einsum("sqhd,skhd->shqk", queries, keys, preferred_element_type=jnp.float32)
        * scale_factor
    )
    probs = jnp.exp(scores - log_total)
    probs_low = probs.astype(jnp.bfloat16)
    grad_probs = jnp.einsum(
        "sqhd,skhd->shqk", grad_heads, values, preferred_element_type=jnp.float32
    )
    grad_scores = probs * (grad_probs - jnp.sum(probs * grad_probs, axis=-1, keepdims=True))
    grad_scores_low = grad_scores.astype(jnp.bfloat16)
    grad_queries = (
        jnp.einsum("shqk,skhd->sqhd", grad_scores_low, keys, preferred_element_type=jnp.float32)
        * scale_factor
    )
    grad_keys = (
        jnp.einsum("shqk,sqhd->skhd", grad_scores_low, queries, preferred_element_type=jnp.float32)
        * scale_factor
    )
    grad_values = jnp.einsum(
        "shqk,sqhd->skhd", probs_low, grad_heads, preferred_element_type=jnp.float32
    )
    slot_count = query_part.shape[0]
    key_count = keys_values.shape[1]
    grad_kv = jnp.concatenate(
        [
            grad_keys.reshape(slot_count, key_count, width),
            grad_values.reshape(slot_count, key_count, width),
        ],
        axis=-1,
    )
    return (grad_queries.reshape(query_part.shape), grad_kv)


def attend_back_slots(query_part, keys_values, log_total, grad_mixed_low, heads):

    def one_slot(inputs):
        grad_queries, grad_kv = attend_back(
            inputs[0][None], inputs[1][None], inputs[2][None], inputs[3][None], heads
        )
        return (grad_queries[0], grad_kv[0])

    return lax.map(one_slot, (query_part, keys_values, log_total, grad_mixed_low))


def layer_forward(stream, cond_low, weights, heads):
    ada_w, ada_b, qkv_w, qv_b, proj_w, proj_b, fc1_w, fc1_b, fc2_w, fc2_b = weights
    width = stream.shape[-1]
    modulation = matmul(cond_low, ada_w) + ada_b.astype(jnp.float32)
    shift_attn, factor_attn, gate_attn, shift_mlp, factor_mlp, gate_mlp = jnp.split(
        modulation, 6, axis=-1
    )
    normed_low = modulate(stream, shift_attn, factor_attn).astype(jnp.bfloat16)
    query_bias = qv_b.astype(jnp.float32)
    full_bias = jnp.concatenate(
        [query_bias[:width], jnp.zeros((width,), jnp.float32), query_bias[width:]]
    )
    projected_low = (matmul(normed_low, qkv_w) + full_bias).astype(jnp.bfloat16)
    own_kv = projected_low[..., width:]
    other_kv = partner(own_kv, "seq", 0)
    keys_values = jnp.concatenate([own_kv, other_kv], axis=1)
    mixed_low, log_total = attend_slots(projected_low[..., :width], keys_values, heads)
    attn_out = matmul(mixed_low, proj_w) + proj_b.astype(jnp.float32)
    middle = stream + gate_attn[:, None, :] * attn_out
    normed_mlp_low = modulate(middle, shift_mlp, factor_mlp).astype(jnp.bfloat16)
    hidden = matmul(normed_mlp_low, fc1_w) + fc1_b.astype(jnp.float32)
    activated_low = gelu_tanh(hidden).astype(jnp.bfloat16)
    mlp_out = matmul(activated_low, fc2_w) + fc2_b.astype(jnp.float32)
    result = middle + gate_mlp[:, None, :] * mlp_out
    kept = (
        stream,
        modulation,
        normed_low,
        projected_low,
        keys_values,
        mixed_low,
        log_total,
        attn_out,
        middle,
        normed_mlp_low,
        hidden,
        activated_low,
        mlp_out,
    )
    return (result, kept)


def layer_backward(grad_out, cond_low, weights, kept, heads):
    ada_w, ada_b, qkv_w, qv_b, proj_w, proj_b, fc1_w, fc1_b, fc2_w, fc2_b = weights
    (
        stream,
        modulation,
        normed_low,
        projected_low,
        keys_values,
        mixed_low,
        log_total,
        attn_out,
        middle,
        normed_mlp_low,
        hidden,
        activated_low,
        mlp_out,
    ) = kept
    width = stream.shape[-1]
    half_tokens = stream.shape[1]
    shift_attn, factor_attn, gate_attn, shift_mlp, factor_mlp, gate_mlp = jnp.split(
        modulation, 6, axis=-1
    )
    grad_gate_mlp = jnp.sum(grad_out * mlp_out, axis=1)
    grad_mlp_low = (grad_out * gate_mlp[:, None, :]).astype(jnp.bfloat16)
    grad_fc2_w = outer_sum(activated_low, grad_mlp_low)
    grad_fc2_b = row_sum(grad_mlp_low)
    grad_activated = matmul_t(grad_mlp_low, fc2_w)
    _, gelu_pull = jax.vjp(gelu_tanh, hidden)
    grad_hidden_low = gelu_pull(grad_activated)[0].astype(jnp.bfloat16)
    grad_fc1_w = outer_sum(normed_mlp_low, grad_hidden_low)
    grad_fc1_b = row_sum(grad_hidden_low)
    grad_normed_mlp = matmul_t(grad_hidden_low, fc1_w)
    _, second_pull = jax.vjp(modulate, middle, shift_mlp, factor_mlp)
    grad_middle_norm, grad_shift_mlp, grad_factor_mlp = second_pull(grad_normed_mlp)
    grad_middle = grad_out + grad_middle_norm
    grad_gate_attn = jnp.sum(grad_middle * attn_out, axis=1)
    grad_attn_low = (grad_middle * gate_attn[:, None, :]).astype(jnp.bfloat16)
    grad_proj_w = outer_sum(mixed_low, grad_attn_low)
    grad_proj_b = row_sum(grad_attn_low)
    grad_mixed_low = matmul_t(grad_attn_low, proj_w).astype(jnp.bfloat16)
    grad_queries, grad_kv_all = attend_back_slots(
        projected_low[..., :width], keys_values, log_total, grad_mixed_low, heads
    )
    returned = partner(grad_kv_all[:, half_tokens:].astype(jnp.bfloat16), "seq", 0).astype(
        jnp.float32
    )
    grad_kv = grad_kv_all[:, :half_tokens] + returned
    grad_projected_low = jnp.concatenate([grad_queries, grad_kv], axis=-1).astype(jnp.bfloat16)
    grad_qkv_w = outer_sum(normed_low, grad_projected_low)
    bias_totals = row_sum(grad_projected_low)
    grad_qv_b = jnp.concatenate([bias_totals[:width], bias_totals[2 * width :]])
    grad_normed = matmul_t(grad_projected_low, qkv_w)
    _, first_pull = jax.vjp(modulate, stream, shift_attn, factor_attn)
    grad_stream_norm, grad_shift_attn, grad_factor_attn = first_pull(grad_normed)
    grad_stream = grad_middle + grad_stream_norm
    grad_modulation = jnp.concatenate(
        [
            grad_shift_attn,
            grad_factor_attn,
            grad_gate_attn,
            grad_shift_mlp,
            grad_factor_mlp,
            grad_gate_mlp,
        ],
        axis=-1,
    )
    grad_modulation_low = lax.psum(grad_modulation, "seq").astype(jnp.bfloat16)
    leader = (lax.axis_index("seq") == 0).astype(jnp.float32)
    grad_ada_w = outer_sum(cond_low, grad_modulation_low) * leader
    grad_ada_b = row_sum(grad_modulation_low) * leader
    grad_cond_part = matmul_t(grad_modulation_low, ada_w)
    grads = (
        grad_ada_w,
        grad_ada_b,
        grad_qkv_w,
        grad_qv_b,
        grad_proj_w,
        grad_proj_b,
        grad_fc1_w,
        grad_fc1_b,
        grad_fc2_w,
        grad_fc2_b,
    )
    return (grad_stream, grad_cond_part, grads)


def shards(
    latents,
    image_loads,
    timesteps,
    classes,
    label_table,
    ada_weight,
    ada_bias,
    qkv_weight,
    qv_bias,
    proj_weight,
    proj_bias,
    fc1_weight,
    fc1_bias,
    fc2_weight,
    fc2_bias,
    cotangent,
):
    params = (
        ada_weight,
        ada_bias,
        qkv_weight,
        qv_bias,
        proj_weight,
        proj_bias,
        fc1_weight,
        fc1_bias,
        fc2_weight,
        fc2_bias,
    )
    slot_count = latents.shape[0]
    width = latents.shape[2]
    live = (jnp.arange(slot_count, dtype=jnp.int32) < image_loads[0]).astype(jnp.float32)
    one_hot = (
        classes[:, None] == jnp.arange(label_table.shape[0], dtype=jnp.int32)[None, :]
    ).astype(jnp.bfloat16)
    cond = matmul(one_hot, label_table) + time_embed(timesteps, width)
    cond_low = jax.nn.silu(cond).astype(jnp.bfloat16)
    stream = latents.astype(jnp.float32)
    kept_list = []
    gathered_list = []
    for layer_index in range(LAYERS):
        gathered = fetch_forward(params, layer_index)
        stream, kept = layer_forward(stream, cond_low, gathered, HEADS)
        kept_list.append(kept)
        gathered_list.append(gathered)
    activations = stream * live[:, None, None]
    grad_stream = cotangent.astype(jnp.float32) * live[:, None, None]
    grad_cond_low = jnp.zeros((slot_count, width), jnp.float32)
    layer_grads = [None] * LAYERS
    for layer_index in reversed(range(LAYERS)):
        gathered = fetch_backward(params, layer_index)
        grad_stream, grad_part, grads = layer_backward(
            grad_stream, cond_low, gathered, kept_list[layer_index], HEADS
        )
        grad_cond_low = grad_cond_low + grad_part
        layer_grads[layer_index] = reduce_layer(grads)
    _, silu_pull = jax.vjp(jax.nn.silu, cond)
    cond_grad = silu_pull(grad_cond_low)[0]
    stacked = tuple(
        (jnp.stack([layer_grads[0][position], layer_grads[1][position]]) for position in range(10))
    )
    return (activations, grad_stream, cond_grad) + stacked


def solution(mesh):
    placed = (
        P(("rep", "shard"), "seq", None),
        P(("rep", "shard")),
        P(("rep", "shard")),
        P(("rep", "shard")),
        P(),
        P(None, "shard", None),
        P(None, "shard"),
        P(None, "shard", None),
        P(None, "shard"),
        P(None, "shard", None),
        P(None, "shard"),
        P(None, "shard", None),
        P(None, "shard"),
        P(None, "shard", None),
        P(None, "shard"),
        P(("rep", "shard"), "seq", None),
    )
    return jax.shard_map(
        shards,
        mesh=mesh,
        in_specs=placed,
        out_specs=(
            P(("rep", "shard"), "seq", None),
            P(("rep", "shard"), "seq", None),
            P(("rep", "shard"), None),
            P(None, "shard", None),
            P(None, "shard"),
            P(None, "shard", None),
            P(None, "shard"),
            P(None, "shard", None),
            P(None, "shard"),
            P(None, "shard", None),
            P(None, "shard"),
            P(None, "shard", None),
            P(None, "shard"),
        ),
        check_vma=False,
    )
```

profile of v0, /device:TPU:0, one launch (start us, length us, event | category | flops | bytes accessed | tf_op | source)
XLA Modules:
  0.0 2507.9 jit_solution(3140503761280492668)
XLA Ops:
  25.7 41.0 %all-reduce.20 = (bf16[1536]{0:T(1024)(128)(2,1)S(1)}, bf16[4608]{0:T(1024)(128)(2,1)S(1)}, bf16[768]{0:T(1024)(128)(2,1)S(1)}, bf16[768]{0:T(1024)(128)(2,1)S(1...) all-reduce(bf16[1536]{0:T(1024)(128)(2,1)S(1)} %dynamic-update-slic, ...), channel_id=5, replica_groups=mesh['rep'=2,'shard'=8,'seq'=2] {'shard'}, use_global_device_ids=true, to_apply=%add.1 | all-reduce | flops 15360 | bytes 61440
  68.4 55.1 %all-gather.31.cloned.1.call-done = bf16[1,768,4608]{2,1,0:T(8,128)(2,1)} async-done(((bf16[1,96,4608]{2,1,0:T(8,128)(2,1)}), bf16[1,768,4608]{2,1,0:T(8,128)(2,1)}) %all-gather.31.cloned.1.call-update) | async-done | bytes 7077904 | tf_op jit(solution)/shard_map/all_gather | solution.py:70
  127.6 62.0 %all-gather.33.cloned.1.call-done = bf16[1,768,2304]{2,1,0:T(8,128)(2,1)} async-done(((bf16[1,96,2304]{2,1,0:T(8,128)(2,1)}), bf16[1,768,2304]{2,1,0:T(8,128)(2,1)}) %all-gather.33.cloned.1.call-update) | async-done | bytes 3538960 | tf_op jit(solution)/shard_map/all_gather | solution.py:72
  198.1 27.0 %all-gather.7 = bf16[1,3072]{1,0:T(2,128)(2,1)S(1)} all-gather(bf16[1,384]{1,0:T(2,128)(2,1)S(1)} %get-tuple-element.208), channel_id=9, replica_groups=mesh['rep'=2,'shard'=8,'seq'=2] {'shard'}, dimensions={1}, use_global_device_ids=true | all-gather | bytes 6912 | tf_op jit(solution)/shard_map/all_gather | solution.py:77
  225.2 74.7 %all-gather.41.cloned.1.call-done = bf16[1,768,4608]{2,1,0:T(8,128)(2,1)} async-done(((bf16[1,96,4608]{2,1,0:T(8,128)(2,1)}), bf16[1,768,4608]{2,1,0:T(8,128)(2,1)}) %all-gather.41.cloned.1.call-update) | async-done | bytes 7077904 | tf_op jit(solution)/shard_map/all_gather | solution.py:70
  313.4 11.6 multiply_reduce_fusion.3
  325.0 11.2 fusion
  336.2 11.0 fusion.101
  352.3 70.1 %all-gather.37.cloned.1.call-done = bf16[1,768,3072]{2,1,0:T(8,128)(2,1)} async-done(((bf16[1,96,3072]{2,1,0:T(8,128)(2,1)}), bf16[1,768,3072]{2,1,0:T(8,128)(2,1)}) %all-gather.37.cloned.1.call-update) | async-done | bytes 4718608 | tf_op jit(solution)/shard_map/all_gather | solution.py:76
  422.4 8.3 fusion.50
  430.7 72.4 %all-gather.39.cloned.1.call-done = bf16[1,3072,768]{2,1,0:T(8,128)(2,1)} async-done(((bf16[1,384,768]{2,1,0:T(8,128)(2,1)}), bf16[1,3072,768]{2,1,0:T(8,128)(2,1)}) %all-gather.39.cloned.1.call-update) | async-done | bytes 4718608 | tf_op jit(solution)/shard_map/all_gather | solution.py:78
  503.1 9.3 fusion.180
  513.9 54.7 %all-gather.43.cloned.1.call-done = bf16[1,768,2304]{2,1,0:T(8,128)(2,1)} async-done(((bf16[1,96,2304]{2,1,0:T(8,128)(2,1)}), bf16[1,768,2304]{2,1,0:T(8,128)(2,1)}) %all-gather.43.cloned.1.call-update) | async-done | bytes 3538960 | tf_op jit(solution)/shard_map/all_gather | solution.py:72
  577.1 26.0 %all-gather.17 = bf16[1,3072]{1,0:T(2,128)(2,1)S(1)} all-gather(bf16[1,384]{1,0:T(2,128)(2,1)S(1)} %get-tuple-element.207), channel_id=19, replica_groups=mesh['rep'=2,'shard'=8,'seq'=2] {'shard'}, dimensions={1}, use_global_device_ids=true | all-gather | bytes 6912 | tf_op jit(solution)/shard_map/all_gather | solution.py:77
  618.4 10.1 multiply_reduce_fusion.2
  628.5 11.2 fusion.1
  639.7 12.2 fusion.100
  656.4 35.0 %all-gather.47.cloned.1.call-done = bf16[1,768,3072]{2,1,0:T(8,128)(2,1)} async-done(((bf16[1,96,3072]{2,1,0:T(8,128)(2,1)}), bf16[1,768,3072]{2,1,0:T(8,128)(2,1)}) %all-gather.47.cloned.1.call-update) | async-done | bytes 4718608 | tf_op jit(solution)/shard_map/all_gather | solution.py:76
  698.5 73.5 %all-gather.49.cloned.1.call-done = bf16[1,3072,768]{2,1,0:T(8,128)(2,1)} async-done(((bf16[1,384,768]{2,1,0:T(8,128)(2,1)}), bf16[1,3072,768]{2,1,0:T(8,128)(2,1)}) %all-gather.49.cloned.1.call-update) | async-done | bytes 4718608 | tf_op jit(solution)/shard_map/all_gather | solution.py:78
  772.1 10.3 convert_reduce_fusion
  794.0 12.6 fusion.6
  806.5 16.8 multiply_reduce_fusion.1
  823.3 16.6 multiply_convert_fusion.1
  851.4 9.3 multiply_convert_fusion.7
  860.7 22.2 collective-permute-done.2
  890.8 11.0 convert_reduce_fusion.5
  901.9 8.2 convert_reduce_fusion.1
  932.7 19.1 multiply_reduce_fusion
  951.8 17.0 multiply_convert_fusion
  975.7 10.7 fusion.4
  989.2 8.5 multiply_convert_fusion.4
  997.8 24.6 collective-permute-done.3
  1031.0 10.9 fusion.131
  1042.6 8.9 fusion.167
  1051.6 10.4 fusion.125
  1062.6 7.2 fusion.172
  1083.5 12.1 all-reduce.19
  1095.8 13.4 multiply_multiply_fusion.1
  1123.5 130.1 %reduce-scatter.15.cloned.1.call-done = f32[96,2304]{1,0:T(8,128)} async-done(((f32[768,2304]{1,0:T(8,128)}), f32[96,2304]{1,0:T(8,128)}) %reduce-scatter.15.cloned.1.call-update) | async-done | bytes 884752 | tf_op jit(solution)/shard_map/reduce_scatter | solution.py:102
  1255.6 164.0 %reduce-scatter.29.cloned.1.call-done = f32[384,768]{1,0:T(8,128)} async-done(((f32[3072,768]{1,0:T(8,128)}), f32[384,768]{1,0:T(8,128)}) %reduce-scatter.29.cloned.1.call-update) | async-done | bytes 1179664 | tf_op jit(solution)/shard_map/reduce_scatter | solution.py:108
  1421.7 163.9 %reduce-scatter.25.cloned.1.call-done = f32[96,3072]{1,0:T(8,128)} async-done(((f32[768,3072]{1,0:T(8,128)}), f32[96,3072]{1,0:T(8,128)}) %reduce-scatter.25.cloned.1.call-update) | async-done | bytes 1179664 | tf_op jit(solution)/shard_map/reduce_scatter | solution.py:106
  1587.8 163.9 %reduce-scatter.27.cloned.1.call-done = f32[384,768]{1,0:T(8,128)} async-done(((f32[3072,768]{1,0:T(8,128)}), f32[384,768]{1,0:T(8,128)}) %reduce-scatter.27.cloned.1.call-update) | async-done | bytes 1179664 | tf_op jit(solution)/shard_map/reduce_scatter | solution.py:108
  1753.8 163.8 %reduce-scatter.23.cloned.1.call-done = f32[96,3072]{1,0:T(8,128)} async-done(((f32[768,3072]{1,0:T(8,128)}), f32[96,3072]{1,0:T(8,128)}) %reduce-scatter.23.cloned.1.call-update) | async-done | bytes 1179664 | tf_op jit(solution)/shard_map/reduce_scatter | solution.py:106
  1919.8 229.8 %reduce-scatter.11.cloned.1.call-done = f32[96,4608]{1,0:T(8,128)} async-done(((f32[768,4608]{1,0:T(8,128)}), f32[96,4608]{1,0:T(8,128)}) %reduce-scatter.11.cloned.1.call-update) | async-done | bytes 1769488 | tf_op jit(solution)/shard_map/reduce_scatter | solution.py:100
  2152.1 229.7 %reduce-scatter.13.cloned.1.call-done = f32[96,4608]{1,0:T(8,128)} async-done(((f32[768,4608]{1,0:T(8,128)}), f32[96,4608]{1,0:T(8,128)}) %reduce-scatter.13.cloned.1.call-update) | async-done | bytes 1769488 | tf_op jit(solution)/shard_map/reduce_scatter | solution.py:100
  2396.7 35.3 %all-reduce.18 = (bf16[4608]{0:T(1024)(128)(2,1)S(1)}, bf16[4608]{0:T(1024)(128)(2,1)S(1)}, bf16[1536]{0:T(1024)(128)(2,1)S(1)}, bf16[1536]{0:T(1024)(128)(2,1)S...) all-reduce(f32[4608]{0:T(1024)S(1)} %multiply_reduce_fusion.7, ...), channel_id=25, replica_groups=mesh['rep'=2,'shard'=8,'seq'=2] {'shard'}, use_global_device_ids=true, to_apply=%region_42.43.clone | all-reduce | flops 21504 | bytes 129024
  2432.8 12.1 all-reduce.21
  2447.9 42.7 %all-reduce.25.cloned.1.call-done = (bf16[1,96,4608]{2,1,0:T(8,128)(2,1)}, bf16[1,96,4608]{2,1,0:T(8,128)(2,1)}, bf16[1,96,2304]{2,1,0:T(8,128)(2,1)}, bf16[1,96...) async-done(((bf16[1,96,4608]{2,1,0:T(8,128)(2,1)}, ...) | async-done | bytes 5308432 | tf_op jit(solution)/shard_map/psum | solution.py:112
  (504 shorter events, 223.3 us)
Async XLA Ops:
  7.2 59.6 %copy-start = (bf16[1000,768]{1,0:T(8,128)(2,1)S(1)}, bf16[1000,768]{1,0:T(8,128)(2,1)}, u32[]{:S(2)}) copy-start(bf16[1000,768]{1,0:T(8,128)(2,1)} %param.20) | copy-start | bytes 4608004
  7.2 116.2 %all-gather.31.cloned.1.call-start = ((), (), s32[]{:S(2)}) async-start(), calls=%async_computation.20 | async-start | bytes 7962624 | tf_op jit(solution)/shard_map/all_gather | solution.py:70
  10.1 179.5 %all-gather.33.cloned.1.call-start = ((), (), s32[]{:S(2)}) async-start(), calls=%async_computation.21 | async-start | bytes 3981312 | tf_op jit(solution)/shard_map/all_gather | solution.py:72
  12.4 287.4 %all-gather.41.cloned.1.call-start = ((), (), s32[]{:S(2)}) async-start(), calls=%async_computation.25 | async-start | bytes 7962624 | tf_op jit(solution)/shard_map/all_gather | solution.py:70
  13.2 334.1 %all-gather.35.cloned.1.call-start = ((), (), s32[]{:S(2)}) async-start(), calls=%async_computation.22 | async-start | bytes 1327104 | tf_op jit(solution)/shard_map/all_gather | solution.py:74
  14.0 408.5 %all-gather.37.cloned.1.call-start = ((), (), s32[]{:S(2)}) async-start(), calls=%async_computation.23 | async-start | bytes 5308416 | tf_op jit(solution)/shard_map/all_gather | solution.py:76
  15.2 487.9 %all-gather.39.cloned.1.call-start = ((), (), s32[]{:S(2)}) async-start(), calls=%async_computation.24 | async-start | bytes 5308416 | tf_op jit(solution)/shard_map/all_gather | solution.py:78
  17.7 550.9 %all-gather.43.cloned.1.call-start = ((), (), s32[]{:S(2)}) async-start(), calls=%async_computation.26 | async-start | bytes 3981312 | tf_op jit(solution)/shard_map/all_gather | solution.py:72
  18.5 633.5 %all-gather.45.cloned.1.call-start = ((), (), s32[]{:S(2)}) async-start(), calls=%async_computation.27 | async-start | bytes 1327104 | tf_op jit(solution)/shard_map/all_gather | solution.py:74
  19.2 672.2 %all-gather.47.cloned.1.call-start = ((), (), s32[]{:S(2)}) async-start(), calls=%async_computation.28 | async-start | bytes 5308416 | tf_op jit(solution)/shard_map/all_gather | solution.py:76
  23.4 166.2 %copy-start.74 = (f32[512]{0:T(512)}, f32[512]{0:T(512)S(1)}, u32[]{:S(2)}) copy-start(f32[512]{0:T(512)S(1)} %broadcast_multiply_fusion.3) | copy-start | bytes 6148
  23.8 165.8 %copy-start.72 = (f32[512]{0:T(512)}, f32[512]{0:T(512)S(1)}, u32[]{:S(2)}) copy-start(f32[512]{0:T(512)S(1)} %fusion.148) | copy-start | bytes 6148
  23.9 103.5 %copy-start.84 = (f32[384]{0:T(512)}, f32[384]{0:T(512)S(1)}, u32[]{:S(2)}) copy-start(f32[384]{0:T(512)S(1)} %get-tuple-element.235) | copy-start | bytes 4612
  23.9 103.5 %copy-start.86 = (f32[384]{0:T(512)}, f32[384]{0:T(512)S(1)}, u32[]{:S(2)}) copy-start(f32[384]{0:T(512)S(1)} %get-tuple-element.236) | copy-start | bytes 4612
  127.6 66.2 %copy-start.66 = (f32[768]{0:T(1024)}, f32[768]{0:T(1024)S(1)}, u32[]{:S(2)}) copy-start(f32[768]{0:T(1024)S(1)} %get-tuple-element.106) | copy-start | bytes 9220
  127.6 66.2 %copy-start.111 = (f32[768]{0:T(1024)}, f32[768]{0:T(1024)S(1)}, u32[]{:S(2)}) copy-start(f32[768]{0:T(1024)S(1)} %get-tuple-element.105) | copy-start | bytes 9220
  127.6 219.7 %copy-start.70 = (f32[768]{0:T(1024)}, f32[768]{0:T(1024)S(1)}, u32[]{:S(2)}) copy-start(f32[768]{0:T(1024)S(1)} %get-tuple-element.107) | copy-start | bytes 9220
  127.6 294.8 %copy-start.91 = (f32[768]{0:T(1024)}, f32[768]{0:T(1024)S(1)}, u32[]{:S(2)}) copy-start(f32[768]{0:T(1024)S(1)} %get-tuple-element.104) | copy-start | bytes 9220
  127.6 294.8 %copy-start.109 = (f32[768]{0:T(1024)}, f32[768]{0:T(1024)S(1)}, u32[]{:S(2)}) copy-start(f32[768]{0:T(1024)S(1)} %get-tuple-element.103) | copy-start | bytes 9220
  196.5 107.8 %collective-permute-start = (bf16[1,512,1536]{2,1,0:T(8,128)(2,1)}, bf16[1,512,1536]{2,1,0:T(8,128)(2,1)}, u32[]{:S(2)}, u32[]{:S(2)}) collective-permute-start(bf16[1,512,1536]{2,1,0:T(8,128)(2,1)} %slice.192), channel_id=1, source_target_pairs={{0,1},{1,0},{2,3},{3,2},{4,5},{5,4},{6,7},{7,6},{8,9},{9,8},{10,11... | collective-permute-start | bytes 4718600 | tf_op jit(solution)/shard_map/ppermute | solution.py:18
  198.0 574.1 %all-gather.49.cloned.1.call-start = ((), (), s32[]{:S(2)}) async-start(), calls=%async_computation.29 | async-start | bytes 5308416 | tf_op jit(solution)/shard_map/all_gather | solution.py:78
  198.0 305.1 %copy-start.89 = (f32[768]{0:T(1024)}, f32[768]{0:T(1024)S(1)}, u32[]{:S(2)}) copy-start(f32[768]{0:T(1024)S(1)} %convert_element_type.439) | copy-start | bytes 9220
  225.1 278.0 %copy-start.97 = (f32[1,3072]{1,0:T(1,128)}, f32[1,3072]{1,0:T(1,128)S(1)}, u32[]{:S(2)}) copy-start(f32[1,3072]{1,0:T(1,128)S(1)} %convert_element_type.429) | copy-start | bytes 36868
  225.1 78.8 %slice-start = ((bf16[1,512,2304]{2,1,0:T(8,128)(2,1)}), bf16[1,512,768]{2,1,0:T(8,128)(2,1)S(1)}, s32[]{:S(2)}) async-start(bf16[1,512,2304]{2,1,0:T(8,128)(2,1)} %copy-done.40), calls=%async_computation.31 | async-start | bytes 1572864 | tf_op jit(solution)/shard_map/slice | solution.py:221
  304.3 264.4 %copy-start.115 = (f32[768]{0:T(1024)}, f32[768]{0:T(1024)S(1)}, u32[]{:S(2)}) copy-start(f32[768]{0:T(1024)S(1)} %get-tuple-element.99) | copy-start | bytes 9220
  304.3 387.1 %copy-start.113 = (f32[768]{0:T(1024)}, f32[768]{0:T(1024)S(1)}, u32[]{:S(2)}) copy-start(f32[768]{0:T(1024)S(1)} %get-tuple-element.97) | copy-start | bytes 9220
  304.3 481.5 %copy-start.93 = (f32[768]{0:T(1024)}, f32[768]{0:T(1024)S(1)}, u32[]{:S(2)}) copy-start(f32[768]{0:T(1024)S(1)} %get-tuple-element.98) | copy-start | bytes 9220
  350.8 79.9 %copy-start.76 = (f32[512]{0:T(512)}, f32[512]{0:T(512)S(1)}, u32[]{:S(2)}) copy-start(f32[512]{0:T(512)S(1)} %broadcast_multiply_fusion.2) | copy-start | bytes 6148
  352.3 78.4 %copy-start.82 = (f32[512]{0:T(512)}, f32[512]{0:T(512)S(1)}, u32[]{:S(2)}) copy-start(f32[512]{0:T(512)S(1)} %multiply_reduce_fusion.6) | copy-start | bytes 6148
  352.3 78.4 %copy-start.100 = (f32[512]{0:T(512)}, f32[512]{0:T(512)S(1)}, u32[]{:S(2)}) copy-start(f32[512]{0:T(512)S(1)} %fusion.149) | copy-start | bytes 6148
  422.4 80.7 %copy-start.11 = (f32[1,512,768]{2,1,0:T(8,128)S(1)}, f32[1,512,768]{2,1,0:T(8,128)}, u32[]{:S(2)}) copy-start(f32[1,512,768]{2,1,0:T(8,128)} %copy-done.10) | copy-start | bytes 4718596
  574.8 35.3 %collective-permute-start.1 = (bf16[1,512,1536]{2,1,0:T(8,128)(2,1)S(1)}, bf16[1,512,1536]{2,1,0:T(8,128)(2,1)}, u32[]{:S(2)}, u32[]{:S(2)}) collective-permute-start(bf16[1,512,1536]{2,1,0:T(8,128)(2,1)S(1)} %slice.198), channel_id=1, source_target_pairs={{0,1},{1,0},{2,3},{3,2},{4,5},{5,4},{6,7},{7,6},{8,9},{9,8},{10,11... | collective-permute-start | bytes 4718600 | tf_op jit(solution)/shard_map/ppermute | solution.py:18
  576.3 536.6 %reduce-scatter.21.cloned.1.call-start = ((), (), s32[]{:S(2)}) async-start(), calls=%async_computation.15 | async-start | bytes 2654208 | tf_op jit(solution)/shard_map/reduce_scatter | solution.py:104
  656.0 232.6 %copy-start.13 = (f32[1,512,768]{2,1,0:T(8,128)}, f32[1,512,768]{2,1,0:T(8,128)S(1)}, u32[]{:S(2)}) copy-start(f32[1,512,768]{2,1,0:T(8,128)S(1)} %get-tuple-element.173) | copy-start | bytes 4718596
  656.0 129.8 %copy-start.78 = (f32[512]{0:T(512)}, f32[512]{0:T(512)S(1)}, u32[]{:S(2)}) copy-start(f32[512]{0:T(512)S(1)} %broadcast_multiply_fusion) | copy-start | bytes 6148
  656.4 129.4 %copy-start.102 = (f32[512]{0:T(512)}, f32[512]{0:T(512)S(1)}, u32[]{:S(2)}) copy-start(f32[512]{0:T(512)S(1)} %fusion.151) | copy-start | bytes 6148
  847.5 35.5 %collective-permute-start.2 = (bf16[1,512,1536]{1,2,0:T(8,128)(2,1)}, bf16[1,512,1536]{1,2,0:T(8,128)(2,1)}, u32[]{:S(2)}, u32[]{:S(2)}) collective-permute-start(bf16[1,512,1536]{1,2,0:T(8,128)(2,1)} %fusion.69), channel_id=1, source_target_pairs={{0,1},{1,0},{2,3},{3,2},{4,5},{5,4},{6,7},{7,6},{8,9},{9,8},{10,11... | collective-permute-start | bytes 4718600 | tf_op jit(solution)/shard_map/ppermute | solution.py:18
  851.1 263.4 %reduce-scatter.19.cloned.1.call-start = ((), (), s32[]{:S(2)}) async-start(), calls=%async_computation.14 | async-start | bytes 2654208 | tf_op jit(solution)/shard_map/reduce_scatter | solution.py:104
  919.8 201.7 %reduce-scatter.17.cloned.1.call-start = ((), (), s32[]{:S(2)}) async-start(), calls=%async_computation.13 | async-start | bytes 7962624 | tf_op jit(solution)/shard_map/reduce_scatter | solution.py:102
  927.0 326.6 %reduce-scatter.15.cloned.1.call-start = ((), (), s32[]{:S(2)}) async-start(), calls=%async_computation.12 | async-start | bytes 7962624 | tf_op jit(solution)/shard_map/reduce_scatter | solution.py:102
  987.9 34.5 %collective-permute-start.3 = (bf16[1,512,1536]{1,2,0:T(8,128)(2,1)}, bf16[1,512,1536]{1,2,0:T(8,128)(2,1)}, u32[]{:S(2)}, u32[]{:S(2)}) collective-permute-start(bf16[1,512,1536]{1,2,0:T(8,128)(2,1)} %fusion.68), channel_id=1, source_target_pairs={{0,1},{1,0},{2,3},{3,2},{4,5},{5,4},{6,7},{7,6},{8,9},{9,8},{10,11... | collective-permute-start | bytes 4718600 | tf_op jit(solution)/shard_map/ppermute | solution.py:18
  1030.9 388.6 %reduce-scatter.29.cloned.1.call-start = ((), (), s32[]{:S(2)}) async-start(), calls=%async_computation.19 | async-start | bytes 10616832 | tf_op jit(solution)/shard_map/reduce_scatter | solution.py:108
  1041.9 543.7 %reduce-scatter.25.cloned.1.call-start = ((), (), s32[]{:S(2)}) async-start(), calls=%async_computation.17 | async-start | bytes 10616832 | tf_op jit(solution)/shard_map/reduce_scatter | solution.py:106
  1051.5 700.2 %reduce-scatter.27.cloned.1.call-start = ((), (), s32[]{:S(2)}) async-start(), calls=%async_computation.18 | async-start | bytes 10616832 | tf_op jit(solution)/shard_map/reduce_scatter | solution.py:108
  1062.0 855.7 %reduce-scatter.23.cloned.1.call-start = ((), (), s32[]{:S(2)}) async-start(), calls=%async_computation.16 | async-start | bytes 10616832 | tf_op jit(solution)/shard_map/reduce_scatter | solution.py:106
  1069.9 1079.7 %reduce-scatter.11.cloned.1.call-start = ((), (), s32[]{:S(2)}) async-start(), calls=%async_computation.10 | async-start | bytes 15925248 | tf_op jit(solution)/shard_map/reduce_scatter | solution.py:100
  1109.2 1272.7 %reduce-scatter.13.cloned.1.call-start = ((), (), s32[]{:S(2)}) async-start(), calls=%async_computation.11 | async-start | bytes 15925248 | tf_op jit(solution)/shard_map/reduce_scatter | solution.py:100
  1109.8 1380.8 %all-reduce.25.cloned.1.call-start = ((), (), s32[]{:S(2)}) async-start(), calls=%async_computation.30 | async-start | bytes 10616832 | tf_op jit(solution)/shard_map/psum | solution.py:112
  (109 other events, 822.3 us)
Sparse Core Ops, SparseCore 0:
  10.8 112.5 all-gather.30
  126.2 63.3 all-gather.32
  192.4 107.4 all-gather.40
  302.4 39.2 all-gather.34
  343.8 78.6 all-gather.36
  425.1 78.0 all-gather.38
  505.3 63.3 all-gather.42
  570.8 39.6 all-gather.44
  612.7 78.6 all-gather.46
  694.0 78.0 all-gather.48
  851.3 66.4 reduce-scatter.20
  921.6 68.0 reduce-scatter.18
  993.4 128.0 reduce-scatter.16
  1125.5 128.0 reduce-scatter.14
  1257.0 162.4 reduce-scatter.28
  1423.0 162.5 reduce-scatter.24
  1589.1 162.5 reduce-scatter.26
  1755.1 162.5 reduce-scatter.22
  1921.3 228.2 reduce-scatter.10
  2153.1 228.6 reduce-scatter.12
  2386.0 104.5 all-reduce.24
where the time goes:
time: 2520 us; the launch traced here: 2510 us
  waiting for transfers between devices  1840 us (73%)
  matrix products  289 us (11%)
  blocking collectives  154 us (6%)
  other arithmetic  131 us (5%)
  local copies, waits for them, and re-layouts  60.3 us (2%)
    reduce_scatter x2, waiting for transfers between devices, reduce_layer(): lax.psum_scatter(grads[0], 'shard', scatter_dimension=0, tiled=True)  460 us
    reduce_scatter x2, waiting for transfers between devices, reduce_layer(): lax.psum_scatter(grads[8], 'shard', scatter_dimension=0, tiled=True)  328 us
    reduce_scatter x2, waiting for transfers between devices, reduce_layer(): lax.psum_scatter(grads[6], 'shard', scatter_dimension=0, tiled=True)  328 us
    all_gather x2, waiting for transfers between devices, fetch_forward(): lax.all_gather(params[8][layer_index], 'shard', axis=0, tiled=True)  146 us
    reduce_scatter x2, waiting for transfers between devices, reduce_layer(): lax.psum_scatter(grads[2], 'shard', scatter_dimension=0, tiled=True)  135 us
    all_gather x2, waiting for transfers between devices, fetch_forward(): lax.all_gather(params[0][layer_index], 'shard', axis=0, tiled=True)  130 us
    all_gather x2, waiting for transfers between devices, fetch_forward(): lax.all_gather(params[2][layer_index], 'shard', axis=0, tiled=True)  117 us
    all_gather x2, waiting for transfers between devices, fetch_forward(): lax.all_gather(params[6][layer_index], 'shard', axis=0, tiled=True)  105 us
  transfers between devices with their start and end apart: 25, of which 20 were waited for; matrix products, arithmetic and copies ran while one was open for 15% of the time, Pallas kernels for 0%

commit v1 on v0

v1 whole, which is shorter than its diff:
```python
import functools
import math

import jax
import jax.numpy as jnp
from jax import lax
from jax.experimental import pallas as pl
from jax.experimental.pallas import tpu as pltpu
from jax.sharding import PartitionSpec as P

HEADS = 12
LAYERS = 2
EPSILON = 1e-06
BF16 = jnp.bfloat16
F32 = jnp.float32


def swap_pairs(value, axis):
    return lax.ppermute(value, axis, [(0, 1), (1, 0)])


def swap_layout(value):
    return lax.ppermute(value, ("rep", "seq"), [(0, 0), (1, 2), (2, 1), (3, 3)])


def ring_order(size):
    half = size // 2
    return [2 * place for place in range(half)] + [2 * place + 1 for place in reversed(range(half))]


def ring_step(value, forward):
    size = lax.axis_size("shard")
    order = ring_order(size)
    step = 1 if forward else size - 1
    return lax.ppermute(
        value, "shard", [(order[at], order[(at + step) % size]) for at in range(size)]
    )


def ring_ids():
    size = lax.axis_size("shard")
    order = ring_order(size)
    places = [order.index(shard) for shard in range(size)]
    place = jnp.array(places, jnp.int32)[lax.axis_index("shard")]
    return jnp.array(order, jnp.int32)[(place + jnp.arange(size, dtype=jnp.int32)) % size]


OFFSETS = (-1, 1, -2, 2, -3, 3, 4)


def place_kernel(plain, split, where, *refs):
    (own, *rest) = refs[:19]
    outs = refs[19:-1]
    sem = refs[-1]
    blocks, near_x, far_x = rest[0:7], rest[7], rest[8]
    core_blocks, core_near_x, core_far_x = rest[9:16], rest[16], rest[17]
    rep, seq = where[8], where[9]
    unit = own.shape[1] // 6

    def put(src, shard, row, rows):
        copies = []
        if plain:
            start = pl.multiple_of(shard * (6 * unit) + row * unit, unit)
            copies.append(
                pltpu.make_async_copy(src.at[0:plain], outs[0].at[:, pl.ds(start, rows), :], sem)
            )
        if split:
            start = pl.multiple_of(row * unit, unit)
            copies.append(
                pltpu.make_async_copy(
                    src.at[plain : plain + split],
                    outs[-1].at[shard, :, pl.ds(start, rows), :],
                    sem,
                )
            )
        for copy in copies:
            copy.start()
        return copies

    copies = put(own, where[0], 0, 6 * unit)
    for slot, offset in enumerate(OFFSETS):
        shard = where[offset % 8]
        beside = (near_x, core_near_x) if slot < 4 else (far_x, core_far_x)
        at = slot if slot < 4 else slot - 4
        copies += put(blocks[slot], shard, 3 * rep + seq, 2 * unit)
        copies += put(beside[0].at[at], shard, 3 * rep + 2 * (1 - seq), unit)
        copies += put(core_blocks[slot], shard, 3 * (1 - rep) + seq, 2 * unit)
        copies += put(beside[1].at[at], shard, 3 * (1 - rep) + 2 * (1 - seq), unit)
    for copy in copies:
        copy.wait()


def gather_ring(piece, split):
    count, rows, width = piece.shape
    shards = lax.axis_size("shard")
    unit = rows // 6
    rep, seq = lax.axis_index("rep"), lax.axis_index("seq")
    mine = lax.dynamic_slice(piece, (0, (3 * rep + seq) * unit, 0), (count, 2 * unit, width))

    def cross(blocks):
        cut = [
            lax.dynamic_slice(block, (0, seq * unit, 0), (count, unit, width)) for block in blocks
        ]
        return swap_pairs(jnp.stack(cut), "seq")

    up1, down1 = ring_step(mine, True), ring_step(mine, False)
    up2, down2 = ring_step(up1, True), ring_step(down1, False)
    near_x = cross([up1, down1, up2, down2])
    up3, down3 = ring_step(up2, True), ring_step(down2, False)
    up4, down4 = ring_step(up3[:, :unit], True), ring_step(down3[:, unit:], False)
    far = jnp.concatenate([up4, down4], axis=1)
    far_x = cross([up3, down3, far])
    parts = [up1, down1, up2, down2, up3, down3, far, near_x, far_x]
    parts += [swap_pairs(part, "rep") for part in parts]
    where = jnp.concatenate([ring_ids(), jnp.stack([rep, seq]).astype(jnp.int32)])
    plain = count - split
    shapes = []
    if plain:
        shapes.append(jax.ShapeDtypeStruct((plain, shards * rows, width), piece.dtype))
    if split:
        shapes.append(jax.ShapeDtypeStruct((shards, split, rows, width), piece.dtype))
    anywhere = pl.BlockSpec(memory_space=pl.ANY)
    return pl.pallas_call(
        functools.partial(place_kernel, plain, split),
        out_shape=tuple(shapes),
        in_specs=[pl.BlockSpec(memory_space=pltpu.SMEM)] + [anywhere] * 19,
        out_specs=(anywhere,) * len(shapes),
        scratch_shapes=[pltpu.SemaphoreType.DMA],
        cost_estimate=pl.CostEstimate(
            flops=0, transcendentals=0, bytes_accessed=2 * shards * piece.size * 2
        ),
    )(where, piece, *parts)


def gather_plain(piece, split):
    count, rows, width = piece.shape
    shards = lax.axis_size("shard")
    plain = count - split
    outs = []
    if plain:
        outs.append(lax.all_gather(piece[:plain], "shard", axis=1, tiled=True))
    if split:
        outs.append(lax.all_gather(piece[plain:], "shard", axis=0, tiled=False))
    return tuple(outs)


def ring_fits(rows):
    return (
        lax.axis_size("shard") == 8
        and lax.axis_size("rep") == 2
        and lax.axis_size("seq") == 2
        and rows % 96 == 0
    )


def gather(piece, split):
    return (gather_ring if ring_fits(piece.shape[1]) else gather_plain)(piece, split)


def add(left, right):
    return (left.astype(F32) + right.astype(F32)).astype(BF16)


def scatter_ring(grads):
    shards, count, rows, width = grads.shape
    unit = rows // 6
    rep, seq = lax.axis_index("rep"), lax.axis_index("seq")
    ids = ring_ids()

    def half(which):
        return lax.dynamic_slice(
            grads, (0, 0, 3 * unit * which, 0), (shards, count, 3 * unit, width)
        )

    paired = add(half(rep), swap_pairs(half(1 - rep), "rep"))

    def parts(offsets):
        blocks = [
            lax.dynamic_index_in_dim(paired, ids[offset % 8], 0, keepdims=False)
            for offset in offsets
        ]
        sent = jnp.stack(
            [
                lax.dynamic_slice(block, (0, 2 * (1 - seq) * unit, 0), (count, unit, width))
                for block in blocks
            ]
        )
        got = swap_pairs(sent, "seq")
        out = []
        for at, block in enumerate(blocks):
            kept = lax.dynamic_slice(block, (0, seq * unit, 0), (count, 2 * unit, width))
            zero = jnp.zeros_like(got[at])
            beside = jnp.where(
                seq == 0,
                jnp.concatenate([got[at], zero], axis=1),
                jnp.concatenate([zero, got[at]], axis=1),
            )
            out.append(add(kept, beside))
        return out

    (far,) = parts((4,))
    up3, down3 = parts((3, -3))
    up2, down2 = parts((2, -2))
    up1, down1, here = parts((1, -1, 0))
    up = ring_step(far[:, :unit], True)
    down = ring_step(far[:, unit:], False)
    up = jnp.concatenate([add(up3[:, :unit], up), up3[:, unit:]], axis=1)
    down = jnp.concatenate([down3[:, :unit], add(down3[:, unit:], down)], axis=1)
    up, down = ring_step(up, True), ring_step(down, False)
    up, down = ring_step(add(up2, up), True), ring_step(add(down2, down), False)
    up, down = ring_step(add(up1, up), True), ring_step(add(down1, down), False)
    total = (here.astype(F32) + up.astype(F32) + down.astype(F32)).astype(BF16)
    other = swap_pairs(total, "seq")
    left, right = jnp.where(seq == 0, total, other), jnp.where(seq == 0, other, total)
    mine = jnp.concatenate(
        [left[:, :unit], add(left[:, unit:], right[:, :unit]), right[:, unit:]], axis=1
    )
    other = swap_pairs(mine, "rep")
    return jnp.where(
        rep == 0,
        jnp.concatenate([mine, other], axis=1),
        jnp.concatenate([other, mine], axis=1),
    ).astype(F32)


def scatter_plain(grads):
    owned = lax.psum_scatter(grads.astype(F32), "shard", scatter_dimension=0, tiled=False)
    return lax.psum(owned.astype(BF16), ("rep", "seq")).astype(F32)


def scatter(grads):
    return (scatter_ring if ring_fits(grads.shape[2]) else scatter_plain)(grads)


def normalize(values):
    centered = values - jnp.mean(values, axis=-1, keepdims=True)
    scale = lax.rsqrt(jnp.mean(centered * centered, axis=-1, keepdims=True) + EPSILON)
    return centered * scale, scale


def norm_back(grad, normal, scale, factor):
    u = grad * (1.0 + factor)
    return (
        u
        - jnp.mean(u, axis=-1, keepdims=True)
        - normal * jnp.mean(u * normal, axis=-1, keepdims=True)
    ) * scale


def time_embed(steps, width):
    half_width = width // 2
    freqs = jnp.exp(-math.log(10000.0) * jnp.arange(half_width, dtype=F32) / half_width)
    angles = steps.astype(F32)[:, None] * freqs[None, :]
    return jnp.concatenate([jnp.cos(angles), jnp.sin(angles)], axis=-1)


def dot(left, right, left_dims, right_dims):
    return lax.dot_general(
        left, right, ((left_dims, right_dims), ((), ())), preferred_element_type=F32
    )


def split_heads(values):
    return values.reshape(values.shape[0], HEADS, values.shape[1] // HEADS)


def attend(queries, keys, values):
    q, k, v = split_heads(queries), split_heads(keys), split_heads(values)
    scale_factor = q.shape[-1] ** (-0.5)
    scores = jnp.einsum("qhd,khd->hqk", q, k, preferred_element_type=F32) * scale_factor
    top_score = jnp.max(scores, axis=-1, keepdims=True)
    expo = jnp.exp(scores - top_score)
    totals = jnp.sum(expo, axis=-1, keepdims=True)
    probs_low = (expo / totals).astype(BF16)
    mixed = jnp.einsum("hqk,khd->qhd", probs_low, v, preferred_element_type=F32)
    return mixed.reshape(queries.shape).astype(BF16), top_score + jnp.log(totals)


def attend_back(queries, keys, values, log_total, grad_mixed):
    q, k, v, g = split_heads(queries), split_heads(keys), split_heads(values), split_heads(grad_mixed)
    scale_factor = q.shape[-1] ** (-0.5)
    scores = jnp.einsum("qhd,khd->hqk", q, k, preferred_element_type=F32) * scale_factor
    probs = jnp.exp(scores - log_total)
    probs_low = probs.astype(BF16)
    grad_probs = jnp.einsum("qhd,khd->hqk", g, v, preferred_element_type=F32)
    grad_scores = probs * (grad_probs - jnp.sum(probs * grad_probs, axis=-1, keepdims=True))
    grad_low = grad_scores.astype(BF16)
    grad_q = jnp.einsum("hqk,khd->qhd", grad_low, k, preferred_element_type=F32) * scale_factor
    grad_k = jnp.einsum("hqk,qhd->khd", grad_low, q, preferred_element_type=F32) * scale_factor
    grad_v = jnp.einsum("hqk,qhd->khd", probs_low, g, preferred_element_type=F32)
    return grad_q.reshape(queries.shape), grad_k.reshape(keys.shape), grad_v.reshape(keys.shape)


def layer_forward(stream, modulation, weights, biases):
    qkv_w, proj_w, fc1_w, fc2_w = weights
    qkv_b, proj_b, fc1_b, fc2_b = biases
    width = stream.shape[-1]
    shift_attn, factor_attn, gate_attn, shift_mlp, factor_mlp, gate_mlp = modulation
    normal, scale = normalize(stream)
    normed = (normal * (1.0 + factor_attn) + shift_attn).astype(BF16)
    queries, keys, values = [
        (dot(normed, qkv_w[part], (1,), (0,)) + qkv_b[part]).astype(BF16) for part in range(3)
    ]
    own_kv = jnp.stack([keys, values])
    both_kv = jnp.concatenate([own_kv, swap_pairs(own_kv, "rep")], axis=1)
    mixed, log_total = attend(queries, both_kv[0], both_kv[1])
    attn_out = dot(mixed, proj_w, (1,), (0,)) + proj_b
    middle = stream + gate_attn * attn_out
    normal_mlp, scale_mlp = normalize(middle)
    normed_mlp = (normal_mlp * (1.0 + factor_mlp) + shift_mlp).astype(BF16)
    hidden = jnp.concatenate(
        [dot(normed_mlp, fc1_w[part], (1,), (0,)) for part in range(fc1_w.shape[0])], axis=-1
    )
    hidden = hidden + fc1_b
    activated = jax.nn.gelu(hidden, approximate=True).astype(BF16)
    mlp_out = dot(activated, fc2_w, (1,), (0,)) + fc2_b
    result = middle + gate_mlp * mlp_out
    return result, (
        stream, normed, queries, both_kv, mixed, log_total, attn_out, middle, normed_mlp, hidden,
        activated, mlp_out,
    )


def token_sum(values):
    return jnp.sum(values.astype(F32), axis=0)


def by_shard(matrix, shards):
    return matrix.reshape(shards, matrix.shape[0] // shards, matrix.shape[1])


def layer_backward(grad_out, modulation, weights, kept, shards):
    qkv_w, proj_w, fc1_w, fc2_w = weights
    (
        stream, normed, queries, both_kv, mixed, log_total, attn_out, middle, normed_mlp, hidden,
        activated, mlp_out,
    ) = kept
    width = stream.shape[-1]
    half_tokens = stream.shape[0]
    shift_attn, factor_attn, gate_attn, shift_mlp, factor_mlp, gate_mlp = modulation
    grad_gate_mlp = token_sum(grad_out * mlp_out)
    grad_mlp = (grad_out * gate_mlp).astype(BF16)
    grad_fc2_w = dot(activated, grad_mlp, (0,), (0,)).astype(BF16)
    grad_fc2_b = token_sum(grad_mlp)
    grad_activated = dot(grad_mlp, fc2_w, (1,), (1,))
    _, gelu_pull = jax.vjp(lambda v: jax.nn.gelu(v, approximate=True), hidden)
    grad_hidden = gelu_pull(grad_activated)[0].astype(BF16)
    parts = [
        grad_hidden[:, part * width : (part + 1) * width] for part in range(fc1_w.shape[0])
    ]
    grad_fc1_w = [dot(normed_mlp, part, (0,), (0,)).astype(BF16) for part in parts]
    grad_fc1_b = token_sum(grad_hidden)
    grad_normed = sum(dot(part, fc1_w[at], (1,), (1,)) for at, part in enumerate(parts))
    fc2_grads = grad_fc2_w.reshape(shards, -1, width // shards, width)
    fc1_grads = jnp.stack([by_shard(part, shards) for part in grad_fc1_w], axis=1)
    mlp_grads = scatter(jnp.concatenate([fc1_grads, fc2_grads], axis=1))
    normal, scale = normalize(middle)
    grad_shift_mlp = token_sum(grad_normed)
    grad_factor_mlp = token_sum(grad_normed * normal)
    grad_middle = grad_out + norm_back(grad_normed, normal, scale, factor_mlp)
    grad_gate_attn = token_sum(grad_middle * attn_out)
    grad_attn = (grad_middle * gate_attn).astype(BF16)
    grad_proj_w = dot(mixed, grad_attn, (0,), (0,)).astype(BF16)
    grad_proj_b = token_sum(grad_attn)
    grad_mixed = dot(grad_attn, proj_w, (1,), (1,)).astype(BF16)
    grad_q, grad_k, grad_v = attend_back(queries, both_kv[0], both_kv[1], log_total, grad_mixed)
    returned = swap_pairs(
        jnp.stack([grad_k[half_tokens:], grad_v[half_tokens:]]).astype(BF16), "rep"
    )
    grad_k = grad_k[:half_tokens] + returned[0].astype(F32)
    grad_v = grad_v[:half_tokens] + returned[1].astype(F32)
    grad_projected = [part.astype(BF16) for part in (grad_q, grad_k, grad_v)]
    grad_qkv_w = [dot(normed, part, (0,), (0,)).astype(BF16) for part in grad_projected]
    attn_grads = scatter(
        jnp.stack([by_shard(part, shards) for part in grad_qkv_w + [grad_proj_w]], axis=1)
    )
    grad_qv_b = jnp.concatenate([token_sum(grad_projected[0]), token_sum(grad_projected[2])])
    grad_normed = sum(dot(part, qkv_w[at], (1,), (1,)) for at, part in enumerate(grad_projected))
    normal, scale = normalize(stream)
    grad_shift_attn = token_sum(grad_normed)
    grad_factor_attn = token_sum(grad_normed * normal)
    grad_stream = grad_middle + norm_back(grad_normed, normal, scale, factor_attn)
    grad_modulation = jnp.concatenate(
        [
            grad_shift_attn,
            grad_factor_attn,
            grad_gate_attn,
            grad_shift_mlp,
            grad_factor_mlp,
            grad_gate_mlp,
        ]
    )
    bias_grads = [
        part.reshape(shards, -1) for part in (grad_qv_b, grad_proj_b, grad_fc1_b, grad_fc2_b)
    ]
    return grad_stream, grad_modulation, jnp.concatenate(bias_grads, axis=1), mlp_grads, attn_grads


def columns(matrix, width):
    return jnp.stack(jnp.split(matrix, matrix.shape[1] // width, axis=1))


def uncolumns(blocks):
    return jnp.concatenate(list(blocks), axis=1)


def shards_program(
    latents,
    image_loads,
    timesteps,
    classes,
    label_table,
    ada_weight,
    ada_bias,
    qkv_weight,
    qv_bias,
    proj_weight,
    proj_bias,
    fc1_weight,
    fc1_bias,
    fc2_weight,
    fc2_bias,
    cotangent,
):
    shards = lax.axis_size("shard")
    width = latents.shape[2]
    own_rows = width // shards
    ff_parts = fc1_weight.shape[2] // width
    shard, rep, seq = lax.axis_index("shard"), lax.axis_index("rep"), lax.axis_index("seq")

    one_hot = (
        classes[:, None] == jnp.arange(label_table.shape[0], dtype=jnp.int32)[None, :]
    ).astype(BF16)
    cond = dot(one_hot, label_table, (1,), (0,)) + time_embed(timesteps, width)
    cond_low = jax.nn.silu(cond).astype(BF16)
    live_own = (image_loads > 0).astype(BF16)
    shared = lax.all_gather(
        jnp.concatenate([cond_low, jnp.broadcast_to(live_own[:, None], (1, 128))], axis=1),
        ("rep", "shard"),
        axis=0,
        tiled=True,
    )
    live = lax.dynamic_slice(shared, (seq * shards + shard, width), (1, 1)).astype(F32)
    cond_rows = lax.dynamic_slice(
        shared[:, :width], (0, shard * own_rows), (shared.shape[0], own_rows)
    )
    stream = swap_layout(latents[0]).astype(F32)

    packs = []
    for layer in range(LAYERS):
        fc2_piece = fc2_weight[layer].reshape(ff_parts, own_rows, width)
        rest = jnp.concatenate(
            [proj_weight[layer][None], columns(fc1_weight[layer], width), fc2_piece]
        )
        packs.append((columns(qkv_weight[layer], width), rest))
    gathered = []
    for layer in range(LAYERS):
        (qkv_w,) = gather(packs[layer][0], 0)
        rest_w, fc2_w = gather(packs[layer][1], ff_parts)
        gathered.append((qkv_w, rest_w[0], rest_w[1:], fc2_w.reshape(ff_parts * width, width)))

    small = jnp.concatenate([ada_bias, qv_bias, proj_bias, fc1_bias, fc2_bias], axis=1)
    small = lax.all_gather(small, "shard", axis=0, tiled=False).astype(F32)
    ends = [0]
    for bias in (ada_bias, qv_bias, proj_bias, fc1_bias, fc2_bias):
        ends.append(ends[-1] + bias.shape[1])
    biases, ada_b = [], []
    for layer in range(LAYERS):
        full = [small[:, layer, ends[at] : ends[at + 1]].reshape(-1) for at in range(5)]
        ada_b.append(full[0])
        qkv_b = [full[1][:width], jnp.zeros((width,), F32), full[1][width:]]
        biases.append((qkv_b, full[2], full[3], full[4]))

    mine = lax.dynamic_slice(cond_rows, (seq * shards, 0), (shards, own_rows))
    partial = jnp.concatenate(
        [dot(mine, ada_weight[layer], (1,), (0,)) for layer in range(LAYERS)], axis=1
    )
    modulations = lax.psum_scatter(partial, "shard", scatter_dimension=0, tiled=True)[0]
    modulations = [
        jnp.split((modulations.reshape(LAYERS, -1)[layer] + ada_b[layer])[None, :], 6, axis=1)
        for layer in range(LAYERS)
    ]

    kept = []
    for layer in range(LAYERS):
        stream, layer_kept = layer_forward(stream, modulations[layer], gathered[layer], biases[layer])
        kept.append(layer_kept)
    activations = swap_layout((stream * live).astype(BF16)).astype(F32)
    grad_stream = swap_layout(cotangent[0]).astype(F32) * live

    weight_grads = [None] * LAYERS
    bias_grads = [None] * LAYERS
    ada_w_grads = [None] * LAYERS
    ada_b_grads = [None] * LAYERS
    grad_cond = 0.0
    for layer in reversed(range(LAYERS)):
        grad_stream, grad_mod, bias_grads[layer], mlp_grads, attn_grads = layer_backward(
            grad_stream, modulations[layer], gathered[layer], kept[layer], shards
        )
        weight_grads[layer] = (
            uncolumns(attn_grads[:3]),
            attn_grads[3],
            uncolumns(mlp_grads[:ff_parts]),
            mlp_grads[ff_parts:].reshape(ff_parts * own_rows, width),
        )
        grad_mod = (grad_mod + swap_pairs(grad_mod, "rep")).astype(BF16)
        all_mod = lax.all_gather(grad_mod, ("seq", "shard"), axis=0, tiled=False)
        ada_w_grads[layer] = dot(cond_rows, all_mod, (0,), (0,))
        own_mod = lax.dynamic_slice(
            all_mod, (0, shard * ada_bias.shape[1]), (all_mod.shape[0], ada_bias.shape[1])
        )
        ada_b_grads[layer] = token_sum(own_mod)
        rep_mod = lax.dynamic_slice(all_mod, (rep * shards, 0), (shards, all_mod.shape[1]))
        grad_cond = grad_cond + dot(rep_mod, ada_weight[layer], (1,), (1,))

    latent_grad = swap_layout(grad_stream.astype(BF16)).astype(F32)
    all_cond = lax.all_gather(grad_cond, "shard", axis=0, tiled=False)
    grad_cond_low = lax.dynamic_slice(all_cond, (0, shard, 0), (shards, 1, own_rows)).reshape(
        1, width
    )
    _, silu_pull = jax.vjp(jax.nn.silu, cond)
    cond_grad = silu_pull(grad_cond_low)[0]

    bias_total = lax.psum_scatter(
        jnp.concatenate(bias_grads, axis=1), "shard", scatter_dimension=0, tiled=True
    ).reshape(LAYERS, -1)
    bias_total = bias_total + swap_pairs(bias_total, "rep")
    bias_total = bias_total + swap_pairs(bias_total, "seq")
    qv_b, proj_b, fc1_b, fc2_b = [
        bias_total[:, ends[at] - ends[1] : ends[at + 1] - ends[1]] for at in range(1, 5)
    ]
    qkv_g, proj_g, fc1_g, fc2_g = [
        jnp.stack([weight_grads[layer][at] for layer in range(LAYERS)]) for at in range(4)
    ]
    return (
        activations[None],
        latent_grad[None],
        cond_grad,
        jnp.stack(ada_w_grads),
        jnp.stack(ada_b_grads),
        qkv_g,
        qv_b,
        proj_g,
        proj_b,
        fc1_g,
        fc1_b,
        fc2_g,
        fc2_b,
    )


def solution(mesh):
    tokens = P(("rep", "shard"), "seq", None)
    images = P(("rep", "shard"))
    matrix = P(None, "shard", None)
    vector = P(None, "shard")
    return jax.shard_map(
        shards_program,
        mesh=mesh,
        in_specs=(tokens, images, images, images, P())
        + (matrix, vector) * 5
        + (tokens,),
        out_specs=(tokens, tokens, P(("rep", "shard"), None)) + (matrix, vector) * 5,
        check_vma=False,
    )
```

time: 2520 us -> 2000 us (0.79)
  waiting for transfers between devices: 1840 us -> 232 us
  Pallas kernels: 0 us -> 865 us
  starting transfers between devices: 6.98 us -> 124 us
  blocking collectives: 154 us -> 211 us
  local copies, waits for them, and re-layouts: 60.3 us -> 108 us
    reduce_scatter x10 -> x0, waiting for transfers between devices: 1250 us -> none  [the longest x2 460 us: reduce_layer(): lax.psum_scatter(grads[0], 'shard', scatter_dimension=0, tiled=True)]
    pallas_call x0 -> x4, Pallas kernels: none -> 865 us  [gather_ring(): pl.pallas_call(functools.partial(place_kernel, plain, split), out_shape=t...]
    all_gather x10 -> x0, waiting for transfers between devices: 498 us -> none  [the longest x2 146 us: fetch_forward(): lax.all_gather(params[8][layer_index], 'shard', axis=0, tiled=True)]
    ppermute x4 -> x148, waiting for transfers between devices: 50.4 us -> 219 us  [the longest x64 146 us: ring_step(): lax.ppermute(value, 'shard', [(order[at], order[(at + step) % size]) for...]
    all_gather x2 -> x5, blocking collectives: 53 us -> 177 us  [the longest x2 78.8 us: shards_program(): all_mod = lax.all_gather(grad_mod, ('seq', 'shard'), axis=0, tiled=False)]
    ppermute x4 -> x148, starting transfers between devices: 5.78 us -> 124 us  [the longest x64 63.8 us: ring_step(): lax.ppermute(value, 'shard', [(order[at], order[(at + step) % size]) for...]
    convert_element_type x8 -> x59, other arithmetic: 33.7 us -> 80.8 us  [the longest x2 43.3 us: attend_back(): grad_low = grad_scores.astype(BF16)]
    psum x1 -> x0, waiting for transfers between devices: 42.7 us -> none  [reduce_layer(): lax.psum(owned[0].astype(jnp.bfloat16), ('rep', 'seq')).astype(jnp.float32)]
  transfers between devices with their start and end apart: 25 -> 149, of which waited for: 20 -> 52; matrix products, arithmetic and copies ran while one was open for 15% -> 19% of each run, Pallas kernels for 0% -> 43%
where the time goes in v1:
time: 2000 us; the launch traced here: 1990 us
  Pallas kernels  865 us (43%)
  matrix products  266 us (13%)
  waiting for transfers between devices  232 us (12%)
  blocking collectives  211 us (11%)
  other arithmetic  149 us (7%)
  starting transfers between devices  124 us (6%)
  local copies, waits for them, and re-layouts  108 us (5%)
  between operations  35.5 us (2%)
    pallas_call x4, Pallas kernels, gather_ring(): pl.pallas_call(functools.partial(place_kernel, plain, split), out_shape=t...  865 us
    ppermute x64, waiting for transfers between devices, ring_step(): lax.ppermute(value, 'shard', [(order[at], order[(at + step) % size]) for...  146 us
    dot_general x61, matrix products, dot(): lax.dot_general(left, right, ((left_dims, right_dims), ((), ())), preferr...  121 us
    all_gather x2, blocking collectives, shards_program(): all_mod = lax.all_gather(grad_mod, ('seq', 'shard'), axis=0, tiled=False)  78.8 us
    ppermute x80, waiting for transfers between devices, swap_pairs(): return lax.ppermute(value, axis, [(0, 1), (1, 0)])  72.3 us
    ppermute x64, starting transfers between devices, ring_step(): lax.ppermute(value, 'shard', [(order[at], order[(at + step) % size]) for...  63.8 us
    convert_element_type x2, other arithmetic, attend_back(): grad_low = grad_scores.astype(BF16)  43.3 us
    ppermute x80, starting transfers between devices, swap_pairs(): return lax.ppermute(value, axis, [(0, 1), (1, 0)])  42 us
  transfers between devices with their start and end apart: 149, of which 52 were waited for; matrix products, arithmetic and copies ran while one was open for 19% of the time, Pallas kernels for 43%

profile of v1, /device:TPU:0, one launch (start us, length us, event | category | flops | bytes accessed | tf_op | source)
XLA Modules:
  0.0 1990.4 jit_solution(11301411874783917755)
XLA Ops:
  19.1 32.1 %all-gather.4 = bf16[16,1,896]{2,1,0:T(2,128)(2,1)S(1)} all-gather(bf16[1,1,896]{2,1,0:T(2,128)(2,1)S(1)} %pad_bitcast_fusion), channel_id=1, replica_groups=mesh['rep'=2,'shard'=8,'seq'=2] {'rep','shard'}, dimensions={0}, use_global_device_ids=true | all-gather | bytes 30464 | tf_op jit(solution)/shard_map/all_gather | solution.py:437
  56.3 35.6 %all-gather.5 = bf16[8,2,1344]{2,1,0:T(2,128)(2,1)S(1)} all-gather(bf16[1,2,1344]{2,1,0:T(2,128)(2,1)S(1)} %bitcast.737), channel_id=2, replica_groups=mesh['rep'=2,'shard'=8,'seq'=2] {'shard'}, dimensions={0}, use_global_device_ids=true | all-gather | bytes 48384 | tf_op jit(solution)/shard_map/all_gather | solution.py:463
  110.5 13.3 all-reduce.69.cloned.1.call-done
  179.6 8.8 collective-permute-done.63.refs_4_
  206.7 109.0 %shard_map.399 = bf16[3,768,768]{2,1,0:T(8,128)(2,1)} custom-call(s32[10]{0:T(128)} %pad_add_fusion.where, bf16[3,96,768]{2,1,0:T(8,128)(2,1)} %copy-done.43, bf16[3,32,768]{2,1,0:T(8,128)(2,1)} %collective-permute-done.1.refs_1_, bf16[3,32,768]{2,1,0:T(8,128)(2,1)} %collective-permute-done.2.refs_2_, bf16[3,32,768]{2,1,0:T(8,128)(2,1)} %copy-done.99, ...), custom_call_target="tpu_custom_call" | custom-call | bytes 7077888 | tf_op jit(solution)/shard_map/pallas_call | solution.py:123
  334.8 109.0 %shard_map.401 = bf16[3,768,768]{2,1,0:T(8,128)(2,1)} custom-call(s32[10]{0:T(128)} %pad_add_fusion.where, bf16[3,96,768]{2,1,0:T(8,128)(2,1)} %copy-done.42, bf16[3,32,768]{2,1,0:T(8,128)(2,1)} %collective-permute-done.40.refs_1_, bf16[3,32,768]{2,1,0:T(8,128)(2,1)} %collective-permute-done.41.refs_2_, bf16[3,32,768]{2,1,0:T(8,128)(2,1)} %collective-permute-done.42.refs_3_, ...), custom_call_target="tpu_custom_call" | custom-call | bytes 7077888 | tf_op jit(solution)/shard_map/pallas_call | solution.py:123
  449.1 7.7 collective-permute-done.64.refs_5_
  477.3 11.9 multiply_reduce_fusion.3
  490.4 11.0 fusion
  506.3 11.7 fusion.54
  520.7 323.4 %shard_map.400 = (bf16[5,768,768]{2,1,0:T(8,128)(2,1)}, bf16[8,4,96,768]{3,2,1,0:T(8,128)(2,1)}) custom-call(s32[10]{0:T(128)} %pad_add_fusion.where, bf16[9,96,768]{2,1,0:T(8,128)(2,1)} %copy-done.41, bf16[9,32,768]{2,1,0:T(8,128)(2,1)} %collective-permute-done.21.refs_1_, bf16[9,32,768]{2,1,0:T(8,128)(2,1)} %collective-permute-done.22.refs_2_, ...), custom_call_target="tpu_custom_call" | custom-call | bytes 21233664 | tf_op jit(solution)/shard_map/pallas_call | solution.py:123
  867.0 15.6 collective-permute-done.69.refs_9_
  905.7 7.4 collective-permute-start.80
  913.9 323.4 %shard_map.402 = (bf16[5,768,768]{2,1,0:T(8,128)(2,1)}, bf16[8,4,96,768]{3,2,1,0:T(8,128)(2,1)}) custom-call(s32[10]{0:T(128)} %pad_add_fusion.where, bf16[9,96,768]{2,1,0:T(8,128)(2,1)} %copy-done.40, bf16[9,32,768]{2,1,0:T(8,128)(2,1)} %collective-permute-done.60.refs_1_, bf16[9,32,768]{2,1,0:T(8,128)(2,1)} %collective-permute-done.61.refs_2_, ...), custom_call_target="tpu_custom_call" | custom-call | bytes 21233664 | tf_op jit(solution)/shard_map/pallas_call | solution.py:123
  1246.6 11.6 multiply_reduce_fusion.2
  1258.2 11.1 fusion.1
  1269.3 10.8 fusion.53
  1291.7 10.6 convert_reduce_fusion
  1315.6 6.3 convert_reduce_fusion.3
  1326.9 12.6 fusion.28
  1339.5 17.3 multiply_reduce_fusion.1
  1356.7 21.6 %multiply_convert_fusion.1 = bf16[12,512,1024]{2,1,0:T(8,128)(2,1)} fusion(f32[12,512,1024]{2,1,0:T(8,128)} %get-tuple-element.269, f32[12,512,1024]{2,1,0:T(8,128)} %get-tuple-element.265, f32[12,512]{1,0:T(8,128)S(1)} %get-tuple-element.268, f32[12,512]{1,0:T(8,128)S(1)} %log_add_fusion.1), kind=kLoop, calls=%fused_computation.4 | loop fusion | flops 31457280 | bytes 62963712 | tf_op jit(solution)/shard_map/convert_element_type | solution.py:287
  1378.4 9.4 convert_reduce_fusion.6
  1387.8 8.5 multiply_bitcast_fusion.1
  1396.5 7.4 collective-permute-start.79
  1444.7 9.4 convert_reduce_fusion.1
  1476.8 12.4 fusion.31
  1489.3 20.4 %multiply_reduce_fusion = (f32[12,512]{1,0:T(8,128)S(1)}, f32[12,512,1024]{2,1,0:T(8,128)}) fusion(f32[12,512,1024]{2,1,0:T(8,128)} %get-tuple-element.261, f32[12,512]{1,0:T(8,128)S(1)} %copy-done.94, bf16[512,12,64]{0,2,1:T(8,128)(2,1)S(1)} %bitcast.674, bf16[1024,12,64]{0,2,1:T(8,128)(2,1)S(1)} %bitcast.676), kind=kOutput, calls=%fused_computation.2 | convolution fusion | flops 830466048 | bytes 52740096 | tf_op jit(solution)/shard_map/qhd,khd->hqk/dot_general | solution.py:285
  1509.6 21.6 %multiply_convert_fusion = bf16[12,512,1024]{2,1,0:T(8,128)(2,1)} fusion(f32[12,512,1024]{2,1,0:T(8,128)} %get-tuple-element.273, f32[12,512,1024]{2,1,0:T(8,128)} %get-tuple-element.261, f32[12,512]{1,0:T(8,128)S(1)} %get-tuple-element.272, f32[12,512]{1,0:T(8,128)S(1)} %copy-done.94), kind=kLoop, calls=%fused_computation.1 | loop fusion | flops 31457280 | bytes 62963712 | tf_op jit(solution)/shard_map/convert_element_type | solution.py:287
  1531.3 9.5 convert_reduce_fusion.10
  1540.8 8.8 multiply_bitcast_fusion
  1579.8 39.8 %all-gather.6 = bf16[16,1,4608]{2,1,0:T(2,128)(2,1)S(1)} all-gather(bf16[1,1,4608]{2,1,0:T(2,128)(2,1)S(1)} %reshape.936), channel_id=3, replica_groups=mesh['rep'=2,'shard'=8,'seq'=2] {'seq','shard'}, dimensions={0}, use_global_device_ids=true | all-gather | bytes 156672 | tf_op jit(solution)/shard_map/all_gather | solution.py:507
  1626.8 33.8 %all-reduce.66 = f32[8,1536]{1,0:T(8,128)S(1)} all-reduce(f32[8,1536]{1,0:T(8,128)S(1)} %concatenate.428), channel_id=7, replica_groups=mesh['rep'=2,'shard'=8,'seq'=2] {'shard'}, use_global_device_ids=true, to_apply=%region_47.48.clone | all-reduce | flops 12288 | bytes 98304
  1683.5 39.0 %all-gather.7 = bf16[16,1,4608]{2,1,0:T(2,128)(2,1)S(1)} all-gather(bf16[1,1,4608]{2,1,0:T(2,128)(2,1)S(1)} %reshape.938), channel_id=4, replica_groups=mesh['rep'=2,'shard'=8,'seq'=2] {'seq','shard'}, dimensions={0}, use_global_device_ids=true | all-gather | bytes 156672 | tf_op jit(solution)/shard_map/all_gather | solution.py:507
  1723.0 30.4 %all-gather.3 = f32[64,96]{1,0:T(8,128)S(1)} all-gather(f32[8,96]{1,0:T(8,128)S(1)} %convolution_add_fusion.2), channel_id=5, replica_groups=mesh['rep'=2,'shard'=8,'seq'=2] {'shard'}, dimensions={0}, use_global_device_ids=true | all-gather | bytes 27648 | tf_op jit(solution)/shard_map/all_gather | solution.py:517
  1771.5 5.6 collective-permute-done.106
  1778.3 5.6 collective-permute-done.107
  1786.9 5.6 collective-permute-done.108
  1795.1 5.1 add_convert_fusion
  1802.5 5.5 collective-permute-done.112
  1833.4 6.3 collective-permute-done.89
  1875.8 5.1 add_convert_fusion.1
  1884.4 8.0 collective-permute-done.97
  1899.6 5.4 collective-permute-done.120
  1927.0 5.5 collective-permute-done.125
  1934.5 10.8 collective-permute-done.128
  1945.6 6.6 collective-permute-done.145
  1961.3 5.8 collective-permute-done.130
  (1081 shorter events, 502.0 us)
Async XLA Ops:
  7.2 116.6 %all-reduce.69.cloned.1.call-start = ((), (), s32[]{:S(2)}) async-start(), calls=%async_computation | async-start | bytes 589824
  10.1 92.4 %collective-permute-start.41 = (bf16[3,32,768]{2,1,0:T(8,128)(2,1)}, bf16[3,32,768]{2,1,0:T(8,128)(2,1)}, u32[]{:S(2)}, u32[]{:S(2)}) collective-permute-start(bf16[3,32,768]{2,1,0:T(8,128)(2,1)} %constant_dynamic-slice_fusion.42), channel_id=1, source_target_pairs={{0,2},{4,0},{8,4},{12,8},{14,12},{10,14},{6,10},{2,6},{1,3},{5,1},... | collective-permute-start | bytes 442376 | tf_op jit(solution)/shard_map/ppermute | solution.py:35
  13.1 90.3 %collective-permute-start.40 = (bf16[3,32,768]{2,1,0:T(8,128)(2,1)}, bf16[3,32,768]{2,1,0:T(8,128)(2,1)}, u32[]{:S(2)}, u32[]{:S(2)}) collective-permute-start(bf16[3,32,768]{2,1,0:T(8,128)(2,1)} %constant_dynamic-slice_fusion.42), channel_id=1, source_target_pairs={{0,4},{4,8},{8,12},{12,14},{14,10},{10,6},{6,2},{2,0},{1,5},{5,9},... | collective-permute-start | bytes 442376 | tf_op jit(solution)/shard_map/ppermute | solution.py:35
  14.6 91.9 %collective-permute-start.2 = (bf16[3,32,768]{2,1,0:T(8,128)(2,1)}, bf16[3,32,768]{2,1,0:T(8,128)(2,1)}, u32[]{:S(2)}, u32[]{:S(2)}) collective-permute-start(bf16[3,32,768]{2,1,0:T(8,128)(2,1)} %constant_dynamic-slice_fusion.44), channel_id=1, source_target_pairs={{0,2},{4,0},{8,4},{12,8},{14,12},{10,14},{6,10},{2,6},{1,3},{5,1},... | collective-permute-start | bytes 442376 | tf_op jit(solution)/shard_map/ppermute | solution.py:35
  16.6 90.9 %collective-permute-start.1 = (bf16[3,32,768]{2,1,0:T(8,128)(2,1)}, bf16[3,32,768]{2,1,0:T(8,128)(2,1)}, u32[]{:S(2)}, u32[]{:S(2)}) collective-permute-start(bf16[3,32,768]{2,1,0:T(8,128)(2,1)} %constant_dynamic-slice_fusion.44), channel_id=1, source_target_pairs={{0,4},{4,8},{8,12},{12,14},{14,10},{10,6},{6,2},{2,0},{1,5},{5,9},... | collective-permute-start | bytes 442376 | tf_op jit(solution)/shard_map/ppermute | solution.py:35
  56.2 97.2 %collective-permute-start.61 = (bf16[9,32,768]{2,1,0:T(8,128)(2,1)}, bf16[9,32,768]{2,1,0:T(8,128)(2,1)}, u32[]{:S(2)}, u32[]{:S(2)}) collective-permute-start(bf16[9,32,768]{2,1,0:T(8,128)(2,1)} %constant_dynamic-slice_fusion.41), channel_id=1, source_target_pairs={{0,2},{4,0},{8,4},{12,8},{14,12},{10,14},{6,10},{2,6},{1,3},{5,1},... | collective-permute-start | bytes 1327112 | tf_op jit(solution)/shard_map/ppermute | solution.py:35
  102.5 55.5 %collective-permute-start.60 = (bf16[9,32,768]{2,1,0:T(8,128)(2,1)}, bf16[9,32,768]{2,1,0:T(8,128)(2,1)}, u32[]{:S(2)}, u32[]{:S(2)}) collective-permute-start(bf16[9,32,768]{2,1,0:T(8,128)(2,1)} %constant_dynamic-slice_fusion.41), channel_id=1, source_target_pairs={{0,4},{4,8},{8,12},{12,14},{14,10},{10,6},{6,2},{2,0},{1,5},{5,9},... | collective-permute-start | bytes 1327112 | tf_op jit(solution)/shard_map/ppermute | solution.py:35
  103.4 56.5 %collective-permute-start.22 = (bf16[9,32,768]{2,1,0:T(8,128)(2,1)S(1)}, bf16[9,32,768]{2,1,0:T(8,128)(2,1)}, u32[]{:S(2)}, u32[]{:S(2)}) collective-permute-start(bf16[9,32,768]{2,1,0:T(8,128)(2,1)S(1)} %constant_dynamic-slice_fusion.43), channel_id=1, source_target_pairs={{0,2},{4,0},{8,4},{12,8},{14,12},{10,14},{6,10},{2,6},{1,3},{5,1},... | collective-permute-start | bytes 1327112 | tf_op jit(solution)/shard_map/ppermute | solution.py:35
  106.6 58.4 %collective-permute-start.21 = (bf16[9,32,768]{2,1,0:T(8,128)(2,1)S(1)}, bf16[9,32,768]{2,1,0:T(8,128)(2,1)}, u32[]{:S(2)}, u32[]{:S(2)}) collective-permute-start(bf16[9,32,768]{2,1,0:T(8,128)(2,1)S(1)} %constant_dynamic-slice_fusion.43), channel_id=1, source_target_pairs={{0,4},{4,8},{8,12},{12,14},{14,10},{10,6},{6,2},{2,0},{1,5},{5,9},... | collective-permute-start | bytes 1327112 | tf_op jit(solution)/shard_map/ppermute | solution.py:35
  157.4 32.9 %collective-permute-start.12 = (bf16[3,32,768]{2,1,0:T(8,128)(2,1)}, bf16[3,32,768]{2,1,0:T(8,128)(2,1)S(1)}, u32[]{:S(2)}, u32[]{:S(2)}) collective-permute-start(bf16[3,32,768]{2,1,0:T(8,128)(2,1)} %collective-permute-done.2.refs_2_), channel_id=1, source_target_pairs={{0,16},{16,0},{1,17},{17,1},{2,18},{18,2},{3,19},{19,3},{4,20},{20... | collective-permute-start | bytes 442376 | tf_op jit(solution)/shard_map/ppermute | solution.py:19
  159.9 31.3 %collective-permute-start.9 = (bf16[4,3,16,768]{3,2,1,0:T(8,128)(2,1)S(1)}, bf16[4,3,16,768]{3,2,1,0:T(8,128)(2,1)S(1)}, u32[]{:S(2)}, u32[]{:S(2)}) collective-permute-start(bf16[4,3,16,768]{3,2,1,0:T(8,128)(2,1)S(1)} %pad_maximum_fusion.32), channel_id=1, source_target_pairs={{0,1},{1,0},{2,3},{3,2},{4,5},{5,4},{6,7},{7,6},{8,9},{9,8},{10,11... | collective-permute-start | bytes 884744 | tf_op jit(solution)/shard_map/ppermute | solution.py:19
  203.3 114.7 %collective-permute-start.51 = (bf16[3,32,768]{2,1,0:T(8,128)(2,1)}, bf16[3,32,768]{2,1,0:T(8,128)(2,1)S(1)}, u32[]{:S(2)}, u32[]{:S(2)}) collective-permute-start(bf16[3,32,768]{2,1,0:T(8,128)(2,1)} %collective-permute-done.41.refs_2_), channel_id=1, source_target_pairs={{0,16},{16,0},{1,17},{17,1},{2,18},{18,2},{3,19},{19,3},{4,20},{20... | collective-permute-start | bytes 442376 | tf_op jit(solution)/shard_map/ppermute | solution.py:19
  203.9 114.4 %collective-permute-start.50 = (bf16[3,32,768]{2,1,0:T(8,128)(2,1)}, bf16[3,32,768]{2,1,0:T(8,128)(2,1)}, u32[]{:S(2)}, u32[]{:S(2)}) collective-permute-start(bf16[3,32,768]{2,1,0:T(8,128)(2,1)} %collective-permute-done.40.refs_1_), channel_id=1, source_target_pairs={{0,16},{16,0},{1,17},{17,1},{2,18},{18,2},{3,19},{19,3},{4,20},{20... | collective-permute-start | bytes 442376 | tf_op jit(solution)/shard_map/ppermute | solution.py:19
  204.0 115.3 %collective-permute-start.48 = (bf16[4,3,16,768]{3,2,1,0:T(8,128)(2,1)}, bf16[4,3,16,768]{3,2,1,0:T(8,128)(2,1)S(1)}, u32[]{:S(2)}, u32[]{:S(2)}) collective-permute-start(bf16[4,3,16,768]{3,2,1,0:T(8,128)(2,1)} %pad_maximum_fusion.33), channel_id=1, source_target_pairs={{0,1},{1,0},{2,3},{3,2},{4,5},{5,4},{6,7},{7,6},{8,9},{9,8},{10,11... | collective-permute-start | bytes 884744 | tf_op jit(solution)/shard_map/ppermute | solution.py:19
  205.3 113.3 %collective-permute-start.53 = (bf16[3,32,768]{2,1,0:T(8,128)(2,1)S(1)}, bf16[3,32,768]{2,1,0:T(8,128)(2,1)}, u32[]{:S(2)}, u32[]{:S(2)}) collective-permute-start(bf16[3,32,768]{2,1,0:T(8,128)(2,1)S(1)} %collective-permute-done.43.refs_4_), channel_id=1, source_target_pairs={{0,16},{16,0},{1,17},{17,1},{2,18},{18,2},{3,19},{19,3},{4,20},{20... | collective-permute-start | bytes 442376 | tf_op jit(solution)/shard_map/ppermute | solution.py:19
  206.3 114.9 %collective-permute-start.52 = (bf16[3,32,768]{2,1,0:T(8,128)(2,1)}, bf16[3,32,768]{2,1,0:T(8,128)(2,1)}, u32[]{:S(2)}, u32[]{:S(2)}) collective-permute-start(bf16[3,32,768]{2,1,0:T(8,128)(2,1)} %collective-permute-done.42.refs_3_), channel_id=1, source_target_pairs={{0,16},{16,0},{1,17},{17,1},{2,18},{18,2},{3,19},{19,3},{4,20},{20... | collective-permute-start | bytes 442376 | tf_op jit(solution)/shard_map/ppermute | solution.py:19
  326.2 117.7 %collective-permute-start.65 = (bf16[9,32,768]{2,1,0:T(8,128)(2,1)}, bf16[9,32,768]{2,1,0:T(8,128)(2,1)S(1)}, u32[]{:S(2)}, u32[]{:S(2)}) collective-permute-start(bf16[9,32,768]{2,1,0:T(8,128)(2,1)} %collective-permute-done.63.refs_4_), channel_id=1, source_target_pairs={{0,2},{4,0},{8,4},{12,8},{14,12},{10,14},{6,10},{2,6},{1,3},{5,1},... | collective-permute-start | bytes 1327112 | tf_op jit(solution)/shard_map/ppermute | solution.py:35
  328.1 116.0 %collective-permute-start.26 = (bf16[9,32,768]{2,1,0:T(8,128)(2,1)}, bf16[9,32,768]{2,1,0:T(8,128)(2,1)}, u32[]{:S(2)}, u32[]{:S(2)}) collective-permute-start(bf16[9,32,768]{2,1,0:T(8,128)(2,1)} %collective-permute-done.24.refs_4_), channel_id=1, source_target_pairs={{0,2},{4,0},{8,4},{12,8},{14,12},{10,14},{6,10},{2,6},{1,3},{5,1},... | collective-permute-start | bytes 1327112 | tf_op jit(solution)/shard_map/ppermute | solution.py:35
  333.0 156.2 %collective-permute-start.32 = (bf16[9,32,768]{2,1,0:T(8,128)(2,1)}, bf16[9,32,768]{2,1,0:T(8,128)(2,1)}, u32[]{:S(2)}, u32[]{:S(2)}) collective-permute-start(bf16[9,32,768]{2,1,0:T(8,128)(2,1)} %collective-permute-done.22.refs_2_), channel_id=1, source_target_pairs={{0,16},{16,0},{1,17},{17,1},{2,18},{18,2},{3,19},{19,3},{4,20},{20... | collective-permute-start | bytes 1327112 | tf_op jit(solution)/shard_map/ppermute | solution.py:19
  333.1 170.0 %collective-permute-start.31 = (bf16[9,32,768]{2,1,0:T(8,128)(2,1)}, bf16[9,32,768]{2,1,0:T(8,128)(2,1)}, u32[]{:S(2)}, u32[]{:S(2)}) collective-permute-start(bf16[9,32,768]{2,1,0:T(8,128)(2,1)} %collective-permute-done.21.refs_1_), channel_id=1, source_target_pairs={{0,16},{16,0},{1,17},{17,1},{2,18},{18,2},{3,19},{19,3},{4,20},{20... | collective-permute-start | bytes 1327112 | tf_op jit(solution)/shard_map/ppermute | solution.py:19
  333.5 113.2 %collective-permute-start.25 = (bf16[9,32,768]{2,1,0:T(8,128)(2,1)}, bf16[9,32,768]{2,1,0:T(8,128)(2,1)}, u32[]{:S(2)}, u32[]{:S(2)}) collective-permute-start(bf16[9,32,768]{2,1,0:T(8,128)(2,1)} %collective-permute-done.23.refs_3_), channel_id=1, source_target_pairs={{0,4},{4,8},{8,12},{12,14},{14,10},{10,6},{6,2},{2,0},{1,5},{5,9},... | collective-permute-start | bytes 1327112 | tf_op jit(solution)/shard_map/ppermute | solution.py:35
  444.0 29.0 %collective-permute-start.20 = (bf16[2,512,768]{2,1,0:T(8,128)(2,1)S(1)}, bf16[2,512,768]{2,1,0:T(8,128)(2,1)S(1)}, u32[]{:S(2)}, u32[]{:S(2)}) collective-permute-start(bf16[2,512,768]{2,1,0:T(8,128)(2,1)S(1)} %pad_maximum_fusion.8), channel_id=1, source_target_pairs={{0,16},{16,0},{1,17},{17,1},{2,18},{18,2},{3,19},{19,3},{4,20},{20... | collective-permute-start | bytes 4718600 | tf_op jit(solution)/shard_map/ppermute | solution.py:19
  469.8 34.0 %collective-permute-start.29 = (bf16[4,9,16,768]{3,2,1,0:T(8,128)(2,1)}, bf16[4,9,16,768]{3,2,1,0:T(8,128)(2,1)}, u32[]{:S(2)}, u32[]{:S(2)}) collective-permute-start(bf16[4,9,16,768]{3,2,1,0:T(8,128)(2,1)} %pad_maximum_fusion.12), channel_id=1, source_target_pairs={{0,1},{1,0},{2,3},{3,2},{4,5},{5,4},{6,7},{7,6},{8,9},{9,8},{10,11... | collective-permute-start | bytes 2654216 | tf_op jit(solution)/shard_map/ppermute | solution.py:19
  471.4 31.8 %collective-permute-start.34 = (bf16[9,32,768]{2,1,0:T(8,128)(2,1)}, bf16[9,32,768]{2,1,0:T(8,128)(2,1)}, u32[]{:S(2)}, u32[]{:S(2)}) collective-permute-start(bf16[9,32,768]{2,1,0:T(8,128)(2,1)} %collective-permute-done.24.refs_4_), channel_id=1, source_target_pairs={{0,16},{16,0},{1,17},{17,1},{2,18},{18,2},{3,19},{19,3},{4,20},{20... | collective-permute-start | bytes 1327112 | tf_op jit(solution)/shard_map/ppermute | solution.py:19
  473.0 30.7 %collective-permute-start.33 = (bf16[9,32,768]{2,1,0:T(8,128)(2,1)}, bf16[9,32,768]{2,1,0:T(8,128)(2,1)}, u32[]{:S(2)}, u32[]{:S(2)}) collective-permute-start(bf16[9,32,768]{2,1,0:T(8,128)(2,1)} %collective-permute-done.23.refs_3_), channel_id=1, source_target_pairs={{0,16},{16,0},{1,17},{17,1},{2,18},{18,2},{3,19},{19,3},{4,20},{20... | collective-permute-start | bytes 1327112 | tf_op jit(solution)/shard_map/ppermute | solution.py:19
  518.8 346.7 %collective-permute-start.71 = (bf16[9,32,768]{2,1,0:T(8,128)(2,1)}, bf16[9,32,768]{2,1,0:T(8,128)(2,1)}, u32[]{:S(2)}, u32[]{:S(2)}) collective-permute-start(bf16[9,32,768]{2,1,0:T(8,128)(2,1)} %collective-permute-done.61.refs_2_), channel_id=1, source_target_pairs={{0,16},{16,0},{1,17},{17,1},{2,18},{18,2},{3,19},{19,3},{4,20},{20... | collective-permute-start | bytes 1327112 | tf_op jit(solution)/shard_map/ppermute | solution.py:19
  519.3 347.0 %collective-permute-start.70 = (bf16[9,32,768]{2,1,0:T(8,128)(2,1)}, bf16[9,32,768]{2,1,0:T(8,128)(2,1)}, u32[]{:S(2)}, u32[]{:S(2)}) collective-permute-start(bf16[9,32,768]{2,1,0:T(8,128)(2,1)} %collective-permute-done.60.refs_1_), channel_id=1, source_target_pairs={{0,16},{16,0},{1,17},{17,1},{2,18},{18,2},{3,19},{19,3},{4,20},{20... | collective-permute-start | bytes 1327112 | tf_op jit(solution)/shard_map/ppermute | solution.py:19
  519.4 347.5 %collective-permute-start.68 = (bf16[4,9,16,768]{3,2,1,0:T(8,128)(2,1)}, bf16[4,9,16,768]{3,2,1,0:T(8,128)(2,1)}, u32[]{:S(2)}, u32[]{:S(2)}) collective-permute-start(bf16[4,9,16,768]{3,2,1,0:T(8,128)(2,1)} %pad_maximum_fusion.13), channel_id=1, source_target_pairs={{0,1},{1,0},{2,3},{3,2},{4,5},{5,4},{6,7},{7,6},{8,9},{9,8},{10,11... | collective-permute-start | bytes 2654216 | tf_op jit(solution)/shard_map/ppermute | solution.py:19
  520.6 345.8 %collective-permute-start.73 = (bf16[9,32,768]{2,1,0:T(8,128)(2,1)}, bf16[9,32,768]{2,1,0:T(8,128)(2,1)}, u32[]{:S(2)}, u32[]{:S(2)}) collective-permute-start(bf16[9,32,768]{2,1,0:T(8,128)(2,1)} %collective-permute-done.63.refs_4_), channel_id=1, source_target_pairs={{0,16},{16,0},{1,17},{17,1},{2,18},{18,2},{3,19},{19,3},{4,20},{20... | collective-permute-start | bytes 1327112 | tf_op jit(solution)/shard_map/ppermute | solution.py:19
  864.0 373.3 %collective-permute-start.59 = (bf16[2,512,768]{2,1,0:T(8,128)(2,1)}, bf16[2,512,768]{2,1,0:T(8,128)(2,1)}, u32[]{:S(2)}, u32[]{:S(2)}) collective-permute-start(bf16[2,512,768]{2,1,0:T(8,128)(2,1)} %pad_maximum_fusion.9), channel_id=1, source_target_pairs={{0,16},{16,0},{1,17},{17,1},{2,18},{18,2},{3,19},{19,3},{4,20},{20... | collective-permute-start | bytes 4718600 | tf_op jit(solution)/shard_map/ppermute | solution.py:19
  866.3 33.5 %collective-permute-start.72 = (bf16[9,32,768]{2,1,0:T(8,128)(2,1)S(1)}, bf16[9,32,768]{2,1,0:T(8,128)(2,1)}, u32[]{:S(2)}, u32[]{:S(2)}) collective-permute-start(bf16[9,32,768]{2,1,0:T(8,128)(2,1)S(1)} %copy-done.73), channel_id=1, source_target_pairs={{0,16},{16,0},{1,17},{17,1},{2,18},{18,2},{3,19},{19,3},{4,20},{20... | collective-permute-start | bytes 1327112 | tf_op jit(solution)/shard_map/ppermute | solution.py:19
  866.4 34.1 %collective-permute-start.75 = (bf16[9,32,768]{2,1,0:T(8,128)(2,1)S(1)}, bf16[9,32,768]{2,1,0:T(8,128)(2,1)}, u32[]{:S(2)}, u32[]{:S(2)}) collective-permute-start(bf16[9,32,768]{2,1,0:T(8,128)(2,1)S(1)} %collective-permute-done.65.refs_6_), channel_id=1, source_target_pairs={{0,16},{16,0},{1,17},{17,1},{2,18},{18,2},{3,19},{19,3},{4,20},{20... | collective-permute-start | bytes 1327112 | tf_op jit(solution)/shard_map/ppermute | solution.py:19
  866.9 46.3 %collective-permute-start.77 = (bf16[4,9,16,768]{3,2,1,0:T(8,128)(2,1)}, bf16[4,9,16,768]{3,2,1,0:T(8,128)(2,1)}, u32[]{:S(2)}, u32[]{:S(2)}) collective-permute-start(bf16[4,9,16,768]{3,2,1,0:T(8,128)(2,1)} %collective-permute-done.68.refs_8_), channel_id=1, source_target_pairs={{0,16},{16,0},{1,17},{17,1},{2,18},{18,2},{3,19},{19,3},{4,20},{20... | collective-permute-start | bytes 2654216 | tf_op jit(solution)/shard_map/ppermute | solution.py:19
  882.6 30.6 %collective-permute-start.78 = (bf16[3,9,16,768]{3,2,1,0:T(8,128)(2,1)}, bf16[3,9,16,768]{3,2,1,0:T(8,128)(2,1)}, u32[]{:S(2)}, u32[]{:S(2)}) collective-permute-start(bf16[3,9,16,768]{3,2,1,0:T(8,128)(2,1)} %collective-permute-done.69.refs_9_), channel_id=1, source_target_pairs={{0,16},{16,0},{1,17},{17,1},{2,18},{18,2},{3,19},{19,3},{4,20},{20... | collective-permute-start | bytes 1990664 | tf_op jit(solution)/shard_map/ppermute | solution.py:19
  905.7 386.0 %collective-permute-start.80 = (bf16[512,768]{1,0:T(8,128)(2,1)}, bf16[512,768]{1,0:T(8,128)(2,1)}, u32[]{:S(2)}, u32[]{:S(2)}) collective-permute-start(bf16[512,768]{1,0:T(8,128)(2,1)} %bitcast.747), channel_id=1, source_target_pairs={{0,0},{1,16},{16,1},{17,17},{2,2},{3,18},{18,3},{19,19},{4,4},{5,2... | collective-permute-start | bytes 2359304 | tf_op jit(solution)/shard_map/ppermute | solution.py:23
  1396.5 33.3 %collective-permute-start.79 = (bf16[512,768]{1,0:T(8,128)(2,1)}, bf16[512,768]{1,0:T(8,128)(2,1)}, u32[]{:S(2)}, u32[]{:S(2)}) collective-permute-start(bf16[512,768]{1,0:T(8,128)(2,1)} %get-tuple-element.148), channel_id=1, source_target_pairs={{0,0},{1,16},{16,1},{17,17},{2,2},{3,18},{18,3},{19,19},{4,4},{5,2... | collective-permute-start | bytes 2359304 | tf_op jit(solution)/shard_map/ppermute | solution.py:23
  1422.6 372.5 %collective-permute-start.133 = (bf16[8,8,48,768]{3,2,1,0:T(8,128)(2,1)}, bf16[8,8,48,768]{3,2,1,0:T(8,128)(2,1)}, u32[]{:S(2)}, u32[]{:S(2)}) collective-permute-start(bf16[8,8,48,768]{3,2,1,0:T(8,128)(2,1)} %constant_dynamic-slice_fusion.9), channel_id=1, source_target_pairs={{0,16},{16,0},{1,17},{17,1},{2,18},{18,2},{3,19},{19,3},{4,20},{20... | collective-permute-start | bytes 14155784 | tf_op jit(solution)/shard_map/ppermute | solution.py:19
  1553.8 26.0 %collective-permute-start.84 = (f32[4608]{0:T(1024)S(1)}, f32[4608]{0:T(1024)S(1)}, u32[]{:S(2)}, u32[]{:S(2)}) collective-permute-start(f32[4608]{0:T(1024)S(1)} %constant_dynamic-update-slice_fusion.22), channel_id=1, source_target_pairs={{0,16},{16,0},{1,17},{17,1},{2,18},{18,2},{3,19},{19,3},{4,20},{20... | collective-permute-start | bytes 55304 | tf_op jit(solution)/shard_map/ppermute | solution.py:19
  1558.6 201.4 %collective-permute-start.101 = (bf16[8,4,48,768]{3,2,1,0:T(8,128)(2,1)}, bf16[8,4,48,768]{3,2,1,0:T(8,128)(2,1)}, u32[]{:S(2)}, u32[]{:S(2)}) collective-permute-start(bf16[8,4,48,768]{3,2,1,0:T(8,128)(2,1)} %constant_dynamic-slice_fusion.27), channel_id=1, source_target_pairs={{0,16},{16,0},{1,17},{17,1},{2,18},{18,2},{3,19},{19,3},{4,20},{20... | collective-permute-start | bytes 7077896 | tf_op jit(solution)/shard_map/ppermute | solution.py:19
  1568.9 306.9 %collective-permute-start.118 = (bf16[8,8,48,768]{3,2,1,0:T(8,128)(2,1)}, bf16[8,8,48,768]{3,2,1,0:T(8,128)(2,1)}, u32[]{:S(2)}, u32[]{:S(2)}) collective-permute-start(bf16[8,8,48,768]{3,2,1,0:T(8,128)(2,1)} %constant_dynamic-slice_fusion.11), channel_id=1, source_target_pairs={{0,16},{16,0},{1,17},{17,1},{2,18},{18,2},{3,19},{19,3},{4,20},{20... | collective-permute-start | bytes 14155784 | tf_op jit(solution)/shard_map/ppermute | solution.py:19
  1575.3 47.4 %collective-permute-start.82 = (bf16[2,512,768]{1,2,0:T(8,128)(2,1)}, bf16[2,512,768]{1,2,0:T(8,128)(2,1)}, u32[]{:S(2)}, u32[]{:S(2)}) collective-permute-start(bf16[2,512,768]{1,2,0:T(8,128)(2,1)} %pad_maximum_fusion.11), channel_id=1, source_target_pairs={{0,16},{16,0},{1,17},{17,1},{2,18},{18,2},{3,19},{19,3},{4,20},{20... | collective-permute-start | bytes 4718600 | tf_op jit(solution)/shard_map/ppermute | solution.py:19
  1678.6 85.9 %collective-permute-start.83 = (bf16[512,768]{1,0:T(8,128)(2,1)}, bf16[512,768]{1,0:T(8,128)(2,1)S(1)}, u32[]{:S(2)}, u32[]{:S(2)}) collective-permute-start(bf16[512,768]{1,0:T(8,128)(2,1)} %get-tuple-element.158), channel_id=1, source_target_pairs={{0,0},{1,16},{16,1},{17,17},{2,2},{3,18},{18,3},{19,19},{4,4},{5,2... | collective-permute-start | bytes 2359304 | tf_op jit(solution)/shard_map/ppermute | solution.py:23
  1682.2 147.5 %collective-permute-start.86 = (bf16[8,4,48,768]{3,2,1,0:T(8,128)(2,1)}, bf16[8,4,48,768]{3,2,1,0:T(8,128)(2,1)}, u32[]{:S(2)}, u32[]{:S(2)}) collective-permute-start(bf16[8,4,48,768]{3,2,1,0:T(8,128)(2,1)} %constant_dynamic-slice_fusion.36), channel_id=1, source_target_pairs={{0,16},{16,0},{1,17},{17,1},{2,18},{18,2},{3,19},{19,3},{4,20},{20... | collective-permute-start | bytes 7077896 | tf_op jit(solution)/shard_map/ppermute | solution.py:19
  1792.9 25.0 %collective-permute-start.109 = (bf16[4,32,768]{2,1,0:T(8,128)(2,1)S(1)}, bf16[4,32,768]{2,1,0:T(8,128)(2,1)S(1)}, u32[]{:S(2)}, u32[]{:S(2)}) collective-permute-start(bf16[4,32,768]{2,1,0:T(8,128)(2,1)S(1)} %get-tuple-element.136), channel_id=1, source_target_pairs={{0,4},{4,8},{8,12},{12,14},{14,10},{10,6},{6,2},{2,0},{1,5},{5,9},... | collective-permute-start | bytes 589832 | tf_op jit(solution)/shard_map/ppermute | solution.py:35
  1823.5 44.6 %collective-permute-start.142 = (bf16[8,16,768]{2,1,0:T(8,128)(2,1)S(1)}, bf16[8,16,768]{2,1,0:T(8,128)(2,1)S(1)}, u32[]{:S(2)}, u32[]{:S(2)}) collective-permute-start(bf16[8,16,768]{2,1,0:T(8,128)(2,1)S(1)} %get-tuple-element.211), channel_id=1, source_target_pairs={{0,2},{4,0},{8,4},{12,8},{14,12},{10,14},{6,10},{2,6},{1,3},{5,1},... | collective-permute-start | bytes 589832 | tf_op jit(solution)/shard_map/ppermute | solution.py:35
  1868.2 77.3 %collective-permute-start.141 = (bf16[8,32,768]{2,1,0:T(8,128)(2,1)S(1)}, bf16[8,32,768]{2,1,0:T(8,128)(2,1)S(1)}, u32[]{:S(2)}, u32[]{:S(2)}) collective-permute-start(bf16[8,32,768]{2,1,0:T(8,128)(2,1)S(1)} %get-tuple-element.94), channel_id=1, source_target_pairs={{0,4},{4,8},{8,12},{12,14},{14,10},{10,6},{6,2},{2,0},{1,5},{5,9},... | collective-permute-start | bytes 1179656 | tf_op jit(solution)/shard_map/ppermute | solution.py:35
  1873.6 37.1 %collective-permute-start.94 = (bf16[4,32,768]{2,1,0:T(8,128)(2,1)S(1)}, bf16[4,32,768]{2,1,0:T(8,128)(2,1)S(1)}, u32[]{:S(2)}, u32[]{:S(2)}) collective-permute-start(bf16[4,32,768]{2,1,0:T(8,128)(2,1)S(1)} %get-tuple-element.124), channel_id=1, source_target_pairs={{0,4},{4,8},{8,12},{12,14},{14,10},{10,6},{6,2},{2,0},{1,5},{5,9},... | collective-permute-start | bytes 589832 | tf_op jit(solution)/shard_map/ppermute | solution.py:35
  1898.9 34.4 %collective-permute-start.144 = (bf16[8,32,768]{2,1,0:T(8,128)(2,1)S(1)}, bf16[8,32,768]{2,1,0:T(8,128)(2,1)S(1)}, u32[]{:S(2)}, u32[]{:S(2)}) collective-permute-start(bf16[8,32,768]{2,1,0:T(8,128)(2,1)S(1)} %add_convert_fusion.17), channel_id=1, source_target_pairs={{0,2},{4,0},{8,4},{12,8},{14,12},{10,14},{6,10},{2,6},{1,3},{5,1},... | collective-permute-start | bytes 1179656 | tf_op jit(solution)/shard_map/ppermute | solution.py:35
  (295 other events, 7198.1 us)
Sparse Core Ops, SparseCore 0:
  53.4 70.3 all-reduce.68

commit v2 on v1

--- a/solution.py
+++ b/solution.py
@@ -21,6 +21,35 @@
 
 def swap_layout(value):
     return lax.ppermute(value, ("rep", "seq"), [(0, 0), (1, 2), (2, 1), (3, 3)])
+
+
+def cube_pairs(value, axis, bit):
+    return lax.ppermute(value, axis, [(at, at ^ bit) for at in range(lax.axis_size(axis))])
+
+
+def cube_bits(axis):
+    return [1 << place for place in range(lax.axis_size(axis).bit_length() - 1)]
+
+
+def cube_gather(value, axes):
+    value = value[None]
+    for axis in reversed(axes):
+        for bit in cube_bits(axis):
+            other = cube_pairs(value, axis, bit)
+            value = jnp.where(
+                lax.axis_index(axis) & bit == 0,
+                jnp.concatenate([value, other]),
+                jnp.concatenate([other, value]),
+            )
+    return value
+
+
+def cube_scatter(value, axis):
+    for bit in reversed(cube_bits(axis)):
+        low, high = value[:bit], value[bit:]
+        first = lax.axis_index(axis) & bit == 0
+        value = jnp.where(first, low, high) + cube_pairs(jnp.where(first, high, low), axis, bit)
+    return value[0]
 
 
 def ring_order(size):
@@ -124,7 +153,8 @@
         functools.partial(place_kernel, plain, split),
         out_shape=tuple(shapes),
         in_specs=[pl.BlockSpec(memory_space=pltpu.SMEM)] + [anywhere] * 19,
-        out_specs=(anywhere,) * len(shapes),
+        out_specs=(pl.BlockSpec(memory_space=pltpu.VMEM),) * len(shapes),
+        compiler_params=pltpu.CompilerParams(vmem_limit_bytes=32 * 2**20),
         scratch_shapes=[pltpu.SemaphoreType.DMA],
         cost_estimate=pl.CostEstimate(
             flops=0, transcendentals=0, bytes_accessed=2 * shards * piece.size * 2
@@ -172,50 +202,56 @@
             grads, (0, 0, 3 * unit * which, 0), (shards, count, 3 * unit, width)
         )
 
-    paired = add(half(rep), swap_pairs(half(1 - rep), "rep"))
-
-    def parts(offsets):
-        blocks = [
-            lax.dynamic_index_in_dim(paired, ids[offset % 8], 0, keepdims=False)
+    (got,) = yield (swap_pairs(half(1 - rep), "rep"),)
+    paired = add(half(rep), got)
+
+    def block(offset):
+        return lax.dynamic_index_in_dim(paired, ids[offset % 8], 0, keepdims=False)
+
+    def send(offsets):
+        sent = [
+            lax.dynamic_slice(block(offset), (0, 2 * (1 - seq) * unit, 0), (count, unit, width))
             for offset in offsets
         ]
-        sent = jnp.stack(
-            [
-                lax.dynamic_slice(block, (0, 2 * (1 - seq) * unit, 0), (count, unit, width))
-                for block in blocks
-            ]
+        return swap_pairs(jnp.stack(sent), "seq")
+
+    def join(offset, got):
+        kept = lax.dynamic_slice(block(offset), (0, seq * unit, 0), (count, 2 * unit, width))
+        zero = jnp.zeros_like(got)
+        beside = jnp.where(
+            seq == 0,
+            jnp.concatenate([got, zero], axis=1),
+            jnp.concatenate([zero, got], axis=1),
         )
-        got = swap_pairs(sent, "seq")
-        out = []
-        for at, block in enumerate(blocks):
-            kept = lax.dynamic_slice(block, (0, seq * unit, 0), (count, 2 * unit, width))
-            zero = jnp.zeros_like(got[at])
-            beside = jnp.where(
-                seq == 0,
-                jnp.concatenate([got[at], zero], axis=1),
-                jnp.concatenate([zero, got[at]], axis=1),
-            )
-            out.append(add(kept, beside))
-        return out
-
-    (far,) = parts((4,))
-    up3, down3 = parts((3, -3))
-    up2, down2 = parts((2, -2))
-    up1, down1, here = parts((1, -1, 0))
-    up = ring_step(far[:, :unit], True)
-    down = ring_step(far[:, unit:], False)
+        return add(kept, beside)
+
+    far, near3 = yield (send((4,)), send((3, -3)))
+    far = join(4, far[0])
+    up, down, near2 = yield (
+        ring_step(far[:, :unit], True),
+        ring_step(far[:, unit:], False),
+        send((2, -2)),
+    )
+    up3, down3 = join(3, near3[0]), join(-3, near3[1])
     up = jnp.concatenate([add(up3[:, :unit], up), up3[:, unit:]], axis=1)
     down = jnp.concatenate([down3[:, :unit], add(down3[:, unit:], down)], axis=1)
-    up, down = ring_step(up, True), ring_step(down, False)
-    up, down = ring_step(add(up2, up), True), ring_step(add(down2, down), False)
-    up, down = ring_step(add(up1, up), True), ring_step(add(down1, down), False)
-    total = (here.astype(F32) + up.astype(F32) + down.astype(F32)).astype(BF16)
-    other = swap_pairs(total, "seq")
+    up, down, near1 = yield (ring_step(up, True), ring_step(down, False), send((1, -1)))
+    up, down, here = yield (
+        ring_step(add(join(2, near2[0]), up), True),
+        ring_step(add(join(-2, near2[1]), down), False),
+        send((0,)),
+    )
+    up, down = yield (
+        ring_step(add(join(1, near1[0]), up), True),
+        ring_step(add(join(-1, near1[1]), down), False),
+    )
+    total = add(join(0, here[0]).astype(F32) + up.astype(F32), down)
+    (other,) = yield (swap_pairs(total, "seq"),)
     left, right = jnp.where(seq == 0, total, other), jnp.where(seq == 0, other, total)
     mine = jnp.concatenate(
         [left[:, :unit], add(left[:, unit:], right[:, :unit]), right[:, unit:]], axis=1
     )
-    other = swap_pairs(mine, "rep")
+    (other,) = yield (swap_pairs(mine, "rep"),)
     return jnp.where(
         rep == 0,
         jnp.concatenate([mine, other], axis=1),
@@ -223,13 +259,40 @@
     ).astype(F32)
 
 
+class Background:
+    def __init__(self):
+        self.running = []
+        self.done = {}
+
+    def start(self, key, grads):
+        if not ring_fits(grads.shape[2]):
+            self.done[key] = scatter_plain(grads)
+            return
+        stages = scatter_ring(grads)
+        self.running.append((key, stages, next(stages)))
+
+    def tick(self, value=None):
+        waiting = [moving for _, _, moving in self.running]
+        if value is not None and waiting:
+            value, waiting = lax.optimization_barrier((value, waiting))
+        still = []
+        for (key, stages, _), moving in zip(self.running, waiting):
+            try:
+                still.append((key, stages, stages.send(moving)))
+            except StopIteration as end:
+                self.done[key] = end.value
+        self.running = still
+        return value
+
+    def finish(self):
+        while self.running:
+            self.tick()
+        return self.done
+
+
 def scatter_plain(grads):
     owned = lax.psum_scatter(grads.astype(F32), "shard", scatter_dimension=0, tiled=False)
     return lax.psum(owned.astype(BF16), ("rep", "seq")).astype(F32)
-
-
-def scatter(grads):
-    return (scatter_ring if ring_fits(grads.shape[2]) else scatter_plain)(grads)
 
 
 def normalize(values):
@@ -260,35 +323,123 @@
     )
 
 
-def split_heads(values):
-    return values.reshape(values.shape[0], HEADS, values.shape[1] // HEADS)
-
-
-def attend(queries, keys, values):
-    q, k, v = split_heads(queries), split_heads(keys), split_heads(values)
-    scale_factor = q.shape[-1] ** (-0.5)
-    scores = jnp.einsum("qhd,khd->hqk", q, k, preferred_element_type=F32) * scale_factor
-    top_score = jnp.max(scores, axis=-1, keepdims=True)
-    expo = jnp.exp(scores - top_score)
-    totals = jnp.sum(expo, axis=-1, keepdims=True)
-    probs_low = (expo / totals).astype(BF16)
-    mixed = jnp.einsum("hqk,khd->qhd", probs_low, v, preferred_element_type=F32)
-    return mixed.reshape(queries.shape).astype(BF16), top_score + jnp.log(totals)
-
-
-def attend_back(queries, keys, values, log_total, grad_mixed):
-    q, k, v, g = split_heads(queries), split_heads(keys), split_heads(values), split_heads(grad_mixed)
-    scale_factor = q.shape[-1] ** (-0.5)
-    scores = jnp.einsum("qhd,khd->hqk", q, k, preferred_element_type=F32) * scale_factor
-    probs = jnp.exp(scores - log_total)
-    probs_low = probs.astype(BF16)
-    grad_probs = jnp.einsum("qhd,khd->hqk", g, v, preferred_element_type=F32)
-    grad_scores = probs * (grad_probs - jnp.sum(probs * grad_probs, axis=-1, keepdims=True))
-    grad_low = grad_scores.astype(BF16)
-    grad_q = jnp.einsum("hqk,khd->qhd", grad_low, k, preferred_element_type=F32) * scale_factor
-    grad_k = jnp.einsum("hqk,qhd->khd", grad_low, q, preferred_element_type=F32) * scale_factor
-    grad_v = jnp.einsum("hqk,qhd->khd", probs_low, g, preferred_element_type=F32)
-    return grad_q.reshape(queries.shape), grad_k.reshape(keys.shape), grad_v.reshape(keys.shape)
+def nt(left, right, **kw):
+    return lax.dot_general(left, right, (((1,), (1,)), ((), ())), preferred_element_type=F32, **kw)
+
+
+def tn(left, right):
+    return lax.dot_general(left, right, (((0,), (0,)), ((), ())), preferred_element_type=F32)
+
+
+def nn(left, right):
+    return lax.dot_general(left, right, (((1,), (0,)), ((), ())), preferred_element_type=F32)
+
+
+def head_mask(values, head, size):
+    lanes = lax.broadcasted_iota(jnp.int32, values.shape, 1)
+    inside = (lanes >= head * size) & (lanes < (head + 1) * size)
+    return jnp.where(inside, values, jnp.zeros_like(values))
+
+
+def attend_kernel(size, q_ref, own_ref, other_ref, mixed_ref, log_ref):
+    pair = q_ref.shape[1] // size
+    queries = q_ref[...] * jnp.asarray(size**-0.5, BF16)
+    blocks = []
+    for head in range(pair):
+        query = head_mask(queries, head, size)
+        scores = [nt(own_ref[0], query), nt(other_ref[0], query)]
+        top = jnp.maximum(*[jnp.max(part, axis=0, keepdims=True) for part in scores])
+        expo = [jnp.exp(part - top) for part in scores]
+        totals = sum(jnp.sum(part, axis=0, keepdims=True) for part in expo)
+        mixed = tn(own_ref[1], expo[0].astype(BF16)) + tn(other_ref[1], expo[1].astype(BF16))
+        blocks.append(mixed[head * size : (head + 1) * size] / totals)
+        log_ref[0, head : head + 1, :] = top + jnp.log(totals)
+    mixed_ref[...] = jnp.transpose(jnp.concatenate(blocks, axis=0)).astype(BF16)
+
+
+def attend(queries, own_kv, other_kv):
+    tokens, width = queries.shape
+    pair = 128 // (width // HEADS)
+    groups = HEADS // pair
+    kv_spec = pl.BlockSpec((2, tokens, 128), lambda group: (0, 0, group))
+    token_spec = pl.BlockSpec((tokens, 128), lambda group: (0, group))
+    flops = 8 * tokens * tokens * width
+    return pl.pallas_call(
+        functools.partial(attend_kernel, width // HEADS),
+        grid=(groups,),
+        in_specs=[token_spec, kv_spec, kv_spec],
+        out_specs=(token_spec, pl.BlockSpec((1, pair, tokens), lambda group: (group, 0, 0))),
+        out_shape=(
+            jax.ShapeDtypeStruct((tokens, width), BF16),
+            jax.ShapeDtypeStruct((groups, pair, tokens), F32),
+        ),
+        compiler_params=pltpu.CompilerParams(vmem_limit_bytes=40 * 2**20),
+        cost_estimate=pl.CostEstimate(
+            flops=4 * flops, transcendentals=2 * HEADS * tokens**2, bytes_accessed=12 * queries.size
+        ),
+    )(queries, own_kv, other_kv)
+
+
+def attend_back_kernel(
+    size, q_ref, own_ref, other_ref, grad_ref, mixed_ref, log_ref, dq_ref, down_ref, dother_ref
+):
+    pair = q_ref.shape[1] // size
+    scale = jnp.asarray(size**-0.5, BF16)
+    queries = q_ref[...] * scale
+    product = grad_ref[...].astype(F32) * mixed_ref[...].astype(F32)
+    ones = jnp.ones((8, product.shape[1]), F32)
+    grad_queries = []
+    grad_kv = {}
+    for head in range(pair):
+        query, grad = head_mask(queries, head, size), head_mask(grad_ref[...], head, size)
+        delta = nt(ones, head_mask(product, head, size), precision=lax.Precision.HIGHEST)[0:1]
+        log_total = log_ref[0, head : head + 1, :]
+        grad_query = None
+        for side, kv_ref in enumerate((own_ref, other_ref)):
+            probs = jnp.exp(nt(kv_ref[0], query) - log_total)
+            grad_scores = (probs * (nt(kv_ref[1], grad) - delta)).astype(BF16)
+            parts = (nn(grad_scores, query), nn(probs.astype(BF16), grad))
+            before = grad_kv.get(side)
+            grad_kv[side] = parts if before is None else tuple(a + b for a, b in zip(before, parts))
+            part = tn(kv_ref[0], grad_scores)[head * size : (head + 1) * size]
+            grad_query = part if grad_query is None else grad_query + part
+        grad_queries.append(grad_query)
+    total = jnp.transpose(jnp.concatenate(grad_queries, axis=0)) * (size**-0.5)
+    dq_ref[...] = total.astype(BF16)
+    for side, out_ref in enumerate((down_ref, dother_ref)):
+        for at in range(2):
+            out_ref[at] = grad_kv[side][at].astype(out_ref.dtype)
+
+
+def attend_back(queries, own_kv, other_kv, grad_mixed, mixed, log_total):
+    tokens, width = queries.shape
+    pair = 128 // (width // HEADS)
+    groups = HEADS // pair
+    kv_spec = pl.BlockSpec((2, tokens, 128), lambda group: (0, 0, group))
+    token_spec = pl.BlockSpec((tokens, 128), lambda group: (0, group))
+    flops = 20 * tokens * tokens * width
+    return pl.pallas_call(
+        functools.partial(attend_back_kernel, width // HEADS),
+        grid=(groups,),
+        in_specs=[
+            token_spec,
+            kv_spec,
+            kv_spec,
+            token_spec,
+            token_spec,
+            pl.BlockSpec((1, pair, tokens), lambda group: (group, 0, 0)),
+        ],
+        out_specs=(token_spec, kv_spec, kv_spec),
+        out_shape=(
+            jax.ShapeDtypeStruct((tokens, width), BF16),
+            jax.ShapeDtypeStruct(own_kv.shape, F32),
+            jax.ShapeDtypeStruct(own_kv.shape, BF16),
+        ),
+        compiler_params=pltpu.CompilerParams(vmem_limit_bytes=40 * 2**20),
+        cost_estimate=pl.CostEstimate(
+            flops=4 * flops, transcendentals=2 * HEADS * tokens**2, bytes_accessed=24 * queries.size
+        ),
+    )(queries, own_kv, other_kv, grad_mixed, mixed, log_total)
 
 
 def layer_forward(stream, modulation, weights, biases):
@@ -302,8 +453,8 @@
         (dot(normed, qkv_w[part], (1,), (0,)) + qkv_b[part]).astype(BF16) for part in range(3)
     ]
     own_kv = jnp.stack([keys, values])
-    both_kv = jnp.concatenate([own_kv, swap_pairs(own_kv, "rep")], axis=1)
-    mixed, log_total = attend(queries, both_kv[0], both_kv[1])
+    other_kv = swap_pairs(own_kv, "rep")
+    mixed, log_total = attend(queries, own_kv, other_kv)
     attn_out = dot(mixed, proj_w, (1,), (0,)) + proj_b
     middle = stream + gate_attn * attn_out
     normal_mlp, scale_mlp = normalize(middle)
@@ -316,7 +467,7 @@
     mlp_out = dot(activated, fc2_w, (1,), (0,)) + fc2_b
     result = middle + gate_mlp * mlp_out
     return result, (
-        stream, normed, queries, both_kv, mixed, log_total, attn_out, middle, normed_mlp, hidden,
+        stream, normed, queries, own_kv, other_kv, mixed, log_total, attn_out, middle, normed_mlp, hidden,
         activated, mlp_out,
     )
 
@@ -329,31 +480,33 @@
     return matrix.reshape(shards, matrix.shape[0] // shards, matrix.shape[1])
 
 
-def layer_backward(grad_out, modulation, weights, kept, shards):
+def layer_backward(layer, grad_out, modulation, weights, kept, shards, background):
     qkv_w, proj_w, fc1_w, fc2_w = weights
     (
-        stream, normed, queries, both_kv, mixed, log_total, attn_out, middle, normed_mlp, hidden,
+        stream, normed, queries, own_kv, other_kv, mixed, log_total, attn_out, middle, normed_mlp, hidden,
         activated, mlp_out,
     ) = kept
     width = stream.shape[-1]
-    half_tokens = stream.shape[0]
     shift_attn, factor_attn, gate_attn, shift_mlp, factor_mlp, gate_mlp = modulation
     grad_gate_mlp = token_sum(grad_out * mlp_out)
     grad_mlp = (grad_out * gate_mlp).astype(BF16)
     grad_fc2_w = dot(activated, grad_mlp, (0,), (0,)).astype(BF16)
     grad_fc2_b = token_sum(grad_mlp)
+    grad_mlp = background.tick(grad_mlp)
     grad_activated = dot(grad_mlp, fc2_w, (1,), (1,))
     _, gelu_pull = jax.vjp(lambda v: jax.nn.gelu(v, approximate=True), hidden)
     grad_hidden = gelu_pull(grad_activated)[0].astype(BF16)
     parts = [
         grad_hidden[:, part * width : (part + 1) * width] for part in range(fc1_w.shape[0])
     ]
+    parts = background.tick(parts)
     grad_fc1_w = [dot(normed_mlp, part, (0,), (0,)).astype(BF16) for part in parts]
     grad_fc1_b = token_sum(grad_hidden)
     grad_normed = sum(dot(part, fc1_w[at], (1,), (1,)) for at, part in enumerate(parts))
     fc2_grads = grad_fc2_w.reshape(shards, -1, width // shards, width)
     fc1_grads = jnp.stack([by_shard(part, shards) for part in grad_fc1_w], axis=1)
-    mlp_grads = scatter(jnp.concatenate([fc1_grads, fc2_grads], axis=1))
+    grad_normed = background.tick(grad_normed)
+    background.start(("mlp", layer), jnp.concatenate([fc1_grads, fc2_grads], axis=1))
     normal, scale = normalize(middle)
     grad_shift_mlp = token_sum(grad_normed)
     grad_factor_mlp = token_sum(grad_normed * normal)
@@ -362,23 +515,27 @@
     grad_attn = (grad_middle * gate_attn).astype(BF16)
     grad_proj_w = dot(mixed, grad_attn, (0,), (0,)).astype(BF16)
     grad_proj_b = token_sum(grad_attn)
+    grad_attn = background.tick(grad_attn)
     grad_mixed = dot(grad_attn, proj_w, (1,), (1,)).astype(BF16)
-    grad_q, grad_k, grad_v = attend_back(queries, both_kv[0], both_kv[1], log_total, grad_mixed)
-    returned = swap_pairs(
-        jnp.stack([grad_k[half_tokens:], grad_v[half_tokens:]]).astype(BF16), "rep"
-    )
-    grad_k = grad_k[:half_tokens] + returned[0].astype(F32)
-    grad_v = grad_v[:half_tokens] + returned[1].astype(F32)
-    grad_projected = [part.astype(BF16) for part in (grad_q, grad_k, grad_v)]
+    grad_mixed = background.tick(grad_mixed)
+    grad_q, grad_own, grad_other = attend_back(
+        queries, own_kv, other_kv, grad_mixed, mixed, log_total
+    )
+    grad_own = background.tick(grad_own)
+    grad_kv = (grad_own + swap_pairs(grad_other, "rep").astype(F32)).astype(BF16)
+    grad_projected = [grad_q, grad_kv[0], grad_kv[1]]
     grad_qkv_w = [dot(normed, part, (0,), (0,)).astype(BF16) for part in grad_projected]
-    attn_grads = scatter(
-        jnp.stack([by_shard(part, shards) for part in grad_qkv_w + [grad_proj_w]], axis=1)
+    grad_qkv_w = background.tick(grad_qkv_w)
+    background.start(
+        ("attn", layer),
+        jnp.stack([by_shard(part, shards) for part in grad_qkv_w + [grad_proj_w]], axis=1),
     )
     grad_qv_b = jnp.concatenate([token_sum(grad_projected[0]), token_sum(grad_projected[2])])
     grad_normed = sum(dot(part, qkv_w[at], (1,), (1,)) for at, part in enumerate(grad_projected))
     normal, scale = normalize(stream)
     grad_shift_attn = token_sum(grad_normed)
     grad_factor_attn = token_sum(grad_normed * normal)
+    grad_normed = background.tick(grad_normed)
     grad_stream = grad_middle + norm_back(grad_normed, normal, scale, factor_attn)
     grad_modulation = jnp.concatenate(
         [
@@ -393,7 +550,7 @@
     bias_grads = [
         part.reshape(shards, -1) for part in (grad_qv_b, grad_proj_b, grad_fc1_b, grad_fc2_b)
     ]
-    return grad_stream, grad_modulation, jnp.concatenate(bias_grads, axis=1), mlp_grads, attn_grads
+    return grad_stream, grad_modulation, jnp.concatenate(bias_grads, axis=1)
 
 
 def columns(matrix, width):
@@ -434,11 +591,8 @@
     cond = dot(one_hot, label_table, (1,), (0,)) + time_embed(timesteps, width)
     cond_low = jax.nn.silu(cond).astype(BF16)
     live_own = (image_loads > 0).astype(BF16)
-    shared = lax.all_gather(
-        jnp.concatenate([cond_low, jnp.broadcast_to(live_own[:, None], (1, 128))], axis=1),
-        ("rep", "shard"),
-        axis=0,
-        tiled=True,
+    shared = cube_gather(
+        jnp.concatenate([cond_low[0], jnp.broadcast_to(live_own, (128,))]), ("rep", "shard")
     )
     live = lax.dynamic_slice(shared, (seq * shards + shard, width), (1, 1)).astype(F32)
     cond_rows = lax.dynamic_slice(
@@ -460,7 +614,7 @@
         gathered.append((qkv_w, rest_w[0], rest_w[1:], fc2_w.reshape(ff_parts * width, width)))
 
     small = jnp.concatenate([ada_bias, qv_bias, proj_bias, fc1_bias, fc2_bias], axis=1)
-    small = lax.all_gather(small, "shard", axis=0, tiled=False).astype(F32)
+    small = cube_gather(small, ("shard",)).astype(F32)
     ends = [0]
     for bias in (ada_bias, qv_bias, proj_bias, fc1_bias, fc2_bias):
         ends.append(ends[-1] + bias.shape[1])
@@ -475,7 +629,7 @@
     partial = jnp.concatenate(
         [dot(mine, ada_weight[layer], (1,), (0,)) for layer in range(LAYERS)], axis=1
     )
-    modulations = lax.psum_scatter(partial, "shard", scatter_dimension=0, tiled=True)[0]
+    modulations = cube_scatter(partial, "shard")
     modulations = [
         jnp.split((modulations.reshape(LAYERS, -1)[layer] + ada_b[layer])[None, :], 6, axis=1)
         for layer in range(LAYERS)
@@ -489,22 +643,17 @@
     grad_stream = swap_layout(cotangent[0]).astype(F32) * live
 
     weight_grads = [None] * LAYERS
+    background = Background()
     bias_grads = [None] * LAYERS
     ada_w_grads = [None] * LAYERS
     ada_b_grads = [None] * LAYERS
     grad_cond = 0.0
     for layer in reversed(range(LAYERS)):
-        grad_stream, grad_mod, bias_grads[layer], mlp_grads, attn_grads = layer_backward(
-            grad_stream, modulations[layer], gathered[layer], kept[layer], shards
-        )
-        weight_grads[layer] = (
-            uncolumns(attn_grads[:3]),
-            attn_grads[3],
-            uncolumns(mlp_grads[:ff_parts]),
-            mlp_grads[ff_parts:].reshape(ff_parts * own_rows, width),
+        grad_stream, grad_mod, bias_grads[layer] = layer_backward(
+            layer, grad_stream, modulations[layer], gathered[layer], kept[layer], shards, background
         )
         grad_mod = (grad_mod + swap_pairs(grad_mod, "rep")).astype(BF16)
-        all_mod = lax.all_gather(grad_mod, ("seq", "shard"), axis=0, tiled=False)
+        all_mod = cube_gather(grad_mod, ("seq", "shard"))
         ada_w_grads[layer] = dot(cond_rows, all_mod, (0,), (0,))
         own_mod = lax.dynamic_slice(
             all_mod, (0, shard * ada_bias.shape[1]), (all_mod.shape[0], ada_bias.shape[1])
@@ -514,21 +663,28 @@
         grad_cond = grad_cond + dot(rep_mod, ada_weight[layer], (1,), (1,))
 
     latent_grad = swap_layout(grad_stream.astype(BF16)).astype(F32)
-    all_cond = lax.all_gather(grad_cond, "shard", axis=0, tiled=False)
+    all_cond = cube_gather(grad_cond, ("shard",))
     grad_cond_low = lax.dynamic_slice(all_cond, (0, shard, 0), (shards, 1, own_rows)).reshape(
         1, width
     )
     _, silu_pull = jax.vjp(jax.nn.silu, cond)
     cond_grad = silu_pull(grad_cond_low)[0]
 
-    bias_total = lax.psum_scatter(
-        jnp.concatenate(bias_grads, axis=1), "shard", scatter_dimension=0, tiled=True
-    ).reshape(LAYERS, -1)
+    bias_total = cube_scatter(jnp.stack(bias_grads, axis=1), "shard")
     bias_total = bias_total + swap_pairs(bias_total, "rep")
     bias_total = bias_total + swap_pairs(bias_total, "seq")
     qv_b, proj_b, fc1_b, fc2_b = [
         bias_total[:, ends[at] - ends[1] : ends[at + 1] - ends[1]] for at in range(1, 5)
     ]
+    done = background.finish()
+    for layer in range(LAYERS):
+        attn_grads, mlp_grads = done["attn", layer], done["mlp", layer]
+        weight_grads[layer] = (
+            uncolumns(attn_grads[:3]),
+            attn_grads[3],
+            uncolumns(mlp_grads[:ff_parts]),
+            mlp_grads[ff_parts:].reshape(ff_parts * own_rows, width),
+        )
     qkv_g, proj_g, fc1_g, fc2_g = [
         jnp.stack([weight_grads[layer][at] for layer in range(LAYERS)]) for at in range(4)
     ]

time: 2000 us -> 855 us (0.43)
  Pallas kernels: 865 us -> 84.3 us
  blocking collectives: 211 us -> 0 us
  matrix products: 266 us -> 109 us
  other arithmetic: 149 us -> 110 us
  starting transfers between devices: 124 us -> 154 us
    pallas_call x4, Pallas kernels: 865 us -> 12.2 us  [gather_ring(): pl.pallas_call(functools.partial(place_kernel, plain, split), out_shape=t...]
    all_gather x5 -> x0, blocking collectives: 177 us -> none  [the longest x2 78.8 us: shards_program(): all_mod = lax.all_gather(grad_mod, ('seq', 'shard'), axis=0, tiled=False)]
    dot_general x12 -> x0, matrix products: 145 us -> none  [the longest x2 37.6 us: attend_back(): grad_probs = jnp.einsum('qhd,khd->hqk', g, v, preferred_element_type=F32)]
    pallas_call x0 -> x4, Pallas kernels: none -> 72.1 us  [the longest x2 45.4 us: attend_back(): pl.pallas_call(functools.partial(attend_back_kernel, width // HEADS), gri...]
    ppermute x0 -> x24, waiting for transfers between devices: none -> 56.1 us  [cube_pairs(): lax.ppermute(value, axis, [(at, at ^ bit) for at in range(lax.axis_size(a...]
    convert_element_type x11 -> x3, other arithmetic: 53.4 us -> 2.3 us  [the longest x2 2.24 us: layer_backward(): (grad_own + swap_pairs(grad_other, 'rep').astype(F32)).astype(BF16)]
    unnamed x1 -> x0, blocking collectives: 33.8 us -> none
    ppermute x0 -> x24, starting transfers between devices: none -> 27.7 us  [cube_pairs(): lax.ppermute(value, axis, [(at, at ^ bit) for at in range(lax.axis_size(a...]
  transfers between devices with their start and end apart: 149 -> 176, of which waited for: 52 -> 74; matrix products, arithmetic and copies ran while one was open for 19% -> 31% of each run, Pallas kernels for 43% -> 10%
where the time goes in v2:
time: 855 us; the launch traced here: 842 us
  waiting for transfers between devices  237 us (28%)
  starting transfers between devices  154 us (18%)
  local copies, waits for them, and re-layouts  125 us (15%)
  other arithmetic  110 us (13%)
  matrix products  109 us (13%)
  Pallas kernels  84.3 us (10%)
  between operations  23.1 us (3%)
    ppermute x64, waiting for transfers between devices, ring_step(): lax.ppermute(value, 'shard', [(order[at], order[(at + step) % size]) for...  121 us
    dot_general x61, matrix products, dot(): lax.dot_general(left, right, ((left_dims, right_dims), ((), ())), preferr...  109 us
    ppermute x64, starting transfers between devices, ring_step(): lax.ppermute(value, 'shard', [(order[at], order[(at + step) % size]) for...  70.1 us
    ppermute x84, waiting for transfers between devices, swap_pairs(): return lax.ppermute(value, axis, [(0, 1), (1, 0)])  59.8 us
    unnamed x550, local copies, waits for them, and re-layouts  58.8 us
    ppermute x24, waiting for transfers between devices, cube_pairs(): lax.ppermute(value, axis, [(at, at ^ bit) for at in range(lax.axis_size(a...  56.1 us
    pallas_call x2, Pallas kernels, attend_back(): pl.pallas_call(functools.partial(attend_back_kernel, width // HEADS), gri...  45.4 us
    convert_element_type x34, other arithmetic, add(): return (left.astype(F32) + right.astype(F32)).astype(BF16)  40.2 us
  transfers between devices with their start and end apart: 176, of which 74 were waited for; matrix products, arithmetic and copies ran while one was open for 31% of the time, Pallas kernels for 10%

profile of v2, /device:TPU:0, one launch (start us, length us, event | category | flops | bytes accessed | tf_op | source)
XLA Modules:
  0.0 842.5 jit_solution(6990379262689030529)
XLA Ops:
  58.0 6.4 collective-permute-done.5
  68.1 7.7 collective-permute-done.6
  78.8 3.8 collective-permute-done.7
  83.6 4.3 collective-permute-done.14.refs_4_
  90.7 4.0 collective-permute-done.53.refs_4_
  95.1 4.7 collective-permute-done.52.refs_3_
  100.3 5.1 collective-permute-done.15.refs_5_
  106.4 4.1 collective-permute-done.16.refs_6_
  118.4 3.9 collective-permute-done.55.refs_6_
  146.0 8.3 collective-permute-done.34.refs_4_
  157.7 5.8 collective-permute-done.73.refs_4_
  173.6 4.2 collective-permute-done.59.refs_9_
  185.2 5.6 collective-permute-done.35.refs_5_
  192.6 7.3 collective-permute-done.74.refs_5_
  216.7 12.9 %collective-permute-done.39.refs_8_ = bf16[4,9,16,768]{3,2,1,0:T(8,128)(2,1)S(1)} collective-permute-done((bf16[4,9,16,768]{3,2,1,0:T(8,128)(2,1)S(1)}, bf16[4,9,16,768]{3,2,1,0:T(8,128)(2,1)S(1)}, u32[]{:S(2)}, u32[]{:S(2)}) %collective-permute-start.39) | collective-permute-done | bytes 884768 | tf_op jit(solution)/shard_map/ppermute | solution.py:19
  231.3 10.5 %collective-permute-done.40.refs_9_ = bf16[3,9,16,768]{3,2,1,0:T(8,128)(2,1)S(1)} collective-permute-done((bf16[3,9,16,768]{3,2,1,0:T(8,128)(2,1)S(1)}, bf16[3,9,16,768]{3,2,1,0:T(8,128)(2,1)S(1)}, u32[]{:S(2)}, u32[]{:S(2)}) %collective-permute-start.40) | collective-permute-done | bytes 663584 | tf_op jit(solution)/shard_map/ppermute | solution.py:19
  244.5 12.4 %shard_map.400 = (bf16[512,768]{1,0:T(8,128)(2,1)S(1)}, f32[6,2,512]{2,1,0:T(2,128)S(1)}) custom-call(bf16[512,768]{1,0:T(8,128)(2,1)S(1)} %add_convert_fusion.12.q_ref, bf16[2,512,768]{2,1,0:T(8,128)(2,1)S(1)} %pad_maximum_fusion.6.own_ref, bf16[2,512,768]{2,1,0:T(8,128)(2,1)S(1)} %collective-permute-done.30.other_ref), custom_call_target="tpu_custom_call" | custom-call | flops 6442450944 | bytes 4718592 | tf_op jit(solution)/shard_map/pallas_call | solution.py:367
  274.6 3.7 shard_map.401
  278.4 4.3 fusion.191
  287.0 13.0 %multiply_convert_fusion.1 = bf16[512,3072]{1,0:T(8,128)(2,1)S(1)} fusion(f32[512,768]{1,0:T(8,128)S(1)} %fusion.54, f32[512,768]{1,0:T(8,128)S(1)} %fusion.60, f32[512,768]{1,0:T(8,128)S(1)} %fusion.64, f32[512,768]{1,0:T(8,128)S(1)} %fusion.68, f32[3072]{0:T(1024)S(1)} %bitcast.604), kind=kLoop, calls=%fused_computation.26 | loop fusion | flops 20447232 | bytes 9449472 | tf_op jit(solution)/shard_map/convert_element_type | solution.py:466
  300.1 3.9 fusion.190
  333.0 4.2 shard_map.404
  338.0 14.2 %shard_map.403 = (bf16[512,768]{1,0:T(8,128)(2,1)S(1)}, f32[6,2,512]{2,1,0:T(2,128)S(1)}) custom-call(bf16[512,768]{1,0:T(8,128)(2,1)S(1)} %add_convert_fusion.8.q_ref, bf16[2,512,768]{2,1,0:T(8,128)(2,1)} %pad_maximum_fusion.7.own_ref, bf16[2,512,768]{2,1,0:T(8,128)(2,1)} %collective-permute-done.69.other_ref), custom_call_target="tpu_custom_call" | custom-call | flops 6442450944 | bytes 4718592 | tf_op jit(solution)/shard_map/pallas_call | solution.py:367
  362.2 9.2 %convert_reduce_fusion = (f32[3072]{0:T(1024)}, bf16[512,3072]{1,0:T(8,128)(2,1)S(1)}) fusion(f32[3072]{0:T(1024)S(1)} %bitcast.607, f32[512,768]{1,0:T(8,128)} %copy-done.120, f32[512,768]{1,0:T(8,128)S(1)} %fusion.40, f32[512,768]{1,0:T(8,128)} %copy-done.121, f32[512,768]{1,0:T(8,128)} %copy-done.122, bf16[3072,768]{1,0:T(8,128)(2,1)S(1)} %bitcast.570, ...), kind=kOutput, calls=%fused_computation.23 | convolution fusion | flops 2458383360 | bytes 14969860 | tf_op jit(solution)/shard_map/dot_general | solution.py:321
  408.9 3.5 multiply_reduce_fusion.4
  412.5 5.3 convert_reduce_fusion.3
  417.8 7.6 collective-permute-start.89
  431.0 5.1 add_convert_fusion.1
  445.3 8.4 %collective-permute-done.93 = bf16[2,8,16,768]{3,2,1,0:T(8,128)(2,1)S(1)} collective-permute-done((bf16[2,8,16,768]{3,2,1,0:T(8,128)(2,1)S(1)}, bf16[2,8,16,768]{3,2,1,0:T(8,128)(2,1)S(1)}, u32[]{:S(2)}, u32[]{:S(2)}) %collective-permute-start.93) | collective-permute-done | bytes 393248 | tf_op jit(solution)/shard_map/ppermute | solution.py:19
  453.8 22.7 %shard_map.405 = (bf16[512,768]{1,0:T(8,128)(2,1)S(1)}, f32[2,512,768]{2,1,0:T(8,128)S(1)}, bf16[2,512,768]{2,1,0:T(8,128)(2,1)S(1)}) custom-call(bf16[512,768]{1,0:T(8,128)(2,1)S(1)} %copy-done.68, bf16[2,512,768]{2,1,0:T(8,128)(2,1)} %pad_maximum_fusion.7.own_ref, bf16[2,512,768]{2,1,0:T(8,128)(2,1)} %collective-permute-done.69.other_ref, ...), custom_call_target="tpu_custom_call" | custom-call | flops 16106127360 | bytes 9437184 | tf_op jit(solution)/shard_map/pallas_call | solution.py:421
  481.0 3.7 collective-permute-done.94
  491.5 5.3 collective-permute-done.98
  517.3 4.2 collective-permute-done.101
  540.9 4.3 convolution_convert_fusion
  551.9 3.8 collective-permute-done.143
  562.2 11.2 %convert_reduce_fusion.1 = (f32[3072]{0:T(1024)}, bf16[512,3072]{1,0:T(8,128)(2,1)S(1)}) fusion(f32[3072]{0:T(1024)S(1)} %bitcast.605, f32[512,768]{1,0:T(8,128)} %copy-done.115, f32[512,768]{1,0:T(8,128)} %copy-done.116, f32[512,768]{1,0:T(8,128)} %copy-done.117, f32[512,768]{1,0:T(8,128)} %copy-done.118, bf16[512,768]{1,0:T(8,128)(2,1)S(1)} %get-tuple-element.121, ...), kind=kOutput, calls=%fused_computation.24 | convolution fusion | flops 2456810496 | bytes 14966784 | tf_op jit(solution)/shard_map/dot_general | solution.py:321
  595.0 4.0 copy-done.93
  626.2 5.1 add_convert_fusion
  641.1 8.4 %collective-permute-done.124 = bf16[2,8,16,768]{3,2,1,0:T(8,128)(2,1)S(1)} collective-permute-done((bf16[2,8,16,768]{3,2,1,0:T(8,128)(2,1)S(1)}, bf16[2,8,16,768]{3,2,1,0:T(8,128)(2,1)S(1)}, u32[]{:S(2)}, u32[]{:S(2)}) %collective-permute-start.124) | collective-permute-done | bytes 393248 | tf_op jit(solution)/shard_map/ppermute | solution.py:19
  649.6 22.7 %shard_map.406 = (bf16[512,768]{1,0:T(8,128)(2,1)S(1)}, f32[2,512,768]{2,1,0:T(8,128)S(1)}, bf16[2,512,768]{2,1,0:T(8,128)(2,1)}) custom-call(bf16[512,768]{1,0:T(8,128)(2,1)S(1)} %copy-done.70, bf16[2,512,768]{2,1,0:T(8,128)(2,1)S(1)} %copy-done.15, bf16[2,512,768]{2,1,0:T(8,128)(2,1)S(1)} %copy-done.66, ...), custom_call_target="tpu_custom_call" | custom-call | flops 16106127360 | bytes 9437184 | tf_op jit(solution)/shard_map/pallas_call | solution.py:421
  703.5 3.2 collective-permute-done.132
  723.6 3.2 collective-permute-done.168
  739.9 7.4 collective-permute-start.138
  764.6 3.6 collective-permute-done.148
  778.0 3.2 collective-permute-done.151
  790.8 3.7 collective-permute-done.157
  797.1 9.3 %collective-permute-done.158 = bf16[4,32,768]{2,1,0:T(8,128)(2,1)S(1)} collective-permute-done((bf16[4,32,768]{2,1,0:T(8,128)(2,1)S(1)}, bf16[4,32,768]{2,1,0:T(8,128)(2,1)S(1)}, u32[]{:S(2)}, u32[]{:S(2)}) %collective-permute-start.158) | collective-permute-done | bytes 196640 | tf_op jit(solution)/shard_map/ppermute | solution.py:64
  820.1 6.0 collective-permute-done.163
  (1245 shorter events, 490.7 us)
Async XLA Ops:
  3.5 54.2 %collective-permute-start.11 = (bf16[3,32,768]{2,1,0:T(8,128)(2,1)}, bf16[3,32,768]{2,1,0:T(8,128)(2,1)S(1)}, u32[]{:S(2)}, u32[]{:S(2)}) collective-permute-start(bf16[3,32,768]{2,1,0:T(8,128)(2,1)} %constant_dynamic-slice_fusion.42), channel_id=1, source_target_pairs={{0,4},{4,8},{8,12},{12,14},{14,10},{10,6},{6,2},{2,0},{1,5},{5,9},... | collective-permute-start | bytes 442376 | tf_op jit(solution)/shard_map/ppermute | solution.py:64
  6.5 48.6 %collective-permute-start.12 = (bf16[3,32,768]{2,1,0:T(8,128)(2,1)}, bf16[3,32,768]{2,1,0:T(8,128)(2,1)}, u32[]{:S(2)}, u32[]{:S(2)}) collective-permute-start(bf16[3,32,768]{2,1,0:T(8,128)(2,1)} %constant_dynamic-slice_fusion.42), channel_id=1, source_target_pairs={{0,2},{4,0},{8,4},{12,8},{14,12},{10,14},{6,10},{2,6},{1,3},{5,1},... | collective-permute-start | bytes 442376 | tf_op jit(solution)/shard_map/ppermute | solution.py:64
  12.6 103.5 %collective-permute-start.31 = (bf16[9,32,768]{2,1,0:T(8,128)(2,1)}, bf16[9,32,768]{2,1,0:T(8,128)(2,1)}, u32[]{:S(2)}, u32[]{:S(2)}) collective-permute-start(bf16[9,32,768]{2,1,0:T(8,128)(2,1)} %constant_dynamic-slice_fusion.41), channel_id=1, source_target_pairs={{0,4},{4,8},{8,12},{12,14},{14,10},{10,6},{6,2},{2,0},{1,5},{5,9},... | collective-permute-start | bytes 1327112 | tf_op jit(solution)/shard_map/ppermute | solution.py:64
  14.7 96.9 %collective-permute-start.32 = (bf16[9,32,768]{2,1,0:T(8,128)(2,1)}, bf16[9,32,768]{2,1,0:T(8,128)(2,1)}, u32[]{:S(2)}, u32[]{:S(2)}) collective-permute-start(bf16[9,32,768]{2,1,0:T(8,128)(2,1)} %constant_dynamic-slice_fusion.41), channel_id=1, source_target_pairs={{0,2},{4,0},{8,4},{12,8},{14,12},{10,14},{6,10},{2,6},{1,3},{5,1},... | collective-permute-start | bytes 1327112 | tf_op jit(solution)/shard_map/ppermute | solution.py:64
  48.3 30.2 %collective-permute-start.50 = (bf16[3,32,768]{2,1,0:T(8,128)(2,1)S(1)}, bf16[3,32,768]{2,1,0:T(8,128)(2,1)S(1)}, u32[]{:S(2)}, u32[]{:S(2)}) collective-permute-start(bf16[3,32,768]{2,1,0:T(8,128)(2,1)S(1)} %constant_dynamic-slice_fusion.40), channel_id=1, source_target_pairs={{0,4},{4,8},{8,12},{12,14},{14,10},{10,6},{6,2},{2,0},{1,5},{5,9},... | collective-permute-start | bytes 442376 | tf_op jit(solution)/shard_map/ppermute | solution.py:64
  64.5 59.0 %collective-permute-start.70 = (bf16[9,32,768]{2,1,0:T(8,128)(2,1)S(1)}, bf16[9,32,768]{2,1,0:T(8,128)(2,1)S(1)}, u32[]{:S(2)}, u32[]{:S(2)}) collective-permute-start(bf16[9,32,768]{2,1,0:T(8,128)(2,1)S(1)} %constant_dynamic-slice_fusion.39), channel_id=1, source_target_pairs={{0,4},{4,8},{8,12},{12,14},{14,10},{10,6},{6,2},{2,0},{1,5},{5,9},... | collective-permute-start | bytes 1327112 | tf_op jit(solution)/shard_map/ppermute | solution.py:64
  88.3 29.9 %collective-permute-start.71 = (bf16[9,32,768]{2,1,0:T(8,128)(2,1)S(1)}, bf16[9,32,768]{2,1,0:T(8,128)(2,1)S(1)}, u32[]{:S(2)}, u32[]{:S(2)}) collective-permute-start(bf16[9,32,768]{2,1,0:T(8,128)(2,1)S(1)} %constant_dynamic-slice_fusion.39), channel_id=1, source_target_pairs={{0,2},{4,0},{8,4},{12,8},{14,12},{10,14},{6,10},{2,6},{1,3},{5,1},... | collective-permute-start | bytes 1327112 | tf_op jit(solution)/shard_map/ppermute | solution.py:64
  111.5 29.6 %collective-permute-start = (bf16[512,768]{1,0:T(8,128)(2,1)S(1)}, bf16[512,768]{1,0:T(8,128)(2,1)S(1)}, u32[]{:S(2)}, u32[]{:S(2)}) collective-permute-start(bf16[512,768]{1,0:T(8,128)(2,1)S(1)} %bitcast.610), channel_id=1, source_target_pairs={{0,0},{1,16},{16,1},{17,17},{2,2},{3,18},{18,3},{19,19},{4,4},{5,2... | collective-permute-start | bytes 2359304 | tf_op jit(solution)/shard_map/ppermute | solution.py:23
  115.7 27.0 %collective-permute-start.21 = (bf16[3,32,768]{2,1,0:T(8,128)(2,1)S(1)}, bf16[3,32,768]{2,1,0:T(8,128)(2,1)S(1)}, u32[]{:S(2)}, u32[]{:S(2)}) collective-permute-start(bf16[3,32,768]{2,1,0:T(8,128)(2,1)S(1)} %collective-permute-done.11.refs_1_), channel_id=1, source_target_pairs={{0,16},{16,0},{1,17},{17,1},{2,18},{18,2},{3,19},{19,3},{4,20},{20... | collective-permute-start | bytes 442376 | tf_op jit(solution)/shard_map/ppermute | solution.py:19
  118.2 25.6 %collective-permute-start.22 = (bf16[3,32,768]{2,1,0:T(8,128)(2,1)}, bf16[3,32,768]{2,1,0:T(8,128)(2,1)S(1)}, u32[]{:S(2)}, u32[]{:S(2)}) collective-permute-start(bf16[3,32,768]{2,1,0:T(8,128)(2,1)} %collective-permute-done.12.refs_2_), channel_id=1, source_target_pairs={{0,16},{16,0},{1,17},{17,1},{2,18},{18,2},{3,19},{19,3},{4,20},{20... | collective-permute-start | bytes 442376 | tf_op jit(solution)/shard_map/ppermute | solution.py:19
  122.2 23.3 %collective-permute-start.19 = (bf16[4,3,16,768]{3,2,1,0:T(8,128)(2,1)S(1)}, bf16[4,3,16,768]{3,2,1,0:T(8,128)(2,1)S(1)}, u32[]{:S(2)}, u32[]{:S(2)}) collective-permute-start(bf16[4,3,16,768]{3,2,1,0:T(8,128)(2,1)S(1)} %pad_maximum_fusion.27), channel_id=1, source_target_pairs={{0,1},{1,0},{2,3},{3,2},{4,5},{5,4},{6,7},{7,6},{8,9},{9,8},{10,11... | collective-permute-start | bytes 884744 | tf_op jit(solution)/shard_map/ppermute | solution.py:19
  180.8 29.2 %collective-permute-start.41 = (bf16[9,32,768]{2,1,0:T(8,128)(2,1)}, bf16[9,32,768]{2,1,0:T(8,128)(2,1)S(1)}, u32[]{:S(2)}, u32[]{:S(2)}) collective-permute-start(bf16[9,32,768]{2,1,0:T(8,128)(2,1)} %collective-permute-done.31.refs_1_), channel_id=1, source_target_pairs={{0,16},{16,0},{1,17},{17,1},{2,18},{18,2},{3,19},{19,3},{4,20},{20... | collective-permute-start | bytes 1327112 | tf_op jit(solution)/shard_map/ppermute | solution.py:19
  180.9 29.6 %collective-permute-start.42 = (bf16[9,32,768]{2,1,0:T(8,128)(2,1)}, bf16[9,32,768]{2,1,0:T(8,128)(2,1)S(1)}, u32[]{:S(2)}, u32[]{:S(2)}) collective-permute-start(bf16[9,32,768]{2,1,0:T(8,128)(2,1)} %collective-permute-done.32.refs_2_), channel_id=1, source_target_pairs={{0,16},{16,0},{1,17},{17,1},{2,18},{18,2},{3,19},{19,3},{4,20},{20... | collective-permute-start | bytes 1327112 | tf_op jit(solution)/shard_map/ppermute | solution.py:19
  192.4 51.7 %collective-permute-start.30 = (bf16[2,512,768]{2,1,0:T(8,128)(2,1)S(1)}, bf16[2,512,768]{2,1,0:T(8,128)(2,1)S(1)}, u32[]{:S(2)}, u32[]{:S(2)}) collective-permute-start(bf16[2,512,768]{2,1,0:T(8,128)(2,1)S(1)} %pad_maximum_fusion.6.own_ref), channel_id=1, source_target_pairs={{0,16},{16,0},{1,17},{17,1},{2,18},{18,2},{3,19},{19,3},{4,20},{20... | collective-permute-start | bytes 4718600 | tf_op jit(solution)/shard_map/ppermute | solution.py:19
  207.1 22.6 %collective-permute-start.39 = (bf16[4,9,16,768]{3,2,1,0:T(8,128)(2,1)S(1)}, bf16[4,9,16,768]{3,2,1,0:T(8,128)(2,1)S(1)}, u32[]{:S(2)}, u32[]{:S(2)}) collective-permute-start(bf16[4,9,16,768]{3,2,1,0:T(8,128)(2,1)S(1)} %pad_maximum_fusion.8), channel_id=1, source_target_pairs={{0,1},{1,0},{2,3},{3,2},{4,5},{5,4},{6,7},{7,6},{8,9},{9,8},{10,11... | collective-permute-start | bytes 2654216 | tf_op jit(solution)/shard_map/ppermute | solution.py:19
  210.5 31.3 %collective-permute-start.40 = (bf16[3,9,16,768]{3,2,1,0:T(8,128)(2,1)S(1)}, bf16[3,9,16,768]{3,2,1,0:T(8,128)(2,1)S(1)}, u32[]{:S(2)}, u32[]{:S(2)}) collective-permute-start(bf16[3,9,16,768]{3,2,1,0:T(8,128)(2,1)S(1)} %pad_maximum_fusion.10), channel_id=1, source_target_pairs={{0,1},{1,0},{2,3},{3,2},{4,5},{5,4},{6,7},{7,6},{8,9},{9,8},{10,11... | collective-permute-start | bytes 1990664 | tf_op jit(solution)/shard_map/ppermute | solution.py:19
  214.2 27.7 %collective-permute-start.43 = (bf16[9,32,768]{2,1,0:T(8,128)(2,1)S(1)}, bf16[9,32,768]{2,1,0:T(8,128)(2,1)S(1)}, u32[]{:S(2)}, u32[]{:S(2)}) collective-permute-start(bf16[9,32,768]{2,1,0:T(8,128)(2,1)S(1)} %collective-permute-done.33.refs_3_), channel_id=1, source_target_pairs={{0,16},{16,0},{1,17},{17,1},{2,18},{18,2},{3,19},{19,3},{4,20},{20... | collective-permute-start | bytes 1327112 | tf_op jit(solution)/shard_map/ppermute | solution.py:19
  216.0 27.2 %collective-permute-start.44 = (bf16[9,32,768]{2,1,0:T(8,128)(2,1)S(1)}, bf16[9,32,768]{2,1,0:T(8,128)(2,1)S(1)}, u32[]{:S(2)}, u32[]{:S(2)}) collective-permute-start(bf16[9,32,768]{2,1,0:T(8,128)(2,1)S(1)} %collective-permute-done.34.refs_4_), channel_id=1, source_target_pairs={{0,16},{16,0},{1,17},{17,1},{2,18},{18,2},{3,19},{19,3},{4,20},{20... | collective-permute-start | bytes 1327112 | tf_op jit(solution)/shard_map/ppermute | solution.py:19
  229.7 32.4 %collective-permute-start.48 = (bf16[4,9,16,768]{3,2,1,0:T(8,128)(2,1)S(1)}, bf16[4,9,16,768]{3,2,1,0:T(8,128)(2,1)S(1)}, u32[]{:S(2)}, u32[]{:S(2)}) collective-permute-start(bf16[4,9,16,768]{3,2,1,0:T(8,128)(2,1)S(1)} %collective-permute-done.39.refs_8_), channel_id=1, source_target_pairs={{0,16},{16,0},{1,17},{17,1},{2,18},{18,2},{3,19},{19,3},{4,20},{20... | collective-permute-start | bytes 2654216 | tf_op jit(solution)/shard_map/ppermute | solution.py:19
  259.2 48.9 %collective-permute-start.80 = (bf16[9,32,768]{2,1,0:T(8,128)(2,1)S(1)}, bf16[9,32,768]{2,1,0:T(8,128)(2,1)S(1)}, u32[]{:S(2)}, u32[]{:S(2)}) collective-permute-start(bf16[9,32,768]{2,1,0:T(8,128)(2,1)S(1)} %collective-permute-done.70.refs_1_), channel_id=1, source_target_pairs={{0,16},{16,0},{1,17},{17,1},{2,18},{18,2},{3,19},{19,3},{4,20},{20... | collective-permute-start | bytes 1327112 | tf_op jit(solution)/shard_map/ppermute | solution.py:19
  260.2 49.0 %collective-permute-start.81 = (bf16[9,32,768]{2,1,0:T(8,128)(2,1)S(1)}, bf16[9,32,768]{2,1,0:T(8,128)(2,1)S(1)}, u32[]{:S(2)}, u32[]{:S(2)}) collective-permute-start(bf16[9,32,768]{2,1,0:T(8,128)(2,1)S(1)} %collective-permute-done.71.refs_2_), channel_id=1, source_target_pairs={{0,16},{16,0},{1,17},{17,1},{2,18},{18,2},{3,19},{19,3},{4,20},{20... | collective-permute-start | bytes 1327112 | tf_op jit(solution)/shard_map/ppermute | solution.py:19
  261.3 49.9 %collective-permute-start.78 = (bf16[4,9,16,768]{3,2,1,0:T(8,128)(2,1)}, bf16[4,9,16,768]{3,2,1,0:T(8,128)(2,1)}, u32[]{:S(2)}, u32[]{:S(2)}) collective-permute-start(bf16[4,9,16,768]{3,2,1,0:T(8,128)(2,1)} %pad_maximum_fusion.9), channel_id=1, source_target_pairs={{0,1},{1,0},{2,3},{3,2},{4,5},{5,4},{6,7},{7,6},{8,9},{9,8},{10,11... | collective-permute-start | bytes 2654216 | tf_op jit(solution)/shard_map/ppermute | solution.py:19
  263.0 47.3 %collective-permute-start.82 = (bf16[9,32,768]{2,1,0:T(8,128)(2,1)S(1)}, bf16[9,32,768]{2,1,0:T(8,128)(2,1)S(1)}, u32[]{:S(2)}, u32[]{:S(2)}) collective-permute-start(bf16[9,32,768]{2,1,0:T(8,128)(2,1)S(1)} %collective-permute-done.72.refs_3_), channel_id=1, source_target_pairs={{0,16},{16,0},{1,17},{17,1},{2,18},{18,2},{3,19},{19,3},{4,20},{20... | collective-permute-start | bytes 1327112 | tf_op jit(solution)/shard_map/ppermute | solution.py:19
  263.9 47.7 %collective-permute-start.79 = (bf16[3,9,16,768]{3,2,1,0:T(8,128)(2,1)S(1)}, bf16[3,9,16,768]{3,2,1,0:T(8,128)(2,1)}, u32[]{:S(2)}, u32[]{:S(2)}) collective-permute-start(bf16[3,9,16,768]{3,2,1,0:T(8,128)(2,1)S(1)} %pad_maximum_fusion.11), channel_id=1, source_target_pairs={{0,1},{1,0},{2,3},{3,2},{4,5},{5,4},{6,7},{7,6},{8,9},{9,8},{10,11... | collective-permute-start | bytes 1990664 | tf_op jit(solution)/shard_map/ppermute | solution.py:19
  308.9 29.1 %collective-permute-start.69 = (bf16[2,512,768]{2,1,0:T(8,128)(2,1)}, bf16[2,512,768]{2,1,0:T(8,128)(2,1)}, u32[]{:S(2)}, u32[]{:S(2)}) collective-permute-start(bf16[2,512,768]{2,1,0:T(8,128)(2,1)} %pad_maximum_fusion.7.own_ref), channel_id=1, source_target_pairs={{0,16},{16,0},{1,17},{17,1},{2,18},{18,2},{3,19},{19,3},{4,20},{20... | collective-permute-start | bytes 4718600 | tf_op jit(solution)/shard_map/ppermute | solution.py:19
  319.7 41.5 %collective-permute-start.90 = (bf16[512,768]{1,0:T(8,128)(2,1)}, bf16[512,768]{1,0:T(8,128)(2,1)S(1)}, u32[]{:S(2)}, u32[]{:S(2)}) collective-permute-start(bf16[512,768]{1,0:T(8,128)(2,1)} %bitcast.611), channel_id=1, source_target_pairs={{0,0},{1,16},{16,1},{17,17},{2,2},{3,18},{18,3},{19,19},{4,4},{5,2... | collective-permute-start | bytes 2359304 | tf_op jit(solution)/shard_map/ppermute | solution.py:23
  384.4 46.5 %collective-permute-start.91 = (bf16[8,8,48,768]{3,2,1,0:T(8,128)(2,1)}, bf16[8,8,48,768]{3,2,1,0:T(8,128)(2,1)}, u32[]{:S(2)}, u32[]{:S(2)}) collective-permute-start(bf16[8,8,48,768]{3,2,1,0:T(8,128)(2,1)} %constant_dynamic-slice_fusion.38), channel_id=1, source_target_pairs={{0,16},{16,0},{1,17},{17,1},{2,18},{18,2},{3,19},{19,3},{4,20},{20... | collective-permute-start | bytes 14155784 | tf_op jit(solution)/shard_map/ppermute | solution.py:19
  417.8 83.7 %collective-permute-start.89 = (bf16[512,768]{1,0:T(8,128)(2,1)}, bf16[512,768]{1,0:T(8,128)(2,1)}, u32[]{:S(2)}, u32[]{:S(2)}) collective-permute-start(bf16[512,768]{1,0:T(8,128)(2,1)} %get-tuple-element.299), channel_id=1, source_target_pairs={{0,0},{1,16},{16,1},{17,17},{2,2},{3,18},{18,3},{19,19},{4,4},{5,2... | collective-permute-start | bytes 2359304 | tf_op jit(solution)/shard_map/ppermute | solution.py:23
  442.6 37.8 %collective-permute-start.96 = (bf16[2,8,16,768]{3,2,1,0:T(8,128)(2,1)}, bf16[2,8,16,768]{3,2,1,0:T(8,128)(2,1)S(1)}, u32[]{:S(2)}, u32[]{:S(2)}) collective-permute-start(bf16[2,8,16,768]{3,2,1,0:T(8,128)(2,1)} %pad_maximum_fusion.18), channel_id=1, source_target_pairs={{0,1},{1,0},{2,3},{3,2},{4,5},{5,4},{6,7},{7,6},{8,9},{9,8},{10,11... | collective-permute-start | bytes 1179656 | tf_op jit(solution)/shard_map/ppermute | solution.py:19
  526.0 34.8 %collective-permute-start.105 = (bf16[8,32,768]{2,1,0:T(8,128)(2,1)S(1)}, bf16[8,32,768]{2,1,0:T(8,128)(2,1)S(1)}, u32[]{:S(2)}, u32[]{:S(2)}) collective-permute-start(bf16[8,32,768]{2,1,0:T(8,128)(2,1)S(1)} %get-tuple-element.246), channel_id=1, source_target_pairs={{0,4},{4,8},{8,12},{12,14},{14,10},{10,6},{6,2},{2,0},{1,5},{5,9},... | collective-permute-start | bytes 1179656 | tf_op jit(solution)/shard_map/ppermute | solution.py:64
  527.2 35.1 %collective-permute-start.106 = (bf16[8,32,768]{2,1,0:T(8,128)(2,1)S(1)}, bf16[8,32,768]{2,1,0:T(8,128)(2,1)}, u32[]{:S(2)}, u32[]{:S(2)}) collective-permute-start(bf16[8,32,768]{2,1,0:T(8,128)(2,1)S(1)} %get-tuple-element.245), channel_id=1, source_target_pairs={{0,2},{4,0},{8,4},{12,8},{14,12},{10,14},{6,10},{2,6},{1,3},{5,1},... | collective-permute-start | bytes 1179656 | tf_op jit(solution)/shard_map/ppermute | solution.py:64
  534.0 25.0 %collective-permute-start.107 = (bf16[1,4,16,768]{3,2,1,0:T(8,128)(2,1)S(1)}, bf16[1,4,16,768]{3,2,1,0:T(8,128)(2,1)S(1)}, u32[]{:S(2)}, u32[]{:S(2)}) collective-permute-start(bf16[1,4,16,768]{3,2,1,0:T(8,128)(2,1)S(1)} %get-tuple-element.293), channel_id=1, source_target_pairs={{0,1},{1,0},{2,3},{3,2},{4,5},{5,4},{6,7},{7,6},{8,9},{9,8},{10,11... | collective-permute-start | bytes 294920 | tf_op jit(solution)/shard_map/ppermute | solution.py:19
  537.1 23.8 %collective-permute-start.108 = (bf16[2,4,16,768]{3,2,1,0:T(8,128)(2,1)S(1)}, bf16[2,4,16,768]{3,2,1,0:T(8,128)(2,1)S(1)}, u32[]{:S(2)}, u32[]{:S(2)}) collective-permute-start(bf16[2,4,16,768]{3,2,1,0:T(8,128)(2,1)S(1)} %pad_maximum_fusion.33), channel_id=1, source_target_pairs={{0,1},{1,0},{2,3},{3,2},{4,5},{5,4},{6,7},{7,6},{8,9},{9,8},{10,11... | collective-permute-start | bytes 589832 | tf_op jit(solution)/shard_map/ppermute | solution.py:19
  555.7 26.4 %collective-permute-start.112 = (bf16[2,4,16,768]{3,2,1,0:T(8,128)(2,1)}, bf16[2,4,16,768]{3,2,1,0:T(8,128)(2,1)}, u32[]{:S(2)}, u32[]{:S(2)}) collective-permute-start(bf16[2,4,16,768]{3,2,1,0:T(8,128)(2,1)} %pad_maximum_fusion.34), channel_id=1, source_target_pairs={{0,1},{1,0},{2,3},{3,2},{4,5},{5,4},{6,7},{7,6},{8,9},{9,8},{10,11... | collective-permute-start | bytes 589832 | tf_op jit(solution)/shard_map/ppermute | solution.py:19
  559.1 47.4 %collective-permute-start.116 = (bf16[2,4,16,768]{3,2,1,0:T(8,128)(2,1)}, bf16[2,4,16,768]{3,2,1,0:T(8,128)(2,1)}, u32[]{:S(2)}, u32[]{:S(2)}) collective-permute-start(bf16[2,4,16,768]{3,2,1,0:T(8,128)(2,1)} %pad_maximum_fusion.37), channel_id=1, source_target_pairs={{0,1},{1,0},{2,3},{3,2},{4,5},{5,4},{6,7},{7,6},{8,9},{9,8},{10,11... | collective-permute-start | bytes 589832 | tf_op jit(solution)/shard_map/ppermute | solution.py:19
  585.1 22.3 %collective-permute-start.113 = (bf16[8,48,768]{2,1,0:T(8,128)(2,1)}, bf16[8,48,768]{2,1,0:T(8,128)(2,1)}, u32[]{:S(2)}, u32[]{:S(2)}) collective-permute-start(bf16[8,48,768]{2,1,0:T(8,128)(2,1)} %pad_maximum_fusion.12), channel_id=1, source_target_pairs={{0,16},{16,0},{1,17},{17,1},{2,18},{18,2},{3,19},{19,3},{4,20},{20... | collective-permute-start | bytes 1769480 | tf_op jit(solution)/shard_map/ppermute | solution.py:19
  586.0 21.3 %collective-permute-start.114 = (bf16[4,32,768]{2,1,0:T(8,128)(2,1)S(1)}, bf16[4,32,768]{2,1,0:T(8,128)(2,1)S(1)}, u32[]{:S(2)}, u32[]{:S(2)}) collective-permute-start(bf16[4,32,768]{2,1,0:T(8,128)(2,1)S(1)} %pad_maximum_fusion.35), channel_id=1, source_target_pairs={{0,4},{4,8},{8,12},{12,14},{14,10},{10,6},{6,2},{2,0},{1,5},{5,9},... | collective-permute-start | bytes 589832 | tf_op jit(solution)/shard_map/ppermute | solution.py:64
  599.0 23.8 %collective-permute-start.120 = (bf16[8,8,48,768]{3,2,1,0:T(8,128)(2,1)}, bf16[8,8,48,768]{3,2,1,0:T(8,128)(2,1)}, u32[]{:S(2)}, u32[]{:S(2)}) collective-permute-start(bf16[8,8,48,768]{3,2,1,0:T(8,128)(2,1)} %constant_dynamic-slice_fusion.15), channel_id=1, source_target_pairs={{0,16},{16,0},{1,17},{17,1},{2,18},{18,2},{3,19},{19,3},{4,20},{20... | collective-permute-start | bytes 14155784 | tf_op jit(solution)/shard_map/ppermute | solution.py:19
  638.5 48.9 %collective-permute-start.128 = (bf16[2,8,16,768]{3,2,1,0:T(8,128)(2,1)}, bf16[2,8,16,768]{3,2,1,0:T(8,128)(2,1)}, u32[]{:S(2)}, u32[]{:S(2)}) collective-permute-start(bf16[2,8,16,768]{3,2,1,0:T(8,128)(2,1)} %pad_maximum_fusion.23), channel_id=1, source_target_pairs={{0,1},{1,0},{2,3},{3,2},{4,5},{5,4},{6,7},{7,6},{8,9},{9,8},{10,11... | collective-permute-start | bytes 1179656 | tf_op jit(solution)/shard_map/ppermute | solution.py:19
  687.7 49.6 %collective-permute-start.136 = (bf16[1,8,16,768]{3,2,1,0:T(8,128)(2,1)}, bf16[1,8,16,768]{3,2,1,0:T(8,128)(2,1)}, u32[]{:S(2)}, u32[]{:S(2)}) collective-permute-start(bf16[1,8,16,768]{3,2,1,0:T(8,128)(2,1)} %get-tuple-element.232), channel_id=1, source_target_pairs={{0,1},{1,0},{2,3},{3,2},{4,5},{5,4},{6,7},{7,6},{8,9},{9,8},{10,11... | collective-permute-start | bytes 589832 | tf_op jit(solution)/shard_map/ppermute | solution.py:19
  709.3 28.0 %collective-permute-start.134 = (bf16[8,32,768]{2,1,0:T(8,128)(2,1)}, bf16[8,32,768]{2,1,0:T(8,128)(2,1)}, u32[]{:S(2)}, u32[]{:S(2)}) collective-permute-start(bf16[8,32,768]{2,1,0:T(8,128)(2,1)} %get-tuple-element.241), channel_id=1, source_target_pairs={{0,4},{4,8},{8,12},{12,14},{14,10},{10,6},{6,2},{2,0},{1,5},{5,9},... | collective-permute-start | bytes 1179656 | tf_op jit(solution)/shard_map/ppermute | solution.py:64
  710.0 27.4 %collective-permute-start.135 = (bf16[8,32,768]{2,1,0:T(8,128)(2,1)}, bf16[8,32,768]{2,1,0:T(8,128)(2,1)}, u32[]{:S(2)}, u32[]{:S(2)}) collective-permute-start(bf16[8,32,768]{2,1,0:T(8,128)(2,1)} %get-tuple-element.240), channel_id=1, source_target_pairs={{0,2},{4,0},{8,4},{12,8},{14,12},{10,14},{6,10},{2,6},{1,3},{5,1},... | collective-permute-start | bytes 1179656 | tf_op jit(solution)/shard_map/ppermute | solution.py:64
  714.9 22.5 %collective-permute-start.137 = (bf16[8,4,48,768]{3,2,1,0:T(8,128)(2,1)}, bf16[8,4,48,768]{3,2,1,0:T(8,128)(2,1)}, u32[]{:S(2)}, u32[]{:S(2)}) collective-permute-start(bf16[8,4,48,768]{3,2,1,0:T(8,128)(2,1)} %constant_dynamic-slice_fusion.22), channel_id=1, source_target_pairs={{0,16},{16,0},{1,17},{17,1},{2,18},{18,2},{3,19},{19,3},{4,20},{20... | collective-permute-start | bytes 7077896 | tf_op jit(solution)/shard_map/ppermute | solution.py:19
  739.9 86.9 %collective-permute-start.138 = (bf16[512,768]{1,0:T(8,128)(2,1)}, bf16[512,768]{1,0:T(8,128)(2,1)}, u32[]{:S(2)}, u32[]{:S(2)}) collective-permute-start(bf16[512,768]{1,0:T(8,128)(2,1)} %get-tuple-element.306), channel_id=1, source_target_pairs={{0,0},{1,16},{16,1},{17,17},{2,2},{3,18},{18,3},{19,19},{4,4},{5,2... | collective-permute-start | bytes 2359304 | tf_op jit(solution)/shard_map/ppermute | solution.py:23
  752.6 30.7 %collective-permute-start.155 = (bf16[2,4,16,768]{3,2,1,0:T(8,128)(2,1)}, bf16[2,4,16,768]{3,2,1,0:T(8,128)(2,1)}, u32[]{:S(2)}, u32[]{:S(2)}) collective-permute-start(bf16[2,4,16,768]{3,2,1,0:T(8,128)(2,1)} %pad_maximum_fusion.40), channel_id=1, source_target_pairs={{0,1},{1,0},{2,3},{3,2},{4,5},{5,4},{6,7},{7,6},{8,9},{9,8},{10,11... | collective-permute-start | bytes 589832 | tf_op jit(solution)/shard_map/ppermute | solution.py:19
  752.6 33.7 %collective-permute-start.156 = (bf16[1,4,16,768]{3,2,1,0:T(8,128)(2,1)}, bf16[1,4,16,768]{3,2,1,0:T(8,128)(2,1)}, u32[]{:S(2)}, u32[]{:S(2)}) collective-permute-start(bf16[1,4,16,768]{3,2,1,0:T(8,128)(2,1)} %get-tuple-element.273), channel_id=1, source_target_pairs={{0,1},{1,0},{2,3},{3,2},{4,5},{5,4},{6,7},{7,6},{8,9},{9,8},{10,11... | collective-permute-start | bytes 294920 | tf_op jit(solution)/shard_map/ppermute | solution.py:19
  755.9 32.8 %collective-permute-start.154 = (bf16[2,4,16,768]{3,2,1,0:T(8,128)(2,1)}, bf16[2,4,16,768]{3,2,1,0:T(8,128)(2,1)}, u32[]{:S(2)}, u32[]{:S(2)}) collective-permute-start(bf16[2,4,16,768]{3,2,1,0:T(8,128)(2,1)} %pad_maximum_fusion.39), channel_id=1, source_target_pairs={{0,1},{1,0},{2,3},{3,2},{4,5},{5,4},{6,7},{7,6},{8,9},{9,8},{10,11... | collective-permute-start | bytes 589832 | tf_op jit(solution)/shard_map/ppermute | solution.py:19
  783.2 46.0 %collective-permute-start.152 = (bf16[1,4,16,768]{3,2,1,0:T(8,128)(2,1)}, bf16[1,4,16,768]{3,2,1,0:T(8,128)(2,1)S(1)}, u32[]{:S(2)}, u32[]{:S(2)}) collective-permute-start(bf16[1,4,16,768]{3,2,1,0:T(8,128)(2,1)} %get-tuple-element.272), channel_id=1, source_target_pairs={{0,1},{1,0},{2,3},{3,2},{4,5},{5,4},{6,7},{7,6},{8,9},{9,8},{10,11... | collective-permute-start | bytes 294920 | tf_op jit(solution)/shard_map/ppermute | solution.py:19
  (389 other events, 4452.2 us)

commit v3 on v2

--- a/solution.py
+++ b/solution.py
@@ -20,7 +20,8 @@
 
 
 def swap_layout(value):
-    return lax.ppermute(value, ("rep", "seq"), [(0, 0), (1, 2), (2, 1), (3, 3)])
+    moved = lax.ppermute(value, ("rep", "seq"), [(1, 2), (2, 1)])
+    return jnp.where(lax.axis_index("rep") == lax.axis_index("seq"), value, moved)
 
 
 def cube_pairs(value, axis, bit):
@@ -77,83 +78,75 @@
 OFFSETS = (-1, 1, -2, 2, -3, 3, 4)
 
 
-def place_kernel(plain, split, where, *refs):
-    (own, *rest) = refs[:19]
-    outs = refs[19:-1]
-    sem = refs[-1]
-    blocks, near_x, far_x = rest[0:7], rest[7], rest[8]
-    core_blocks, core_near_x, core_far_x = rest[9:16], rest[16], rest[17]
+def place_kernel(where, *refs):
+    (own, *rest) = refs[:23]
+    out, sem = refs[23:]
+    blocks, beside = rest[0:7], rest[7:11]
+    core_blocks, core_beside = rest[11:18], rest[18:22]
     rep, seq = where[8], where[9]
     unit = own.shape[1] // 6
 
     def put(src, shard, row, rows):
-        copies = []
-        if plain:
-            start = pl.multiple_of(shard * (6 * unit) + row * unit, unit)
-            copies.append(
-                pltpu.make_async_copy(src.at[0:plain], outs[0].at[:, pl.ds(start, rows), :], sem)
-            )
-        if split:
-            start = pl.multiple_of(row * unit, unit)
-            copies.append(
-                pltpu.make_async_copy(
-                    src.at[plain : plain + split],
-                    outs[-1].at[shard, :, pl.ds(start, rows), :],
-                    sem,
-                )
-            )
-        for copy in copies:
-            copy.start()
-        return copies
+        start = pl.multiple_of(row * unit, unit)
+        copy = pltpu.make_async_copy(src, out.at[shard, :, pl.ds(start, rows), :], sem)
+        copy.start()
+        return [copy]
 
     copies = put(own, where[0], 0, 6 * unit)
     for slot, offset in enumerate(OFFSETS):
         shard = where[offset % 8]
-        beside = (near_x, core_near_x) if slot < 4 else (far_x, core_far_x)
-        at = slot if slot < 4 else slot - 4
+        far = 3 * rep + 2 * (1 - seq)
         copies += put(blocks[slot], shard, 3 * rep + seq, 2 * unit)
-        copies += put(beside[0].at[at], shard, 3 * rep + 2 * (1 - seq), unit)
+        copies += put(beside[slot // 2].at[slot % 2], shard, far, unit)
+        far = 3 * (1 - rep) + 2 * (1 - seq)
         copies += put(core_blocks[slot], shard, 3 * (1 - rep) + seq, 2 * unit)
-        copies += put(beside[1].at[at], shard, 3 * (1 - rep) + 2 * (1 - seq), unit)
+        copies += put(core_beside[slot // 2].at[slot % 2], shard, far, unit)
     for copy in copies:
         copy.wait()
 
 
-def gather_ring(piece, split):
+def gather_ring(piece):
     count, rows, width = piece.shape
     shards = lax.axis_size("shard")
     unit = rows // 6
     rep, seq = lax.axis_index("rep"), lax.axis_index("seq")
     mine = lax.dynamic_slice(piece, (0, (3 * rep + seq) * unit, 0), (count, 2 * unit, width))
 
-    def cross(blocks):
+    def cross(*blocks):
         cut = [
             lax.dynamic_slice(block, (0, seq * unit, 0), (count, unit, width)) for block in blocks
         ]
         return swap_pairs(jnp.stack(cut), "seq")
 
-    up1, down1 = ring_step(mine, True), ring_step(mine, False)
-    up2, down2 = ring_step(up1, True), ring_step(down1, False)
-    near_x = cross([up1, down1, up2, down2])
-    up3, down3 = ring_step(up2, True), ring_step(down2, False)
-    up4, down4 = ring_step(up3[:, :unit], True), ring_step(down3[:, unit:], False)
+    def core(block):
+        return swap_pairs(block, "rep")
+
+    def around(up, down):
+        return ring_step(up, True), ring_step(down, False)
+
+    up1, down1 = yield around(mine, mine)
+    up2, down2, x1, *core1 = yield (
+        *around(up1, down1), cross(up1, down1), core(up1), core(down1)
+    )
+    up3, down3, x2, *core2 = yield (
+        *around(up2, down2), cross(up2, down2), core(up2), core(down2), core(x1)
+    )
+    up4, down4, x3, *core3 = yield (
+        *around(up3[:, :unit], down3[:, unit:]), cross(up3, down3), core(up3), core(down3), core(x2)
+    )
     far = jnp.concatenate([up4, down4], axis=1)
-    far_x = cross([up3, down3, far])
-    parts = [up1, down1, up2, down2, up3, down3, far, near_x, far_x]
-    parts += [swap_pairs(part, "rep") for part in parts]
+    x4, *core4 = yield (cross(far), core(far), core(x3))
+    (core_x4,) = yield (core(x4),)
+    parts = [up1, down1, up2, down2, up3, down3, far, x1, x2, x3, x4]
+    parts += core1 + core2[:2] + core3[:2] + core4[:1]
+    parts += [core2[2], core3[2], core4[1], core_x4]
     where = jnp.concatenate([ring_ids(), jnp.stack([rep, seq]).astype(jnp.int32)])
-    plain = count - split
-    shapes = []
-    if plain:
-        shapes.append(jax.ShapeDtypeStruct((plain, shards * rows, width), piece.dtype))
-    if split:
-        shapes.append(jax.ShapeDtypeStruct((shards, split, rows, width), piece.dtype))
     anywhere = pl.BlockSpec(memory_space=pl.ANY)
     return pl.pallas_call(
-        functools.partial(place_kernel, plain, split),
-        out_shape=tuple(shapes),
-        in_specs=[pl.BlockSpec(memory_space=pltpu.SMEM)] + [anywhere] * 19,
-        out_specs=(pl.BlockSpec(memory_space=pltpu.VMEM),) * len(shapes),
+        place_kernel,
+        out_shape=jax.ShapeDtypeStruct((shards, count, rows, width), piece.dtype),
+        in_specs=[pl.BlockSpec(memory_space=pltpu.SMEM)] + [anywhere] * 23,
+        out_specs=pl.BlockSpec(memory_space=pltpu.VMEM),
         compiler_params=pltpu.CompilerParams(vmem_limit_bytes=32 * 2**20),
         scratch_shapes=[pltpu.SemaphoreType.DMA],
         cost_estimate=pl.CostEstimate(
@@ -162,16 +155,26 @@
     )(where, piece, *parts)
 
 
-def gather_plain(piece, split):
+def gather_wide(piece):
     count, rows, width = piece.shape
-    shards = lax.axis_size("shard")
-    plain = count - split
-    outs = []
-    if plain:
-        outs.append(lax.all_gather(piece[:plain], "shard", axis=1, tiled=True))
-    if split:
-        outs.append(lax.all_gather(piece[plain:], "shard", axis=0, tiled=False))
-    return tuple(outs)
+    copies = lax.axis_size("rep") * lax.axis_size("seq")
+    at = lax.axis_index("rep") * lax.axis_size("seq") + lax.axis_index("seq")
+    own = lax.dynamic_slice(piece, (at * (count // copies), 0, 0), (count // copies, rows, width))
+    whole_piece = lax.all_gather(
+        own.reshape(-1, width), ("shard", "rep", "seq"), axis=0, tiled=True
+    )
+    return whole_piece.reshape(-1, count, rows, width)
+
+
+def gather_plain(piece, stacked):
+    first, parts = stacked
+    width = piece.shape[2]
+    whole_piece = lax.all_gather(piece, "shard", axis=0, tiled=False)
+    flat = whole_piece.transpose(1, 0, 2, 3).reshape(-1, width, width)
+    if parts:
+        tall = whole_piece[:, first : first + parts].reshape(parts, width, width)
+        flat = jnp.concatenate([flat[:first], tall, flat[first + parts :]])
+    return flat[None]
 
 
 def ring_fits(rows):
@@ -183,24 +186,25 @@
     )
 
 
-def gather(piece, split):
-    return (gather_ring if ring_fits(piece.shape[1]) else gather_plain)(piece, split)
-
-
 def add(left, right):
     return (left.astype(F32) + right.astype(F32)).astype(BF16)
 
 
 def scatter_ring(grads):
-    shards, count, rows, width = grads.shape
+    shards, _, rows, width = grads[0].shape
+    count = sum(part.shape[1] for part in grads)
     unit = rows // 6
     rep, seq = lax.axis_index("rep"), lax.axis_index("seq")
     ids = ring_ids()
 
     def half(which):
-        return lax.dynamic_slice(
-            grads, (0, 0, 3 * unit * which, 0), (shards, count, 3 * unit, width)
-        )
+        cut = [
+            lax.dynamic_slice(
+                part, (0, 0, 3 * unit * which, 0), (shards, part.shape[1], 3 * unit, width)
+            )
+            for part in grads
+        ]
+        return jnp.concatenate(cut, axis=1)
 
     (got,) = yield (swap_pairs(half(1 - rep), "rep"),)
     paired = add(half(rep), got)
@@ -259,35 +263,66 @@
     ).astype(F32)
 
 
-class Background:
-    def __init__(self):
+class Moves:
+    def __init__(self, queue=()):
+        self.queue = list(queue)
         self.running = []
         self.done = {}
+        if self.queue:
+            self.pull()
+
+    def pull(self):
+        (key, piece, stacked) = self.queue.pop(0)
+        if not ring_fits(piece.shape[1]):
+            self.done[key] = gather_plain(piece, stacked)
+            return
+        if self.running:
+            piece, moving = lax.optimization_barrier(
+                (piece, [moving for _, _, moving, _ in self.running])
+            )
+            self.running = [
+                (*move[:2], got, move[3]) for move, got in zip(self.running, moving)
+            ]
+        stages = gather_ring(piece)
+        self.running.append((key, stages, next(stages), 1))
 
     def start(self, key, grads):
-        if not ring_fits(grads.shape[2]):
-            self.done[key] = scatter_plain(grads)
-            return
         stages = scatter_ring(grads)
-        self.running.append((key, stages, next(stages)))
+        self.running.append((key, stages, next(stages), 9))
 
     def tick(self, value=None):
-        waiting = [moving for _, _, moving in self.running]
+        waiting = [moving for _, _, moving, _ in self.running]
         if value is not None and waiting:
             value, waiting = lax.optimization_barrier((value, waiting))
         still = []
-        for (key, stages, _), moving in zip(self.running, waiting):
+        for (key, stages, _, count), moving in zip(self.running, waiting):
             try:
-                still.append((key, stages, stages.send(moving)))
+                still.append((key, stages, stages.send(moving), count + 1))
             except StopIteration as end:
                 self.done[key] = end.value
         self.running = still
+        if self.queue and all(count > 4 for _, _, _, count in still):
+            self.pull()
         return value
 
+    def need(self, key):
+        while key not in self.done:
+            self.tick()
+        return self.done[key]
+
     def finish(self):
-        while self.running:
+        while self.running or self.queue:
             self.tick()
         return self.done
+
+
+def scatter_wide(grads):
+    return lax.psum_scatter(
+        grads.reshape(-1, grads.shape[-1]),
+        ("shard", "rep", "seq"),
+        scatter_dimension=0,
+        tiled=True,
+    )
 
 
 def scatter_plain(grads):
@@ -442,113 +477,366 @@
     )(queries, own_kv, other_kv, grad_mixed, mixed, log_total)
 
 
-def layer_forward(stream, modulation, weights, biases):
-    qkv_w, proj_w, fc1_w, fc2_w = weights
+def params_of(megabytes=48):
+    return pltpu.CompilerParams(vmem_limit_bytes=megabytes * 2**20)
+
+
+def whole(shape):
+    return pl.BlockSpec(shape, lambda *at: (0,) * len(shape))
+
+
+def column_sum(values):
+    return jnp.sum(values, axis=0, keepdims=True)
+
+
+def matrix_at(array, at, moving=True):
+    shards, _, rows, width = array.shape
+    return pl.BlockSpec(
+        (shards, 1, rows, width), lambda part: (0, at + part if moving else at, 0, 0)
+    )
+
+
+def tall_at(array, at, parts):
+    shards, _, rows, width = array.shape
+    if shards == 1:
+        return matrix_at(array, at)
+    return pl.BlockSpec((shards // parts, parts, rows, width), lambda part: (part, at // parts, 0, 0))
+
+
+def square(ref):
+    return ref[...].reshape(ref.shape[-1], ref.shape[-1])
+
+
+def put_square(ref, value):
+    ref[...] = value.astype(ref.dtype).reshape(ref.shape)
+
+
+def project_kernel(stream_ref, mod_ref, weight_ref, bias_ref, normed_ref, q_ref, kv_ref):
+    part = pl.program_id(0)
+
+    @pl.when(part == 0)
+    def _():
+        normal, _ = normalize(stream_ref[...])
+        normed_ref[...] = (normal * (1.0 + mod_ref[1:2]) + mod_ref[0:1]).astype(BF16)
+
+    result = (nn(normed_ref[...], square(weight_ref)) + bias_ref[0]).astype(BF16)
+
+    @pl.when(part == 0)
+    def _():
+        q_ref[...] = result
+
+    @pl.when(part > 0)
+    def _():
+        kv_ref[0] = result
+
+
+def project(stream, modulation, weights, at, bias):
+    tokens, width = stream.shape
+    return pl.pallas_call(
+        project_kernel,
+        grid=(3,),
+        in_specs=[
+            whole((tokens, width)),
+            whole((6, width)),
+            matrix_at(weights, at),
+            pl.BlockSpec((1, 1, width), lambda part: (part, 0, 0)),
+        ],
+        out_specs=(
+            whole((tokens, width)),
+            whole((tokens, width)),
+            pl.BlockSpec((1, tokens, width), lambda part: (jnp.maximum(part - 1, 0), 0, 0)),
+        ),
+        out_shape=(
+            jax.ShapeDtypeStruct((tokens, width), BF16),
+            jax.ShapeDtypeStruct((tokens, width), BF16),
+            jax.ShapeDtypeStruct((2, tokens, width), BF16),
+        ),
+        compiler_params=params_of(),
+        cost_estimate=pl.CostEstimate(
+            flops=6 * tokens * width**2, transcendentals=0, bytes_accessed=12 * tokens * width
+        ),
+    )(stream, modulation, weights, bias)
+
+
+GELU_SCALE = math.sqrt(2.0 / math.pi)
+
+
+def gelu_parts(value):
+    square = value * value
+    tanh = jnp.tanh(GELU_SCALE * value * (1.0 + 0.044715 * square))
+    return square, tanh
+
+
+def mlp_kernel(
+    mixed_ref, stream_ref, mod_ref, proj_ref, proj_b_ref, fc1_ref, fc1_b_ref, fc2_ref, fc2_b_ref,
+    attn_ref, middle_ref, normed_ref, hidden_ref, active_ref, mlp_ref, result_ref,
+):
+    part = pl.program_id(0)
+
+    @pl.when(part == 0)
+    def _():
+        attn_out = nn(mixed_ref[...], square(proj_ref)) + proj_b_ref[...]
+        attn_ref[...] = attn_out
+        middle = stream_ref[...] + mod_ref[2:3] * attn_out
+        middle_ref[...] = middle
+        normal, _ = normalize(middle)
+        normed_ref[...] = (normal * (1.0 + mod_ref[4:5]) + mod_ref[3:4]).astype(BF16)
+
+    hidden = nn(normed_ref[...], square(fc1_ref)) + fc1_b_ref[0]
+    hidden_ref[0] = hidden
+    _, tanh = gelu_parts(hidden)
+    active = (0.5 * hidden * (1.0 + tanh)).astype(BF16)
+    active_ref[0] = active
+    product = nn(active, square(fc2_ref))
+
+    @pl.when(part == 0)
+    def _():
+        mlp_ref[...] = product + fc2_b_ref[...]
+
+    @pl.when(part > 0)
+    def _():
+        mlp_ref[...] += product
+
+    @pl.when(part == pl.num_programs(0) - 1)
+    def _():
+        result_ref[...] = middle_ref[...] + mod_ref[5:6] * mlp_ref[...]
+
+
+def mlp(mixed, stream, modulation, weights, proj_b, fc1_b, fc2_b):
+    tokens, width = stream.shape
+    parts = fc1_b.shape[0]
+    token, row = whole((tokens, width)), whole((1, width))
+    by_part = lambda rows: pl.BlockSpec((1, rows, width), lambda part: (part, 0, 0))
+    shape = lambda *dims: jax.ShapeDtypeStruct(dims[:-1], dims[-1])
+    return pl.pallas_call(
+        mlp_kernel,
+        grid=(parts,),
+        in_specs=[
+            token, token, whole((6, width)), matrix_at(weights, 2 * parts, False), row,
+            matrix_at(weights, 0), by_part(1), tall_at(weights, parts, parts), row,
+        ],
+        out_specs=(token, token, token, by_part(tokens), by_part(tokens), token, token),
+        out_shape=(
+            shape(tokens, width, F32),
+            shape(tokens, width, F32),
+            shape(tokens, width, BF16),
+            shape(parts, tokens, width, F32),
+            shape(parts, tokens, width, BF16),
+            shape(tokens, width, F32),
+            shape(tokens, width, F32),
+        ),
+        compiler_params=params_of(),
+        cost_estimate=pl.CostEstimate(
+            flops=(2 + 4 * parts) * tokens * width**2,
+            transcendentals=parts * tokens * width,
+            bytes_accessed=(20 + 6 * parts) * tokens * width,
+        ),
+    )(mixed, stream, modulation, weights, proj_b, weights, fc1_b, weights, fc2_b)
+
+
+def mlp_back_kernel(
+    grad_ref, mlp_ref, mod_ref, fc2_ref, fc1_ref, hidden_ref, active_ref, normed_ref, middle_ref,
+    attn_ref, mixed_ref, proj_ref,
+    fc2_g_ref, fc1_g_ref, proj_g_ref, fc1_b_ref, sums_ref, grad_middle_ref, grad_mixed_ref,
+    low_ref, total_ref,
+):
+    part = pl.program_id(0)
+
+    @pl.when(part == 0)
+    def _():
+        grad = grad_ref[...]
+        sums_ref[2:3] = column_sum(grad * mlp_ref[...])
+        low = (grad * mod_ref[5:6]).astype(BF16)
+        low_ref[...] = low
+        sums_ref[4:5] = column_sum(low.astype(F32))
+
+    low = low_ref[...]
+    put_square(fc2_g_ref, tn(active_ref[0], low))
+    hidden = hidden_ref[0]
+    squared, tanh = gelu_parts(hidden)
+    slope = 0.5 * (1.0 + tanh) + (0.5 * GELU_SCALE) * hidden * (1.0 - tanh * tanh) * (
+        1.0 + (3 * 0.044715) * squared
+    )
+    grad_hidden = (nt(low, square(fc2_ref)) * slope).astype(BF16)
+    fc1_b_ref[0] = column_sum(grad_hidden.astype(F32))
+    put_square(fc1_g_ref, tn(normed_ref[...], grad_hidden))
+    product = nt(grad_hidden, square(fc1_ref))
+
+    @pl.when(part == 0)
+    def _():
+        total_ref[...] = product
+
+    @pl.when(part > 0)
+    def _():
+        total_ref[...] += product
+
+    @pl.when(part == pl.num_programs(0) - 1)
+    def _():
+        grad_normed = total_ref[...]
+        normal, scale = normalize(middle_ref[...])
+        sums_ref[0:1] = column_sum(grad_normed)
+        sums_ref[1:2] = column_sum(grad_normed * normal)
+        grad_middle = grad_ref[...] + norm_back(grad_normed, normal, scale, mod_ref[4:5])
+        grad_middle_ref[...] = grad_middle
+        sums_ref[3:4] = column_sum(grad_middle * attn_ref[...])
+        grad_attn = (grad_middle * mod_ref[2:3]).astype(BF16)
+        sums_ref[5:6] = column_sum(grad_attn.astype(F32))
+        put_square(proj_g_ref, tn(mixed_ref[...], grad_attn))
+        grad_mixed_ref[...] = nt(grad_attn, square(proj_ref)).astype(BF16)
+
+
+def mlp_back(grad, mlp_out, modulation, weights, hidden, active, normed, middle, attn_out, mixed):
+    tokens, width = grad.shape
+    parts = hidden.shape[0]
+    token = whole((tokens, width))
+    form = (weights.shape[0], parts) + weights.shape[2:]
+    fc_form, proj_form = jax.ShapeDtypeStruct(form, BF16), jax.ShapeDtypeStruct(
+        (form[0], 1) + form[2:], BF16
+    )
+    by_part = lambda rows: pl.BlockSpec((1, rows, width), lambda part: (part, 0, 0))
+    shape = lambda *dims: jax.ShapeDtypeStruct(dims[:-1], dims[-1])
+    return pl.pallas_call(
+        mlp_back_kernel,
+        grid=(parts,),
+        in_specs=[
+            token, token, whole((6, width)), tall_at(weights, parts, parts), matrix_at(weights, 0),
+            by_part(tokens), by_part(tokens), token, token, token, token,
+            matrix_at(weights, 2 * parts, False),
+        ],
+        out_specs=(
+            tall_at(fc_form, 0, parts), matrix_at(fc_form, 0), matrix_at(proj_form, 0, False),
+            by_part(1), whole((6, width)), token, token,
+        ),
+        out_shape=(
+            fc_form,
+            fc_form,
+            proj_form,
+            shape(parts, 1, width, F32),
+            shape(6, width, F32),
+            shape(tokens, width, F32),
+            shape(tokens, width, BF16),
+        ),
+        scratch_shapes=[pltpu.VMEM((tokens, width), BF16), pltpu.VMEM((tokens, width), F32)],
+        compiler_params=params_of(56),
+        cost_estimate=pl.CostEstimate(
+            flops=(4 + 8 * parts) * tokens * width**2,
+            transcendentals=parts * tokens * width,
+            bytes_accessed=(20 + 6 * parts) * tokens * width + 8 * parts * width**2,
+        ),
+    )(
+        grad, mlp_out, modulation, weights, weights, hidden, active, normed, middle, attn_out,
+        mixed, weights,
+    )
+
+
+def project_back_kernel(
+    gq_ref, own_ref, back_ref, normed_ref, weight_ref, stream_ref, mod_ref, middle_ref,
+    weight_g_ref, sums_ref, bias_ref, grad_ref, total_ref,
+):
+    part = pl.program_id(0)
+
+    def step(grad, first):
+        put_square(weight_g_ref, tn(normed_ref[...], grad))
+        bias_ref[0] = column_sum(grad.astype(F32))
+        product = nt(grad, square(weight_ref))
+        total_ref[...] = product if first else total_ref[...] + product
+
+    @pl.when(part == 0)
+    def _():
+        step(gq_ref[...], True)
+
+    @pl.when(part > 0)
+    def _():
+        step((own_ref[0] + back_ref[0].astype(F32)).astype(BF16), False)
+
+    @pl.when(part == 2)
+    def _():
+        grad_normed = total_ref[...]
+        normal, scale = normalize(stream_ref[...])
+        sums_ref[0:1] = column_sum(grad_normed)
+        sums_ref[1:2] = column_sum(grad_normed * normal)
+        grad_ref[...] = middle_ref[...] + norm_back(grad_normed, normal, scale, mod_ref[1:2])
+
+
+def project_back(grad_q, grad_own, returned, normed, weights, at, stream, modulation, grad_middle):
+    tokens, width = stream.shape
+    token = whole((tokens, width))
+    form = jax.ShapeDtypeStruct((weights.shape[0], 3) + weights.shape[2:], BF16)
+    kv = pl.BlockSpec((1, tokens, width), lambda part: (jnp.maximum(part - 1, 0), 0, 0))
+    return pl.pallas_call(
+        project_back_kernel,
+        grid=(3,),
+        in_specs=[
+            token, kv, kv, token, matrix_at(weights, at), token, whole((6, width)), token,
+        ],
+        out_specs=(
+            matrix_at(form, 0),
+            whole((2, width)),
+            pl.BlockSpec((1, 1, width), lambda part: (part, 0, 0)),
+            token,
+        ),
+        out_shape=(
+            form,
+            jax.ShapeDtypeStruct((2, width), F32),
+            jax.ShapeDtypeStruct((3, 1, width), F32),
+            jax.ShapeDtypeStruct((tokens, width), F32),
+        ),
+        scratch_shapes=[pltpu.VMEM((tokens, width), F32)],
+        compiler_params=params_of(),
+        cost_estimate=pl.CostEstimate(
+            flops=12 * tokens * width**2,
+            transcendentals=0,
+            bytes_accessed=24 * tokens * width + 12 * width**2,
+        ),
+    )(grad_q, grad_own, returned, normed, weights, stream, modulation, grad_middle)
+
+
+def layer_forward(stream, modulation, biases, moves, weights_of):
     qkv_b, proj_b, fc1_b, fc2_b = biases
-    width = stream.shape[-1]
-    shift_attn, factor_attn, gate_attn, shift_mlp, factor_mlp, gate_mlp = modulation
-    normal, scale = normalize(stream)
-    normed = (normal * (1.0 + factor_attn) + shift_attn).astype(BF16)
-    queries, keys, values = [
-        (dot(normed, qkv_w[part], (1,), (0,)) + qkv_b[part]).astype(BF16) for part in range(3)
-    ]
-    own_kv = jnp.stack([keys, values])
+    qkv_w, at = weights_of("qkv")
+    normed, queries, own_kv = project(stream, modulation, qkv_w, at, qkv_b)
+    own_kv = moves.tick(own_kv)
     other_kv = swap_pairs(own_kv, "rep")
     mixed, log_total = attend(queries, own_kv, other_kv)
-    attn_out = dot(mixed, proj_w, (1,), (0,)) + proj_b
-    middle = stream + gate_attn * attn_out
-    normal_mlp, scale_mlp = normalize(middle)
-    normed_mlp = (normal_mlp * (1.0 + factor_mlp) + shift_mlp).astype(BF16)
-    hidden = jnp.concatenate(
-        [dot(normed_mlp, fc1_w[part], (1,), (0,)) for part in range(fc1_w.shape[0])], axis=-1
-    )
-    hidden = hidden + fc1_b
-    activated = jax.nn.gelu(hidden, approximate=True).astype(BF16)
-    mlp_out = dot(activated, fc2_w, (1,), (0,)) + fc2_b
-    result = middle + gate_mlp * mlp_out
+    mixed = moves.tick(mixed)
+    rest_w, _ = weights_of("rest")
+    attn_out, middle, normed_mlp, hidden, active, mlp_out, result = mlp(
+        mixed, stream, modulation, rest_w, proj_b, fc1_b, fc2_b
+    )
+    result = moves.tick(result)
     return result, (
-        stream, normed, queries, own_kv, other_kv, mixed, log_total, attn_out, middle, normed_mlp, hidden,
-        activated, mlp_out,
-    )
-
-
-def token_sum(values):
-    return jnp.sum(values.astype(F32), axis=0)
-
-
-def by_shard(matrix, shards):
-    return matrix.reshape(shards, matrix.shape[0] // shards, matrix.shape[1])
-
-
-def layer_backward(layer, grad_out, modulation, weights, kept, shards, background):
-    qkv_w, proj_w, fc1_w, fc2_w = weights
+        stream, normed, queries, own_kv, other_kv, mixed, log_total, attn_out, middle, normed_mlp,
+        hidden, active, mlp_out, qkv_w, at, rest_w,
+    )
+
+
+def layer_backward(grad_out, modulation, kept, shards, moves, send_rest, send_qkv):
     (
-        stream, normed, queries, own_kv, other_kv, mixed, log_total, attn_out, middle, normed_mlp, hidden,
-        activated, mlp_out,
+        stream, normed, queries, own_kv, other_kv, mixed, log_total, attn_out, middle, normed_mlp,
+        hidden, active, mlp_out, qkv_w, at, rest_w,
     ) = kept
     width = stream.shape[-1]
-    shift_attn, factor_attn, gate_attn, shift_mlp, factor_mlp, gate_mlp = modulation
-    grad_gate_mlp = token_sum(grad_out * mlp_out)
-    grad_mlp = (grad_out * gate_mlp).astype(BF16)
-    grad_fc2_w = dot(activated, grad_mlp, (0,), (0,)).astype(BF16)
-    grad_fc2_b = token_sum(grad_mlp)
-    grad_mlp = background.tick(grad_mlp)
-    grad_activated = dot(grad_mlp, fc2_w, (1,), (1,))
-    _, gelu_pull = jax.vjp(lambda v: jax.nn.gelu(v, approximate=True), hidden)
-    grad_hidden = gelu_pull(grad_activated)[0].astype(BF16)
-    parts = [
-        grad_hidden[:, part * width : (part + 1) * width] for part in range(fc1_w.shape[0])
-    ]
-    parts = background.tick(parts)
-    grad_fc1_w = [dot(normed_mlp, part, (0,), (0,)).astype(BF16) for part in parts]
-    grad_fc1_b = token_sum(grad_hidden)
-    grad_normed = sum(dot(part, fc1_w[at], (1,), (1,)) for at, part in enumerate(parts))
-    fc2_grads = grad_fc2_w.reshape(shards, -1, width // shards, width)
-    fc1_grads = jnp.stack([by_shard(part, shards) for part in grad_fc1_w], axis=1)
-    grad_normed = background.tick(grad_normed)
-    background.start(("mlp", layer), jnp.concatenate([fc1_grads, fc2_grads], axis=1))
-    normal, scale = normalize(middle)
-    grad_shift_mlp = token_sum(grad_normed)
-    grad_factor_mlp = token_sum(grad_normed * normal)
-    grad_middle = grad_out + norm_back(grad_normed, normal, scale, factor_mlp)
-    grad_gate_attn = token_sum(grad_middle * attn_out)
-    grad_attn = (grad_middle * gate_attn).astype(BF16)
-    grad_proj_w = dot(mixed, grad_attn, (0,), (0,)).astype(BF16)
-    grad_proj_b = token_sum(grad_attn)
-    grad_attn = background.tick(grad_attn)
-    grad_mixed = dot(grad_attn, proj_w, (1,), (1,)).astype(BF16)
-    grad_mixed = background.tick(grad_mixed)
+    fc2_g, fc1_g, proj_g, fc1_b, sums, grad_middle, grad_mixed = mlp_back(
+        grad_out, mlp_out, modulation, rest_w, hidden, active, normed_mlp, middle, attn_out, mixed
+    )
+    grad_mixed = moves.tick(grad_mixed)
+    send_rest(fc1_g, fc2_g, proj_g)
     grad_q, grad_own, grad_other = attend_back(
         queries, own_kv, other_kv, grad_mixed, mixed, log_total
     )
-    grad_own = background.tick(grad_own)
-    grad_kv = (grad_own + swap_pairs(grad_other, "rep").astype(F32)).astype(BF16)
-    grad_projected = [grad_q, grad_kv[0], grad_kv[1]]
-    grad_qkv_w = [dot(normed, part, (0,), (0,)).astype(BF16) for part in grad_projected]
-    grad_qkv_w = background.tick(grad_qkv_w)
-    background.start(
-        ("attn", layer),
-        jnp.stack([by_shard(part, shards) for part in grad_qkv_w + [grad_proj_w]], axis=1),
-    )
-    grad_qv_b = jnp.concatenate([token_sum(grad_projected[0]), token_sum(grad_projected[2])])
-    grad_normed = sum(dot(part, qkv_w[at], (1,), (1,)) for at, part in enumerate(grad_projected))
-    normal, scale = normalize(stream)
-    grad_shift_attn = token_sum(grad_normed)
-    grad_factor_attn = token_sum(grad_normed * normal)
-    grad_normed = background.tick(grad_normed)
-    grad_stream = grad_middle + norm_back(grad_normed, normal, scale, factor_attn)
+    grad_other = moves.tick(grad_other)
+    returned = swap_pairs(grad_other, "rep")
+    qkv_g, attn_sums, qkv_b, grad_stream = project_back(
+        grad_q, grad_own, returned, normed, qkv_w, at, stream, modulation, grad_middle
+    )
+    grad_stream = moves.tick(grad_stream)
+    send_qkv(qkv_g, proj_g)
     grad_modulation = jnp.concatenate(
-        [
-            grad_shift_attn,
-            grad_factor_attn,
-            grad_gate_attn,
-            grad_shift_mlp,
-            grad_factor_mlp,
-            grad_gate_mlp,
-        ]
-    )
+        [attn_sums[0], attn_sums[1], sums[3], sums[0], sums[1], sums[2]]
+    )
+    query_value = jnp.concatenate([qkv_b[0, 0], qkv_b[2, 0]])
     bias_grads = [
-        part.reshape(shards, -1) for part in (grad_qv_b, grad_proj_b, grad_fc1_b, grad_fc2_b)
+        part.reshape(shards, -1) for part in (query_value, sums[5], fc1_b.reshape(-1), sums[4])
     ]
     return grad_stream, grad_modulation, jnp.concatenate(bias_grads, axis=1)
 
@@ -600,18 +888,28 @@
     )
     stream = swap_layout(latents[0]).astype(F32)
 
+    rings = ring_fits(own_rows)
     packs = []
     for layer in range(LAYERS):
         fc2_piece = fc2_weight[layer].reshape(ff_parts, own_rows, width)
-        rest = jnp.concatenate(
-            [proj_weight[layer][None], columns(fc1_weight[layer], width), fc2_piece]
+        packs.append(
+            (
+                jnp.concatenate(
+                    [columns(fc1_weight[layer], width), fc2_piece, proj_weight[layer][None]]
+                ),
+                columns(qkv_weight[layer], width),
+            )
         )
-        packs.append((columns(qkv_weight[layer], width), rest))
-    gathered = []
-    for layer in range(LAYERS):
-        (qkv_w,) = gather(packs[layer][0], 0)
-        rest_w, fc2_w = gather(packs[layer][1], ff_parts)
-        gathered.append((qkv_w, rest_w[0], rest_w[1:], fc2_w.reshape(ff_parts * width, width)))
+    tall = (ff_parts, ff_parts)
+    moves = Moves([("qkv", packs[0][1], (0, 0)), ("rest", packs[0][0], tall)])
+    later = jnp.concatenate(packs[1])
+    later = gather_wide(later) if rings else gather_plain(later, tall)
+
+    def first_weights(name):
+        return moves.need(name), 0
+
+    def later_weights(name):
+        return later, 2 * ff_parts + 1
 
     small = jnp.concatenate([ada_bias, qv_bias, proj_bias, fc1_bias, fc2_bias], axis=1)
     small = cube_gather(small, ("shard",)).astype(F32)
@@ -622,8 +920,15 @@
     for layer in range(LAYERS):
         full = [small[:, layer, ends[at] : ends[at + 1]].reshape(-1) for at in range(5)]
         ada_b.append(full[0])
-        qkv_b = [full[1][:width], jnp.zeros((width,), F32), full[1][width:]]
-        biases.append((qkv_b, full[2], full[3], full[4]))
+        qkv_b = jnp.concatenate([full[1][:width], jnp.zeros((width,), F32), full[1][width:]])
+        biases.append(
+            (
+                qkv_b.reshape(3, 1, width),
+                full[2][None],
+                full[3].reshape(ff_parts, 1, width),
+                full[4][None],
+            )
+        )
 
     mine = lax.dynamic_slice(cond_rows, (seq * shards, 0), (shards, own_rows))
     partial = jnp.concatenate(
@@ -631,26 +936,64 @@
     )
     modulations = cube_scatter(partial, "shard")
     modulations = [
-        jnp.split((modulations.reshape(LAYERS, -1)[layer] + ada_b[layer])[None, :], 6, axis=1)
+        (modulations.reshape(LAYERS, -1)[layer] + ada_b[layer]).reshape(6, width)
         for layer in range(LAYERS)
     ]
 
     kept = []
     for layer in range(LAYERS):
-        stream, layer_kept = layer_forward(stream, modulations[layer], gathered[layer], biases[layer])
+        stream, layer_kept = layer_forward(
+            stream,
+            modulations[layer],
+            biases[layer],
+            moves,
+            later_weights if layer else first_weights,
+        )
         kept.append(layer_kept)
+    moves = Moves()
     activations = swap_layout((stream * live).astype(BF16)).astype(F32)
     grad_stream = swap_layout(cotangent[0]).astype(F32) * live
 
-    weight_grads = [None] * LAYERS
-    background = Background()
+    shares = []
+    done = {}
+
+    def flat(part):
+        return part.reshape(part.shape[1], shards, own_rows, width).transpose(1, 0, 2, 3)
+
+    def send_rest(layer, fc1_g, fc2_g, proj_g):
+        if not rings:
+            done["rest", layer] = scatter_plain(
+                jnp.concatenate(
+                    [flat(fc1_g), fc2_g.reshape(shards, ff_parts, own_rows, width), flat(proj_g)],
+                    axis=1,
+                )
+            )
+        elif layer:
+            shares.extend([scatter_wide(fc1_g), scatter_wide(fc2_g)])
+        else:
+            moves.start("rest", [fc1_g, fc2_g, proj_g])
+
+    def send_qkv(layer, qkv_g, proj_g):
+        if not rings:
+            done["qkv", layer] = scatter_plain(flat(qkv_g))
+        elif layer:
+            shares.append(scatter_wide(jnp.concatenate([proj_g, qkv_g], axis=1)))
+        else:
+            moves.start("qkv", [qkv_g])
+
     bias_grads = [None] * LAYERS
     ada_w_grads = [None] * LAYERS
     ada_b_grads = [None] * LAYERS
     grad_cond = 0.0
     for layer in reversed(range(LAYERS)):
         grad_stream, grad_mod, bias_grads[layer] = layer_backward(
-            layer, grad_stream, modulations[layer], gathered[layer], kept[layer], shards, background
+            grad_stream,
+            modulations[layer],
+            kept[layer],
+            shards,
+            moves,
+            functools.partial(send_rest, layer),
+            functools.partial(send_qkv, layer),
         )
         grad_mod = (grad_mod + swap_pairs(grad_mod, "rep")).astype(BF16)
         all_mod = cube_gather(grad_mod, ("seq", "shard"))
@@ -658,7 +1001,7 @@
         own_mod = lax.dynamic_slice(
             all_mod, (0, shard * ada_bias.shape[1]), (all_mod.shape[0], ada_bias.shape[1])
         )
-        ada_b_grads[layer] = token_sum(own_mod)
+        ada_b_grads[layer] = jnp.sum(own_mod.astype(F32), axis=0)
         rep_mod = lax.dynamic_slice(all_mod, (rep * shards, 0), (shards, all_mod.shape[1]))
         grad_cond = grad_cond + dot(rep_mod, ada_weight[layer], (1,), (1,))
 
@@ -676,14 +1019,23 @@
     qv_b, proj_b, fc1_b, fc2_b = [
         bias_total[:, ends[at] - ends[1] : ends[at + 1] - ends[1]] for at in range(1, 5)
     ]
-    done = background.finish()
+    if rings:
+        moved = moves.finish()
+        done["qkv", 0], done["rest", 0] = moved["qkv"], moved["rest"]
+        spread = cube_gather(jnp.stack([share.reshape(own_rows, width) for share in shares]), ("rep", "seq"))
+        spread = spread.astype(F32)
+        done["qkv", 1] = spread[1:, 2]
+        done["rest", 1] = jnp.concatenate([spread[:, 0], spread[:, 1], spread[:1, 2]])
+    weight_grads = []
     for layer in range(LAYERS):
-        attn_grads, mlp_grads = done["attn", layer], done["mlp", layer]
-        weight_grads[layer] = (
-            uncolumns(attn_grads[:3]),
-            attn_grads[3],
-            uncolumns(mlp_grads[:ff_parts]),
-            mlp_grads[ff_parts:].reshape(ff_parts * own_rows, width),
+        qkv_grads, rest_grads = done["qkv", layer], done["rest", layer]
+        weight_grads.append(
+            (
+                uncolumns(qkv_grads),
+                rest_grads[2 * ff_parts],
+                uncolumns(rest_grads[:ff_parts]),
+                rest_grads[ff_parts : 2 * ff_parts].reshape(ff_parts * own_rows, width),
+            )
         )
     qkv_g, proj_g, fc1_g, fc2_g = [
         jnp.stack([weight_grads[layer][at] for layer in range(LAYERS)]) for at in range(4)

time: 855 us -> 860 us (level)
  waiting for transfers between devices: 237 us -> 355 us
  matrix products: 109 us -> 7.5 us
  Pallas kernels: 84.3 us -> 185 us
  other arithmetic: 110 us -> 53 us
  local copies, waits for them, and re-layouts: 125 us -> 91.2 us
  starting transfers between devices: 154 us -> 124 us
  between operations: 23.1 us -> 34.6 us
    reduce_scatter x0 -> x3, waiting for transfers between devices: none -> 181 us  [scatter_wide(): lax.psum_scatter(grads.reshape(-1, grads.shape[-1]), ('shard', 'rep', 'se...]
    dot_general x61 -> x7, matrix products: 109 us -> 7.5 us  [dot(): lax.dot_general(left, right, ((left_dims, right_dims), ((), ())), preferr...]
    pallas_call x4 -> x10, Pallas kernels: 12.2 us -> 114 us  [the longest x2 48.6 us: mlp_back(): pl.pallas_call(mlp_back_kernel, grid=(parts,), in_specs=[token, token, wh...]
    ppermute x64 -> x32, waiting for transfers between devices: 121 us -> 84.1 us  [ring_step(): lax.ppermute(value, 'shard', [(order[at], order[(at + step) % size]) for...]
    ppermute x64 -> x32, starting transfers between devices: 70.1 us -> 37.3 us  [ring_step(): lax.ppermute(value, 'shard', [(order[at], order[(at + step) % size]) for...]
    convert_element_type x34 -> x20, other arithmetic: 40.2 us -> 19.4 us  [add(): return (left.astype(F32) + right.astype(F32)).astype(BF16)]
    ppermute x84 -> x54, waiting for transfers between devices: 59.8 us -> 39.6 us  [swap_pairs(): return lax.ppermute(value, axis, [(0, 1), (1, 0)])]
    unnamed x550 -> x296, local copies, waits for them, and re-layouts: 58.8 us -> 44.7 us
  transfers between devices with their start and end apart: 176 -> 120, of which waited for: 74 -> 44; matrix products, arithmetic and copies ran while one was open for 31% -> 12% of each run, Pallas kernels for 10% -> 15%
where the time goes in v3:
time: 860 us; the launch traced here: 850 us
  waiting for transfers between devices  355 us (41%)
  Pallas kernels  185 us (22%)
  starting transfers between devices  124 us (14%)
  local copies, waits for them, and re-layouts  91.2 us (11%)
  other arithmetic  53 us (6%)
  between operations  34.6 us (4%)
    reduce_scatter x3, waiting for transfers between devices, scatter_wide(): lax.psum_scatter(grads.reshape(-1, grads.shape[-1]), ('shard', 'rep', 'se...  181 us
    ppermute x32, waiting for transfers between devices, ring_step(): lax.ppermute(value, 'shard', [(order[at], order[(at + step) % size]) for...  84.1 us
    ppermute x26, waiting for transfers between devices, cube_pairs(): lax.ppermute(value, axis, [(at, at ^ bit) for at in range(lax.axis_size(a...  48.9 us
    pallas_call x2, Pallas kernels, mlp_back(): pl.pallas_call(mlp_back_kernel, grid=(parts,), in_specs=[token, token, wh...  48.6 us
    pallas_call x2, Pallas kernels, attend_back(): pl.pallas_call(functools.partial(attend_back_kernel, width // HEADS), gri...  45.6 us
    unnamed x296, local copies, waits for them, and re-layouts  44.7 us
    ppermute x54, starting transfers between devices, swap_pairs(): return lax.ppermute(value, axis, [(0, 1), (1, 0)])  43.9 us
    ppermute x54, waiting for transfers between devices, swap_pairs(): return lax.ppermute(value, axis, [(0, 1), (1, 0)])  39.6 us
  transfers between devices with their start and end apart: 120, of which 44 were waited for; matrix products, arithmetic and copies ran while one was open for 12% of the time, Pallas kernels for 15%

profile of v3, /device:TPU:0, one launch (start us, length us, event | category | flops | bytes accessed | tf_op | source)
XLA Modules:
  0.0 850.4 jit_solution(2864086891618527838)
XLA Ops:
  18.2 3.0 collective-permute-start.11
  31.7 3.1 collective-permute-start.3
  55.7 4.2 collective-permute-done.13.refs_3_
  59.9 6.1 collective-permute-start.15
  68.3 4.0 collective-permute-done.15.refs_5_
  72.3 4.8 collective-permute-start.17
  77.1 3.0 collective-permute-done.16.refs_6_
  86.2 3.8 collective-permute-done.21.refs_10_
  96.3 21.8 %collective-permute-done.7 = f32[1,9216]{1,0:T(1,128)S(1)} collective-permute-done((f32[1,9216]{1,0:T(1,128)S(1)}, f32[1,9216]{1,0:T(1,128)S(1)}, u32[]{:S(2)}, u32[]{:S(2)}) %collective-permute-start.7) | collective-permute-done | bytes 36896 | tf_op jit(solution)/shard_map/ppermute | solution.py:28
  124.4 16.9 %collective-permute-done.37.refs_2_ = bf16[9,32,768]{2,1,0:T(8,128)(2,1)} collective-permute-done((bf16[9,32,768]{2,1,0:T(8,128)(2,1)S(1)}, bf16[9,32,768]{2,1,0:T(8,128)(2,1)}, u32[]{:S(2)}, u32[]{:S(2)}) %collective-permute-start.37) | collective-permute-done | bytes 442400 | tf_op jit(solution)/shard_map/ppermute | solution.py:65
  151.1 4.2 collective-permute-done.38.refs_4_
  166.4 4.8 shard_map.328
  175.6 5.3 collective-permute-done.46
  181.3 12.4 %shard_map.329 = (bf16[512,768]{1,0:T(8,128)(2,1)S(1)}, f32[6,2,512]{2,1,0:T(2,128)S(1)}) custom-call(bf16[512,768]{1,0:T(8,128)(2,1)S(1)} %get-tuple-element.91.q_ref, bf16[2,512,768]{2,1,0:T(8,128)(2,1)S(1)} %get-tuple-element.94.own_ref, bf16[2,512,768]{2,1,0:T(8,128)(2,1)S(1)} %collective-permute-done.45.other_ref), custom_call_target="tpu_custom_call" | custom-call | flops 6442450944 | bytes 4718592 | tf_op jit(solution)/shard_map/pallas_call | solution.py:402
  203.1 4.2 collective-permute-done.52.refs_11_
  216.0 3.2 shard_map.330.proj_ref.fc1_ref.fc2_ref
  219.3 4.0 copy-done.2
  223.3 14.4 %shard_map.331 = (f32[512,768]{1,0:T(8,128)S(1)}, f32[512,768]{1,0:T(8,128)S(1)}, bf16[512,768]{1,0:T(8,128)(2,1)S(1)}, f32[4,512,768]{2,1,0:T(8,128)}, bf16[4,5...) custom-call(bf16[512,768]{1,0:T(8,128)(2,1)S(1)} %get-tuple-element.99.mixed_ref, ...), custom_call_target="tpu_custom_call" | custom-call | flops 5435817984 | bytes 17301504 | tf_op jit(solution)/shard_map/pallas_call | solution.py:611
  242.3 5.7 shard_map.332
  253.5 13.5 %shard_map.333 = (bf16[512,768]{1,0:T(8,128)(2,1)S(1)}, f32[6,2,512]{2,1,0:T(2,128)S(1)}) custom-call(bf16[512,768]{1,0:T(8,128)(2,1)S(1)} %get-tuple-element.110.q_ref, bf16[2,512,768]{2,1,0:T(8,128)(2,1)} %get-tuple-element.111.own_ref, bf16[2,512,768]{2,1,0:T(8,128)(2,1)} %collective-permute-done.58.other_ref), custom_call_target="tpu_custom_call" | custom-call | flops 6442450944 | bytes 4718592 | tf_op jit(solution)/shard_map/pallas_call | solution.py:402
  267.0 14.6 %shard_map.334 = (f32[512,768]{1,0:T(8,128)S(1)}, f32[512,768]{1,0:T(8,128)S(1)}, bf16[512,768]{1,0:T(8,128)(2,1)S(1)}, f32[4,512,768]{2,1,0:T(8,128)}, bf16[4,5...) custom-call(bf16[512,768]{1,0:T(8,128)(2,1)S(1)} %get-tuple-element.112.mixed_ref, ...), custom_call_target="tpu_custom_call" | custom-call | flops 5435817984 | bytes 17301504 | tf_op jit(solution)/shard_map/pallas_call | solution.py:611
  284.9 24.3 %shard_map.335 = (bf16[8,4,96,768]{3,2,1,0:T(8,128)(2,1)}, bf16[8,4,96,768]{3,2,1,0:T(8,128)(2,1)}, bf16[8,1,96,768]{3,2,1,0:T(8,128)(2,1)}, f32[4,1,768]{2,1,0:...) custom-call(f32[512,768]{1,0:T(8,128)} %convert_multiply_fusion.grad_ref, ...), custom_call_target="tpu_custom_call" | custom-call | flops 10871635968 | bytes 36175872 | tf_op jit(solution)/shard_map/pallas_call | solution.py:698
  311.8 23.1 %shard_map.336 = (bf16[512,768]{1,0:T(8,128)(2,1)S(1)}, f32[2,512,768]{2,1,0:T(8,128)S(1)}, bf16[2,512,768]{2,1,0:T(8,128)(2,1)}) custom-call(bf16[512,768]{1,0:T(8,128)(2,1)S(1)} %copy-done.78, bf16[2,512,768]{2,1,0:T(8,128)(2,1)} %get-tuple-element.111.own_ref, bf16[2,512,768]{2,1,0:T(8,128)(2,1)} %collective-permute-done.58.other_ref, ...), custom_call_target="tpu_custom_call" | custom-call | flops 16106127360 | bytes 9437184 | tf_op jit(solution)/shard_map/pallas_call | solution.py:456
  336.6 10.9 %collective-permute-start.61 = (bf16[2,512,768]{2,1,0:T(8,128)(2,1)}, bf16[2,512,768]{2,1,0:T(8,128)(2,1)S(1)}, u32[]{:S(2)}, u32[]{:S(2)}) collective-permute-start(bf16[2,512,768]{2,1,0:T(8,128)(2,1)} %get-tuple-element.124), channel_id=1, source_target_pairs={{0,16},{16,0},{1,17},{17,1},{2,18},{18,2},{3,19},{19,3},{4,20},{20... | collective-permute-start | bytes 4718600 | tf_op jit(solution)/shard_map/ppermute | solution.py:19
  367.8 9.9 %shard_map.337 = (bf16[8,3,96,768]{3,2,1,0:T(8,128)(2,1)}, f32[2,768]{1,0:T(2,128)S(1)}, f32[3,1,768]{2,1,0:T(1,128)S(1)}, f32[512,768]{1,0:T(8,128)S(1)}) custom-call(bf16[512,768]{1,0:T(8,128)(2,1)S(1)} %get-tuple-element.122.gq_ref, f32[2,512,768]{2,1,0:T(8,128)} %copy-done.8, bf16[2,512,768]{2,1,0:T(8,128)(2,1)S(1)} %collective-permute-done.61.back_ref, ...), custom_call_target="tpu_custom_call" | custom-call | flops 3623878656 | bytes 16515072 | tf_op jit(solution)/shard_map/pallas_call | solution.py:766
  378.9 24.3 %shard_map.338 = (bf16[8,4,96,768]{3,2,1,0:T(8,128)(2,1)}, bf16[8,4,96,768]{3,2,1,0:T(8,128)(2,1)}, bf16[8,1,96,768]{3,2,1,0:T(8,128)(2,1)}, f32[4,1,768]{2,1,0:...) custom-call(f32[512,768]{1,0:T(8,128)} %copy-done.17, ...), custom_call_target="tpu_custom_call" | custom-call | flops 10871635968 | bytes 36175872 | tf_op jit(solution)/shard_map/pallas_call | solution.py:698
  405.6 4.3 constant_dynamic-slice_fusion.19
  422.5 2.9 collective-permute-done.67
  427.5 22.5 %shard_map.339 = (bf16[512,768]{1,0:T(8,128)(2,1)S(1)}, f32[2,512,768]{2,1,0:T(8,128)S(1)}, bf16[2,512,768]{2,1,0:T(8,128)(2,1)S(1)}) custom-call(bf16[512,768]{1,0:T(8,128)(2,1)S(1)} %copy-done.86, bf16[2,512,768]{2,1,0:T(8,128)(2,1)S(1)} %copy-done.73, bf16[2,512,768]{2,1,0:T(8,128)(2,1)S(1)} %copy-done.75, bf16[512,768]{1,0:T(8,128)(2,1)S(1)} %copy-done.76, ...), custom_call_target="tpu_custom_call" | custom-call | flops 16106127360 | bytes 9437184 | tf_op jit(solution)/shard_map/pallas_call | solution.py:456
  455.7 3.2 collective-permute-start.70
  466.0 7.8 add_convert_fusion
  473.8 3.2 constant_dynamic-slice_fusion.1
  485.9 69.8 %reduce-scatter.4.cloned.1.call-done = bf16[96,768]{1,0:T(8,128)(2,1)} async-done(((bf16[3072,768]{1,0:T(8,128)(2,1)}), bf16[96,768]{1,0:T(8,128)(2,1)}) %reduce-scatter.4.cloned.1.call-update) | async-done | bytes 147472 | tf_op jit(solution)/shard_map/reduce_scatter | solution.py:320
  555.7 111.5 %reduce-scatter.8.cloned.1.call-done = bf16[96,768]{1,0:T(8,128)(2,1)} async-done(((bf16[3072,768]{1,0:T(8,128)(2,1)}), bf16[96,768]{1,0:T(8,128)(2,1)}) %reduce-scatter.8.cloned.1.call-update) | async-done | bytes 147472 | tf_op jit(solution)/shard_map/reduce_scatter | solution.py:320
  674.0 7.0 collective-permute-done.96
  682.1 9.9 %shard_map.340 = (bf16[8,3,96,768]{3,2,1,0:T(8,128)(2,1)}, f32[2,768]{1,0:T(2,128)S(1)}, f32[3,1,768]{2,1,0:T(1,128)S(1)}, f32[512,768]{1,0:T(8,128)S(1)}) custom-call(bf16[512,768]{1,0:T(8,128)(2,1)S(1)} %copy-done.84, f32[2,512,768]{2,1,0:T(8,128)} %copy-done.80, bf16[2,512,768]{2,1,0:T(8,128)(2,1)S(1)} %collective-permute-done.63.back_ref, ...), custom_call_target="tpu_custom_call" | custom-call | flops 3623878656 | bytes 16515072 | tf_op jit(solution)/shard_map/pallas_call | solution.py:766
  733.8 5.1 collective-permute-done.107
  754.1 9.4 %collective-permute-done.111 = bf16[9,32,768]{2,1,0:T(8,128)(2,1)S(1)} collective-permute-done((bf16[9,32,768]{2,1,0:T(8,128)(2,1)S(1)}, bf16[9,32,768]{2,1,0:T(8,128)(2,1)S(1)}, u32[]{:S(2)}, u32[]{:S(2)}) %collective-permute-start.111) | collective-permute-done | bytes 442400 | tf_op jit(solution)/shard_map/ppermute | solution.py:65
  767.0 5.1 collective-permute-done.84
  772.1 5.0 collective-permute-done.85
  777.4 4.9 collective-permute-done.83
  783.0 3.7 collective-permute-done.86
  786.8 5.0 collective-permute-done.82
  792.4 4.5 collective-permute-done.87
  800.4 2.9 collective-permute-done.88
  804.4 11.3 %collective-permute-done.91 = bf16[3,32,768]{2,1,0:T(8,128)(2,1)S(1)} collective-permute-done((bf16[3,32,768]{2,1,0:T(8,128)(2,1)S(1)}, bf16[3,32,768]{2,1,0:T(8,128)(2,1)S(1)}, u32[]{:S(2)}, u32[]{:S(2)}) %collective-permute-start.91) | collective-permute-done | bytes 147488 | tf_op jit(solution)/shard_map/ppermute | solution.py:65
  824.6 3.3 collective-permute-done.93
  830.2 3.1 collective-permute-done.94
  (739 shorter events, 260.5 us)
Async XLA Ops:
  7.2 233.7 %all-gather.2.cloned.1.call-start = ((), (), s32[]{:S(2)}) async-start(), calls=%async_computation.3 | async-start | bytes 14598144 | tf_op jit(solution)/shard_map/all_gather | solution.py:163
  17.2 468.6 %reduce-scatter.6.cloned.1.call-start = ((), (), s32[]{:S(2)}) async-start(), calls=%async_computation.5 | async-start | bytes 4866048 | tf_op jit(solution)/shard_map/reduce_scatter | solution.py:320
  18.2 30.2 %collective-permute-start.11 = (bf16[3,32,768]{2,1,0:T(8,128)(2,1)}, bf16[3,32,768]{2,1,0:T(8,128)(2,1)}, u32[]{:S(2)}, u32[]{:S(2)}) collective-permute-start(bf16[3,32,768]{2,1,0:T(8,128)(2,1)} %constant_dynamic-slice_fusion.26), channel_id=1, source_target_pairs={{0,4},{4,8},{8,12},{12,14},{14,10},{10,6},{6,2},{2,0},{1,5},{5,9},... | collective-permute-start | bytes 442376 | tf_op jit(solution)/shard_map/ppermute | solution.py:65
  21.2 26.2 %collective-permute-start.12 = (bf16[3,32,768]{2,1,0:T(8,128)(2,1)}, bf16[3,32,768]{2,1,0:T(8,128)(2,1)}, u32[]{:S(2)}, u32[]{:S(2)}) collective-permute-start(bf16[3,32,768]{2,1,0:T(8,128)(2,1)} %constant_dynamic-slice_fusion.26), channel_id=1, source_target_pairs={{0,2},{4,0},{8,4},{12,8},{14,12},{10,14},{6,10},{2,6},{1,3},{5,1},... | collective-permute-start | bytes 442376 | tf_op jit(solution)/shard_map/ppermute | solution.py:65
  43.2 12.5 %collective-permute-start.5 = (f32[4,9216]{1,0:T(4,128)S(1)}, f32[4,9216]{1,0:T(4,128)S(1)}, u32[]{:S(2)}, u32[]{:S(2)}) collective-permute-start(f32[4,9216]{1,0:T(4,128)S(1)} %broadcast_select_fusion.5), channel_id=1, source_target_pairs={{0,8},{2,10},{4,12},{6,14},{8,0},{10,2},{12,4},{14,6},{1,9},{3,11}... | collective-permute-start | bytes 442376 | tf_op jit(solution)/shard_map/ppermute | solution.py:28
  49.2 71.4 %collective-permute-start.19 = (bf16[2,3,16,768]{3,2,1,0:T(8,128)(2,1)S(1)}, bf16[2,3,16,768]{3,2,1,0:T(8,128)(2,1)S(1)}, u32[]{:S(2)}, u32[]{:S(2)}) collective-permute-start(bf16[2,3,16,768]{3,2,1,0:T(8,128)(2,1)S(1)} %pad_maximum_fusion.19), channel_id=1, source_target_pairs={{0,1},{1,0},{2,3},{3,2},{4,5},{5,4},{6,7},{7,6},{8,9},{9,8},{10,11... | collective-permute-start | bytes 442376 | tf_op jit(solution)/shard_map/ppermute | solution.py:19
  52.3 16.1 %collective-permute-start.14 = (bf16[3,32,768]{2,1,0:T(8,128)(2,1)}, bf16[3,32,768]{2,1,0:T(8,128)(2,1)S(1)}, u32[]{:S(2)}, u32[]{:S(2)}) collective-permute-start(bf16[3,32,768]{2,1,0:T(8,128)(2,1)} %collective-permute-done.12.refs_2_), channel_id=1, source_target_pairs={{0,2},{4,0},{8,4},{12,8},{14,12},{10,14},{6,10},{2,6},{1,3},{5,1},... | collective-permute-start | bytes 442376 | tf_op jit(solution)/shard_map/ppermute | solution.py:65
  52.8 67.8 %collective-permute-start.25 = (bf16[3,32,768]{2,1,0:T(8,128)(2,1)}, bf16[3,32,768]{2,1,0:T(8,128)(2,1)S(1)}, u32[]{:S(2)}, u32[]{:S(2)}) collective-permute-start(bf16[3,32,768]{2,1,0:T(8,128)(2,1)} %collective-permute-done.11.refs_1_), channel_id=1, source_target_pairs={{0,16},{16,0},{1,17},{17,1},{2,18},{18,2},{3,19},{19,3},{4,20},{20... | collective-permute-start | bytes 442376 | tf_op jit(solution)/shard_map/ppermute | solution.py:19
  66.1 18.6 %collective-permute-start.6 = (f32[2,9216]{1,0:T(2,128)S(1)}, f32[2,9216]{1,0:T(2,128)S(1)}, u32[]{:S(2)}, u32[]{:S(2)}) collective-permute-start(f32[2,9216]{1,0:T(2,128)S(1)} %broadcast_select_fusion.6), channel_id=1, source_target_pairs={{0,4},{2,6},{4,0},{6,2},{8,12},{10,14},{12,8},{14,10},{1,5},{3,7},... | collective-permute-start | bytes 221192 | tf_op jit(solution)/shard_map/ppermute | solution.py:28
  92.4 30.4 %collective-permute-start.26 = (bf16[3,32,768]{2,1,0:T(8,128)(2,1)}, bf16[3,32,768]{2,1,0:T(8,128)(2,1)S(1)}, u32[]{:S(2)}, u32[]{:S(2)}) collective-permute-start(bf16[3,32,768]{2,1,0:T(8,128)(2,1)} %collective-permute-done.12.refs_2_), channel_id=1, source_target_pairs={{0,16},{16,0},{1,17},{17,1},{2,18},{18,2},{3,19},{19,3},{4,20},{20... | collective-permute-start | bytes 442376 | tf_op jit(solution)/shard_map/ppermute | solution.py:19
  93.7 27.0 %collective-permute-start.34 = (bf16[9,32,768]{2,1,0:T(8,128)(2,1)S(1)}, bf16[9,32,768]{2,1,0:T(8,128)(2,1)}, u32[]{:S(2)}, u32[]{:S(2)}) collective-permute-start(bf16[9,32,768]{2,1,0:T(8,128)(2,1)S(1)} %constant_dynamic-slice_fusion.25), channel_id=1, source_target_pairs={{0,4},{4,8},{8,12},{12,14},{14,10},{10,6},{6,2},{2,0},{1,5},{5,9},... | collective-permute-start | bytes 1327112 | tf_op jit(solution)/shard_map/ppermute | solution.py:65
  93.9 24.3 %collective-permute-start.7 = (f32[1,9216]{1,0:T(1,128)S(1)}, f32[1,9216]{1,0:T(1,128)S(1)}, u32[]{:S(2)}, u32[]{:S(2)}) collective-permute-start(f32[1,9216]{1,0:T(1,128)S(1)} %broadcast_select_fusion.7), channel_id=1, source_target_pairs={{0,2},{2,0},{4,6},{6,4},{8,10},{10,8},{12,14},{14,12},{1,3},{3,1},... | collective-permute-start | bytes 110600 | tf_op jit(solution)/shard_map/ppermute | solution.py:28
  118.1 24.1 %collective-permute-start.20 = (bf16[2,3,16,768]{3,2,1,0:T(8,128)(2,1)S(1)}, bf16[2,3,16,768]{3,2,1,0:T(8,128)(2,1)S(1)}, u32[]{:S(2)}, u32[]{:S(2)}) collective-permute-start(bf16[2,3,16,768]{3,2,1,0:T(8,128)(2,1)S(1)} %pad_maximum_fusion.20), channel_id=1, source_target_pairs={{0,1},{1,0},{2,3},{3,2},{4,5},{5,4},{6,7},{7,6},{8,9},{9,8},{10,11... | collective-permute-start | bytes 442376 | tf_op jit(solution)/shard_map/ppermute | solution.py:19
  120.6 22.2 %collective-permute-start.27 = (bf16[3,32,768]{2,1,0:T(8,128)(2,1)S(1)}, bf16[3,32,768]{2,1,0:T(8,128)(2,1)S(1)}, u32[]{:S(2)}, u32[]{:S(2)}) collective-permute-start(bf16[3,32,768]{2,1,0:T(8,128)(2,1)S(1)} %collective-permute-done.13.refs_3_), channel_id=1, source_target_pairs={{0,16},{16,0},{1,17},{17,1},{2,18},{18,2},{3,19},{19,3},{4,20},{20... | collective-permute-start | bytes 442376 | tf_op jit(solution)/shard_map/ppermute | solution.py:19
  120.6 20.6 %collective-permute-start.37 = (bf16[9,32,768]{2,1,0:T(8,128)(2,1)S(1)}, bf16[9,32,768]{2,1,0:T(8,128)(2,1)}, u32[]{:S(2)}, u32[]{:S(2)}) collective-permute-start(bf16[9,32,768]{2,1,0:T(8,128)(2,1)S(1)} %constant_dynamic-slice_fusion.25), channel_id=1, source_target_pairs={{0,2},{4,0},{8,4},{12,8},{14,12},{10,14},{6,10},{2,6},{1,3},{5,1},... | collective-permute-start | bytes 1327112 | tf_op jit(solution)/shard_map/ppermute | solution.py:65
  120.7 26.8 %collective-permute-start.35 = (bf16[9,32,768]{2,1,0:T(8,128)(2,1)}, bf16[9,32,768]{2,1,0:T(8,128)(2,1)}, u32[]{:S(2)}, u32[]{:S(2)}) collective-permute-start(bf16[9,32,768]{2,1,0:T(8,128)(2,1)} %collective-permute-done.34.refs_1_), channel_id=1, source_target_pairs={{0,4},{4,8},{8,12},{12,14},{14,10},{10,6},{6,2},{2,0},{1,5},{5,9},... | collective-permute-start | bytes 1327112 | tf_op jit(solution)/shard_map/ppermute | solution.py:65
  122.8 36.4 %collective-permute-start = (bf16[512,768]{1,0:T(8,128)(2,1)}, bf16[512,768]{1,0:T(8,128)(2,1)}, u32[]{:S(2)}, u32[]{:S(2)}) collective-permute-start(bf16[512,768]{1,0:T(8,128)(2,1)} %bitcast), channel_id=1, source_target_pairs={{1,16},{16,1},{3,18},{18,3},{5,20},{20,5},{7,22},{22,7},{9,24},{24... | collective-permute-start | bytes 2359304 | tf_op jit(solution)/shard_map/ppermute | solution.py:23
  142.8 12.5 %collective-permute-start.38 = (bf16[9,32,768]{2,1,0:T(8,128)(2,1)}, bf16[9,32,768]{2,1,0:T(8,128)(2,1)}, u32[]{:S(2)}, u32[]{:S(2)}) collective-permute-start(bf16[9,32,768]{2,1,0:T(8,128)(2,1)} %collective-permute-done.37.refs_2_), channel_id=1, source_target_pairs={{0,2},{4,0},{8,4},{12,8},{14,12},{10,14},{6,10},{2,6},{1,3},{5,1},... | collective-permute-start | bytes 1327112 | tf_op jit(solution)/shard_map/ppermute | solution.py:65
  146.1 13.4 %collective-permute-start.43 = (bf16[2,9,16,768]{3,2,1,0:T(8,128)(2,1)}, bf16[2,9,16,768]{3,2,1,0:T(8,128)(2,1)}, u32[]{:S(2)}, u32[]{:S(2)}) collective-permute-start(bf16[2,9,16,768]{3,2,1,0:T(8,128)(2,1)} %pad_maximum_fusion.10), channel_id=1, source_target_pairs={{0,1},{1,0},{2,3},{3,2},{4,5},{5,4},{6,7},{7,6},{8,9},{9,8},{10,11... | collective-permute-start | bytes 1327112 | tf_op jit(solution)/shard_map/ppermute | solution.py:19
  147.5 12.5 %collective-permute-start.36 = (bf16[9,32,768]{2,1,0:T(8,128)(2,1)}, bf16[9,32,768]{2,1,0:T(8,128)(2,1)S(1)}, u32[]{:S(2)}, u32[]{:S(2)}) collective-permute-start(bf16[9,32,768]{2,1,0:T(8,128)(2,1)} %collective-permute-done.35.refs_3_), channel_id=1, source_target_pairs={{0,4},{4,8},{8,12},{12,14},{14,10},{10,6},{6,2},{2,0},{1,5},{5,9},... | collective-permute-start | bytes 1327112 | tf_op jit(solution)/shard_map/ppermute | solution.py:65
  157.7 14.4 %collective-permute-start.40 = (bf16[2,9,16,768]{3,2,1,0:T(8,128)(2,1)S(1)}, bf16[2,9,16,768]{3,2,1,0:T(8,128)(2,1)S(1)}, u32[]{:S(2)}, u32[]{:S(2)}) collective-permute-start(bf16[2,9,16,768]{3,2,1,0:T(8,128)(2,1)S(1)} %pad_maximum_fusion.9), channel_id=1, source_target_pairs={{0,1},{1,0},{2,3},{3,2},{4,5},{5,4},{6,7},{7,6},{8,9},{9,8},{10,11... | collective-permute-start | bytes 1327112 | tf_op jit(solution)/shard_map/ppermute | solution.py:19
  159.2 12.9 %collective-permute-start.39 = (bf16[9,32,768]{2,1,0:T(8,128)(2,1)}, bf16[9,32,768]{2,1,0:T(8,128)(2,1)S(1)}, u32[]{:S(2)}, u32[]{:S(2)}) collective-permute-start(bf16[9,32,768]{2,1,0:T(8,128)(2,1)} %collective-permute-done.38.refs_4_), channel_id=1, source_target_pairs={{0,2},{4,0},{8,4},{12,8},{14,12},{10,14},{6,10},{2,6},{1,3},{5,1},... | collective-permute-start | bytes 1327112 | tf_op jit(solution)/shard_map/ppermute | solution.py:65
  159.5 12.7 %collective-permute-start.41 = (bf16[9,32,768]{2,1,0:T(8,128)(2,1)}, bf16[9,32,768]{2,1,0:T(8,128)(2,1)S(1)}, u32[]{:S(2)}, u32[]{:S(2)}) collective-permute-start(bf16[9,32,768]{2,1,0:T(8,128)(2,1)} %collective-permute-done.35.refs_3_), channel_id=1, source_target_pairs={{0,16},{16,0},{1,17},{17,1},{2,18},{18,2},{3,19},{19,3},{4,20},{20... | collective-permute-start | bytes 1327112 | tf_op jit(solution)/shard_map/ppermute | solution.py:19
  159.5 12.7 %collective-permute-start.42 = (bf16[9,32,768]{2,1,0:T(8,128)(2,1)}, bf16[9,32,768]{2,1,0:T(8,128)(2,1)S(1)}, u32[]{:S(2)}, u32[]{:S(2)}) collective-permute-start(bf16[9,32,768]{2,1,0:T(8,128)(2,1)} %collective-permute-done.38.refs_4_), channel_id=1, source_target_pairs={{0,16},{16,0},{1,17},{17,1},{2,18},{18,2},{3,19},{19,3},{4,20},{20... | collective-permute-start | bytes 1327112 | tf_op jit(solution)/shard_map/ppermute | solution.py:19
  172.9 21.0 %collective-permute-start.49 = (bf16[9,32,768]{2,1,0:T(8,128)(2,1)S(1)}, bf16[9,32,768]{2,1,0:T(8,128)(2,1)S(1)}, u32[]{:S(2)}, u32[]{:S(2)}) collective-permute-start(bf16[9,32,768]{2,1,0:T(8,128)(2,1)S(1)} %copy-done.12), channel_id=1, source_target_pairs={{0,16},{16,0},{1,17},{17,1},{2,18},{18,2},{3,19},{19,3},{4,20},{20... | collective-permute-start | bytes 1327112 | tf_op jit(solution)/shard_map/ppermute | solution.py:19
  175.0 19.6 %collective-permute-start.50 = (bf16[9,32,768]{2,1,0:T(8,128)(2,1)S(1)}, bf16[9,32,768]{2,1,0:T(8,128)(2,1)S(1)}, u32[]{:S(2)}, u32[]{:S(2)}) collective-permute-start(bf16[9,32,768]{2,1,0:T(8,128)(2,1)S(1)} %collective-permute-done.39.refs_6_), channel_id=1, source_target_pairs={{0,16},{16,0},{1,17},{17,1},{2,18},{18,2},{3,19},{19,3},{4,20},{20... | collective-permute-start | bytes 1327112 | tf_op jit(solution)/shard_map/ppermute | solution.py:19
  175.3 18.6 %collective-permute-start.47 = (bf16[9,16,768]{2,1,0:T(8,128)(2,1)S(1)}, bf16[9,16,768]{2,1,0:T(8,128)(2,1)S(1)}, u32[]{:S(2)}, u32[]{:S(2)}) collective-permute-start(bf16[9,16,768]{2,1,0:T(8,128)(2,1)S(1)} %get-tuple-element.260), channel_id=1, source_target_pairs={{0,2},{4,0},{8,4},{12,8},{14,12},{10,14},{6,10},{2,6},{1,3},{5,1},... | collective-permute-start | bytes 663560 | tf_op jit(solution)/shard_map/ppermute | solution.py:65
  180.9 13.0 %collective-permute-start.48 = (bf16[2,9,16,768]{3,2,1,0:T(8,128)(2,1)S(1)}, bf16[2,9,16,768]{3,2,1,0:T(8,128)(2,1)}, u32[]{:S(2)}, u32[]{:S(2)}) collective-permute-start(bf16[2,9,16,768]{3,2,1,0:T(8,128)(2,1)S(1)} %pad_maximum_fusion.11), channel_id=1, source_target_pairs={{0,1},{1,0},{2,3},{3,2},{4,5},{5,4},{6,7},{7,6},{8,9},{9,8},{10,11... | collective-permute-start | bytes 1327112 | tf_op jit(solution)/shard_map/ppermute | solution.py:19
  181.3 14.2 %collective-permute-start.51 = (bf16[2,9,16,768]{3,2,1,0:T(8,128)(2,1)S(1)}, bf16[2,9,16,768]{3,2,1,0:T(8,128)(2,1)S(1)}, u32[]{:S(2)}, u32[]{:S(2)}) collective-permute-start(bf16[2,9,16,768]{3,2,1,0:T(8,128)(2,1)S(1)} %collective-permute-done.40.refs_9_), channel_id=1, source_target_pairs={{0,16},{16,0},{1,17},{17,1},{2,18},{18,2},{3,19},{19,3},{4,20},{20... | collective-permute-start | bytes 1327112 | tf_op jit(solution)/shard_map/ppermute | solution.py:19
  309.3 246.4 %reduce-scatter.4.cloned.1.call-start = ((), (), s32[]{:S(2)}) async-start(), calls=%async_computation.4 | async-start | bytes 4866048 | tf_op jit(solution)/shard_map/reduce_scatter | solution.py:320
  310.0 357.2 %reduce-scatter.8.cloned.1.call-start = ((), (), s32[]{:S(2)}) async-start(), calls=%async_computation.6 | async-start | bytes 4866048 | tf_op jit(solution)/shard_map/reduce_scatter | solution.py:320
  336.6 31.2 %collective-permute-start.61 = (bf16[2,512,768]{2,1,0:T(8,128)(2,1)}, bf16[2,512,768]{2,1,0:T(8,128)(2,1)S(1)}, u32[]{:S(2)}, u32[]{:S(2)}) collective-permute-start(bf16[2,512,768]{2,1,0:T(8,128)(2,1)} %get-tuple-element.124), channel_id=1, source_target_pairs={{0,16},{16,0},{1,17},{17,1},{2,18},{18,2},{3,19},{19,3},{4,20},{20... | collective-permute-start | bytes 4718600 | tf_op jit(solution)/shard_map/ppermute | solution.py:19
  365.9 55.3 %collective-permute-start.59 = (bf16[512,768]{1,0:T(8,128)(2,1)}, bf16[512,768]{1,0:T(8,128)(2,1)}, u32[]{:S(2)}, u32[]{:S(2)}) collective-permute-start(bf16[512,768]{1,0:T(8,128)(2,1)} %multiply_convert_fusion), channel_id=1, source_target_pairs={{1,16},{16,1},{3,18},{18,3},{5,20},{20,5},{7,22},{22,7},{9,24},{24... | collective-permute-start | bytes 2359304 | tf_op jit(solution)/shard_map/ppermute | solution.py:23
  414.5 51.5 %collective-permute-start.62 = (bf16[8,9,48,768]{3,2,1,0:T(8,128)(2,1)}, bf16[8,9,48,768]{3,2,1,0:T(8,128)(2,1)}, u32[]{:S(2)}, u32[]{:S(2)}) collective-permute-start(bf16[8,9,48,768]{3,2,1,0:T(8,128)(2,1)} %pad_maximum_fusion), channel_id=1, source_target_pairs={{0,16},{16,0},{1,17},{17,1},{2,18},{18,2},{3,19},{19,3},{4,20},{20... | collective-permute-start | bytes 15925256 | tf_op jit(solution)/shard_map/ppermute | solution.py:19
  425.4 26.3 %collective-permute-start.68 = (bf16[1,4608]{1,0:T(2,128)(2,1)S(1)}, bf16[1,4608]{1,0:T(2,128)(2,1)S(1)}, u32[]{:S(2)}, u32[]{:S(2)}) collective-permute-start(bf16[1,4608]{1,0:T(2,128)(2,1)S(1)} %broadcast_in_dim.54), channel_id=1, source_target_pairs={{0,2},{2,0},{4,6},{6,4},{8,10},{10,8},{12,14},{14,12},{1,3},{3,1},... | collective-permute-start | bytes 27656 | tf_op jit(solution)/shard_map/ppermute | solution.py:28
  466.0 216.1 %collective-permute-start.63 = (bf16[2,512,768]{2,1,0:T(8,128)(2,1)S(1)}, bf16[2,512,768]{2,1,0:T(8,128)(2,1)S(1)}, u32[]{:S(2)}, u32[]{:S(2)}) collective-permute-start(bf16[2,512,768]{2,1,0:T(8,128)(2,1)S(1)} %get-tuple-element.142), channel_id=1, source_target_pairs={{0,16},{16,0},{1,17},{17,1},{2,18},{18,2},{3,19},{19,3},{4,20},{20... | collective-permute-start | bytes 4718600 | tf_op jit(solution)/shard_map/ppermute | solution.py:19
  477.8 190.5 %collective-permute-start.105 = (bf16[2,9,16,768]{3,2,1,0:T(8,128)(2,1)}, bf16[2,9,16,768]{3,2,1,0:T(8,128)(2,1)}, u32[]{:S(2)}, u32[]{:S(2)}) collective-permute-start(bf16[2,9,16,768]{3,2,1,0:T(8,128)(2,1)} %pad_maximum_fusion.14), channel_id=1, source_target_pairs={{0,1},{1,0},{2,3},{3,2},{4,5},{5,4},{6,7},{7,6},{8,9},{9,8},{10,11... | collective-permute-start | bytes 1327112 | tf_op jit(solution)/shard_map/ppermute | solution.py:19
  481.2 210.9 %collective-permute-start.64 = (bf16[1,9,16,768]{3,2,1,0:T(8,128)(2,1)}, bf16[1,9,16,768]{3,2,1,0:T(8,128)(2,1)}, u32[]{:S(2)}, u32[]{:S(2)}) collective-permute-start(bf16[1,9,16,768]{3,2,1,0:T(8,128)(2,1)} %get-tuple-element.202), channel_id=1, source_target_pairs={{0,1},{1,0},{2,3},{3,2},{4,5},{5,4},{6,7},{7,6},{8,9},{9,8},{10,11... | collective-permute-start | bytes 663560 | tf_op jit(solution)/shard_map/ppermute | solution.py:19
  483.0 188.6 %collective-permute-start.104 = (bf16[2,9,16,768]{3,2,1,0:T(8,128)(2,1)}, bf16[2,9,16,768]{3,2,1,0:T(8,128)(2,1)}, u32[]{:S(2)}, u32[]{:S(2)}) collective-permute-start(bf16[2,9,16,768]{3,2,1,0:T(8,128)(2,1)} %pad_maximum_fusion.13), channel_id=1, source_target_pairs={{0,1},{1,0},{2,3},{3,2},{4,5},{5,4},{6,7},{7,6},{8,9},{9,8},{10,11... | collective-permute-start | bytes 1327112 | tf_op jit(solution)/shard_map/ppermute | solution.py:19
  484.8 207.3 %collective-permute-start.65 = (bf16[2,9,16,768]{3,2,1,0:T(8,128)(2,1)}, bf16[2,9,16,768]{3,2,1,0:T(8,128)(2,1)}, u32[]{:S(2)}, u32[]{:S(2)}) collective-permute-start(bf16[2,9,16,768]{3,2,1,0:T(8,128)(2,1)} %pad_maximum_fusion.12), channel_id=1, source_target_pairs={{0,1},{1,0},{2,3},{3,2},{4,5},{5,4},{6,7},{7,6},{8,9},{9,8},{10,11... | collective-permute-start | bytes 1327112 | tf_op jit(solution)/shard_map/ppermute | solution.py:19
  668.3 12.7 %collective-permute-start.96 = (bf16[1,3,96,768]{3,2,1,0:T(8,128)(2,1)S(1)}, bf16[1,3,96,768]{3,2,1,0:T(8,128)(2,1)S(1)}, u32[]{:S(2)}, u32[]{:S(2)}) collective-permute-start(bf16[1,3,96,768]{3,2,1,0:T(8,128)(2,1)S(1)} %maximum_bitcast_fusion.4), channel_id=1, source_target_pairs={{0,1},{1,0},{2,3},{3,2},{4,5},{5,4},{6,7},{7,6},{8,9},{9,8},{10,11... | collective-permute-start | bytes 1327112 | tf_op jit(solution)/shard_map/ppermute | solution.py:28
  671.7 144.2 %collective-permute-start.103 = (bf16[1,9,16,768]{3,2,1,0:T(8,128)(2,1)}, bf16[1,9,16,768]{3,2,1,0:T(8,128)(2,1)}, u32[]{:S(2)}, u32[]{:S(2)}) collective-permute-start(bf16[1,9,16,768]{3,2,1,0:T(8,128)(2,1)} %get-tuple-element.195), channel_id=1, source_target_pairs={{0,1},{1,0},{2,3},{3,2},{4,5},{5,4},{6,7},{7,6},{8,9},{9,8},{10,11... | collective-permute-start | bytes 663560 | tf_op jit(solution)/shard_map/ppermute | solution.py:19
  682.1 61.3 %collective-permute-start.97 = (bf16[2,3,96,768]{3,2,1,0:T(8,128)(2,1)}, bf16[2,3,96,768]{3,2,1,0:T(8,128)(2,1)}, u32[]{:S(2)}, u32[]{:S(2)}) collective-permute-start(bf16[2,3,96,768]{3,2,1,0:T(8,128)(2,1)} %maximum_select_fusion.2), channel_id=1, source_target_pairs={{0,16},{16,0},{1,17},{17,1},{2,18},{18,2},{3,19},{19,3},{4,20},{20... | collective-permute-start | bytes 2654216 | tf_op jit(solution)/shard_map/ppermute | solution.py:28
  693.1 130.2 %collective-permute-start.66 = (bf16[512,768]{1,0:T(8,128)(2,1)}, bf16[512,768]{1,0:T(8,128)(2,1)}, u32[]{:S(2)}, u32[]{:S(2)}) collective-permute-start(bf16[512,768]{1,0:T(8,128)(2,1)} %convert_element_type.417), channel_id=1, source_target_pairs={{1,16},{16,1},{3,18},{18,3},{5,20},{20,5},{7,22},{22,7},{9,24},{24... | collective-permute-start | bytes 2359304 | tf_op jit(solution)/shard_map/ppermute | solution.py:23
  742.7 23.1 %collective-permute-start.80 = (bf16[8,3,48,768]{3,2,1,0:T(8,128)(2,1)}, bf16[8,3,48,768]{3,2,1,0:T(8,128)(2,1)S(1)}, u32[]{:S(2)}, u32[]{:S(2)}) collective-permute-start(bf16[8,3,48,768]{3,2,1,0:T(8,128)(2,1)} %constant_dynamic-slice_fusion.13), channel_id=1, source_target_pairs={{0,16},{16,0},{1,17},{17,1},{2,18},{18,2},{3,19},{19,3},{4,20},{20... | collective-permute-start | bytes 5308424 | tf_op jit(solution)/shard_map/ppermute | solution.py:19
  753.7 63.8 %collective-permute-start.109 = (bf16[9,32,768]{2,1,0:T(8,128)(2,1)S(1)}, bf16[9,32,768]{2,1,0:T(8,128)(2,1)S(1)}, u32[]{:S(2)}, u32[]{:S(2)}) collective-permute-start(bf16[9,32,768]{2,1,0:T(8,128)(2,1)S(1)} %get-tuple-element.203), channel_id=1, source_target_pairs={{0,4},{4,8},{8,12},{12,14},{14,10},{10,6},{6,2},{2,0},{1,5},{5,9},... | collective-permute-start | bytes 1327112 | tf_op jit(solution)/shard_map/ppermute | solution.py:65
  764.7 33.4 %collective-permute-start.112 = (bf16[9,32,768]{2,1,0:T(8,128)(2,1)S(1)}, bf16[9,32,768]{2,1,0:T(8,128)(2,1)S(1)}, u32[]{:S(2)}, u32[]{:S(2)}) collective-permute-start(bf16[9,32,768]{2,1,0:T(8,128)(2,1)S(1)} %add_convert_fusion.4), channel_id=1, source_target_pairs={{0,2},{4,0},{8,4},{12,8},{14,12},{10,14},{6,10},{2,6},{1,3},{5,1},... | collective-permute-start | bytes 1327112 | tf_op jit(solution)/shard_map/ppermute | solution.py:65
  803.4 14.6 %collective-permute-start.113 = (bf16[9,32,768]{2,1,0:T(8,128)(2,1)S(1)}, bf16[9,32,768]{2,1,0:T(8,128)(2,1)S(1)}, u32[]{:S(2)}, u32[]{:S(2)}) collective-permute-start(bf16[9,32,768]{2,1,0:T(8,128)(2,1)S(1)} %add_convert_fusion.3), channel_id=1, source_target_pairs={{0,2},{4,0},{8,4},{12,8},{14,12},{10,14},{6,10},{2,6},{1,3},{5,1},... | collective-permute-start | bytes 1327112 | tf_op jit(solution)/shard_map/ppermute | solution.py:65
  (210 other events, 2137.1 us)
Sparse Core Ops, SparseCore 0:
  17.4 128.0 all-gather.1
  309.4 123.7 reduce-scatter.5
  439.5 116.1 reduce-scatter.3
  561.0 106.1 reduce-scatter.7
